TPU v7x, 32 devices: a whole 2x2x4 slice. The times are simulated.
32 devices in a mesh: dp: 8 (over z, y), mp: 4 (over x, core).
Axes of the slice: x: 2, y: 2, z: 4, core: 2. Of those that a mesh axis runs over, the one named last changes fastest.
Arguments:
- inputs: bfloat16 [64, 197, 768], P('dp'), may hold values from -6 to 6
- cotangent: bfloat16 [64, 197, 768], P('dp'), may hold values from -6 to 6
- counts: int32 [8], P('dp'), may hold values from 1 to 8, 36 in all
- qkv_weight: float32 [2, 768, 3, 768], P(None, 'dp', None, 'mp'), may hold values from -0.21875 to 0.21875
- out_weight: float32 [2, 768, 768], P(None, 'mp', 'dp'), may hold values from -0.875 to 0.875
- up_weight: float32 [2, 768, 3072], P(None, 'dp', 'mp'), may hold values from -0.21875 to 0.21875
- down_weight: float32 [2, 3072, 768], P(None, 'mp', 'dp'), may hold values from -0.109375 to 0.109375
- vectors: float32 [2, 4, 8, 288], P(None, 'mp', 'dp'), may hold values from 0.5 to 1.5
- qkv_first: float32 [2, 768, 3, 768], P(None, 'dp', None, 'mp'), may hold values from -48 to 48
- qkv_second: float32 [2, 768, 3, 768], P(None, 'dp', None, 'mp'), may hold values from 425.52 to 1418.4
- out_first: float32 [2, 768, 768], P(None, 'mp', 'dp'), may hold values from -48 to 48
- out_second: float32 [2, 768, 768], P(None, 'mp', 'dp'), may hold values from 425.52 to 1418.4
- up_first: float32 [2, 768, 3072], P(None, 'dp', 'mp'), may hold values from -48 to 48
- up_second: float32 [2, 768, 3072], P(None, 'dp', 'mp'), may hold values from 425.52 to 1418.4
- down_first: float32 [2, 3072, 768], P(None, 'mp', 'dp'), may hold values from -48 to 48
- down_second: float32 [2, 3072, 768], P(None, 'mp', 'dp'), may hold values from 425.52 to 1418.4
- vector_first: float32 [2, 4, 8, 288], P(None, 'mp', 'dp'), may hold values from -48 to 48
- vector_second: float32 [2, 4, 8, 288], P(None, 'mp', 'dp'), may hold values from 425.52 to 1418.4
Outputs:
- output_tokens: bfloat16 [64, 197, 768], P('dp')
- input_grad: float32 [64, 197, 768], P('dp')
- qkv_first_new: float32 [2, 768, 3, 768], P(None, 'dp', None, 'mp')
- qkv_second_new: float32 [2, 768, 3, 768], P(None, 'dp', None, 'mp')
- qkv_weight_new: float32 [2, 768, 3, 768], P(None, 'dp', None, 'mp')
- out_first_new: float32 [2, 768, 768], P(None, 'mp', 'dp')
- out_second_new: float32 [2, 768, 768], P(None, 'mp', 'dp')
- out_weight_new: float32 [2, 768, 768], P(None, 'mp', 'dp')
- up_first_new: float32 [2, 768, 3072], P(None, 'dp', 'mp')
- up_second_new: float32 [2, 768, 3072], P(None, 'dp', 'mp')
- up_weight_new: float32 [2, 768, 3072], P(None, 'dp', 'mp')
- down_first_new: float32 [2, 3072, 768], P(None, 'mp', 'dp')
- down_second_new: float32 [2, 3072, 768], P(None, 'mp', 'dp')
- down_weight_new: float32 [2, 3072, 768], P(None, 'mp', 'dp')
- vector_first_new: float32 [2, 4, 8, 288], P(None, 'mp', 'dp')
- vector_second_new: float32 [2, 4, 8, 288], P(None, 'mp', 'dp')
- vector_new: float32 [2, 4, 8, 288], P(None, 'mp', 'dp')
Inputs may be any that keep to these rules, and one draw needn't show every extreme that they name: counts sums to 36, and some index of dp holds exactly 8 images.
All inputs are finite; a program needn't handle non-finite values. No bound on the sum of `counts` on one device may be relied on, other than what follows from the above.
Results may differ from a plain program's by a relative error of at most 0.017.
Values may be sent and summed in bfloat16 or wider, within the bound.
A program may use at most 192 MiB of HBM per device.

v0:
```python
import jax
import jax.numpy as jnp
from jax import lax
from jax.sharding import PartitionSpec as P

D = 768
HEAD_DIM = 64
STEP = 10


norm_epsilon = 1e-06


def layer_norm(values, gain_row, shift_row):
    average = jnp.mean(values, axis=-1, keepdims=True)
    centered = values - average
    variance = jnp.mean(centered * centered, axis=-1, keepdims=True)
    return centered * lax.rsqrt(variance + norm_epsilon) * gain_row + shift_row


def gelu_exact(values):
    return jax.nn.gelu(values, approximate=False)


def adam_update(weight, first_moment, second_moment, gradient, step_rate, decay_rate):
    first_new = 0.9 * first_moment + 0.1 * gradient
    second_new = 0.95 * second_moment + 0.05 * gradient * gradient
    first_hat = first_new / (1.0 - 0.9**STEP)
    second_hat = second_new / (1.0 - 0.95**STEP)
    weight_new = weight - step_rate * (
        first_hat / (jnp.sqrt(second_hat) + 1e-08) + decay_rate * weight
    )
    return (first_new, second_new, weight_new)


def split_heads(values, slot_count):
    return values.reshape(slot_count, values.shape[0] // slot_count, -1, HEAD_DIM)


def join_heads(values):
    return values.reshape(values.shape[0] * values.shape[1], -1)


def attention_scores(query_rows, key_rows, slot_count):
    return jnp.einsum(
        "bqhd,bkhd->bhqk",
        split_heads(query_rows, slot_count),
        split_heads(key_rows, slot_count),
        preferred_element_type=jnp.float32,
    ) * HEAD_DIM ** (-0.5)


def attention_forward(query_rows, key_rows, value_rows, slot_count):
    scores = attention_scores(query_rows, key_rows, slot_count)
    row_peak = jnp.max(scores, axis=-1, keepdims=True)
    row_total = jnp.sum(jnp.exp(scores - row_peak), axis=-1, keepdims=True)
    log_total = row_peak + jnp.log(row_total)
    softmax_rows = jnp.exp(scores - log_total).astype(jnp.bfloat16)
    attended = jnp.einsum(
        "bhqk,bkhd->bqhd",
        softmax_rows,
        split_heads(value_rows, slot_count),
        preferred_element_type=jnp.float32,
    )
    return (join_heads(attended).astype(jnp.bfloat16), log_total)


def attention_backward(query_rows, key_rows, value_rows, log_total, attended_grad, slot_count):
    scores = attention_scores(query_rows, key_rows, slot_count)
    softmax_rows = jnp.exp(scores - log_total)
    grad_heads = split_heads(attended_grad, slot_count)
    value_grad = jnp.einsum(
        "bhqk,bqhd->bkhd",
        softmax_rows.astype(jnp.bfloat16),
        grad_heads,
        preferred_element_type=jnp.float32,
    )
    prob_grad = jnp.einsum(
        "bqhd,bkhd->bhqk",
        grad_heads,
        split_heads(value_rows, slot_count),
        preferred_element_type=jnp.float32,
    )
    score_grad = (
        softmax_rows * (prob_grad - jnp.sum(softmax_rows * prob_grad, axis=-1, keepdims=True))
    ).astype(jnp.bfloat16)
    query_grad = jnp.einsum(
        "bhqk,bkhd->bqhd",
        score_grad,
        split_heads(key_rows, slot_count),
        preferred_element_type=jnp.float32,
    ) * HEAD_DIM ** (-0.5)
    key_grad = jnp.einsum(
        "bhqk,bqhd->bkhd",
        score_grad,
        split_heads(query_rows, slot_count),
        preferred_element_type=jnp.float32,
    ) * HEAD_DIM ** (-0.5)
    return (
        join_heads(query_grad).astype(jnp.bfloat16),
        join_heads(key_grad).astype(jnp.bfloat16),
        join_heads(value_grad).astype(jnp.bfloat16),
    )


def branch_sum(partial_rows):
    return lax.psum(partial_rows.astype(jnp.bfloat16), "mp").astype(jnp.float32)


def input_sum(partial_rows):
    return lax.psum(partial_rows.astype(jnp.bfloat16), "mp").astype(jnp.float32)


def on_device(
    inputs,
    cotangent,
    counts,
    qkv_weight,
    out_weight,
    up_weight,
    down_weight,
    vectors,
    qkv_first,
    qkv_second,
    out_first,
    out_second,
    up_first,
    up_second,
    down_first,
    down_second,
    vector_first,
    vector_second,
):
    slot_count, seq_len, model_width = inputs.shape
    row_count = slot_count * seq_len
    dp_count = lax.axis_size("dp")
    mp_count = lax.axis_size("mp")
    mp_index = lax.axis_index("mp")
    layers = qkv_weight.shape[0]
    head_cols = qkv_weight.shape[3]
    row_width = 6 * model_width // mp_count
    bf16 = jnp.bfloat16
    f32 = jnp.float32
    gathered = (
        lax.all_gather(qkv_weight.astype(bf16), "dp", axis=1, tiled=True),
        lax.all_gather(out_weight.astype(bf16), "dp", axis=2, tiled=True),
        lax.all_gather(up_weight.astype(bf16), "dp", axis=1, tiled=True),
        lax.all_gather(down_weight.astype(bf16), "dp", axis=2, tiled=True),
    )
    vector_flat = lax.all_gather(vectors.reshape(layers, -1), ("dp", "mp"), axis=1, tiled=True)
    block_width = vector_flat.shape[1] // mp_count
    vector_blocks = (
        vector_flat.reshape(layers, dp_count, mp_count, -1)
        .transpose(0, 2, 1, 3)
        .reshape(layers, mp_count, block_width)
    )
    row_part = vector_blocks[:, :, :row_width].reshape(layers, 6, model_width)
    own_block = lax.dynamic_index_in_dim(vector_blocks, mp_index, 1, keepdims=False)
    query_bias = own_block[:, row_width : row_width + head_cols]
    value_bias = own_block[:, row_width + head_cols : row_width + 2 * head_cols]
    hidden_bias = own_block[:, row_width + 2 * head_cols :]
    live_slots = (
        (jnp.arange(slot_count, dtype=jnp.int32) < counts[0]).astype(f32).reshape(slot_count, 1, 1)
    )
    stream = inputs.astype(f32).reshape(row_count, model_width)
    kept_layers = []
    for layer_index in range(layers):
        qkv_layer, out_layer, up_layer, down_layer = (
            gathered[0][layer_index],
            gathered[1][layer_index],
            gathered[2][layer_index],
            gathered[3][layer_index],
        )
        normed_low = layer_norm(stream, row_part[layer_index, 0], row_part[layer_index, 1]).astype(
            bf16
        )
        projected = jnp.einsum("rd,dce->rce", normed_low, qkv_layer, preferred_element_type=f32)
        query_rows = (projected[:, 0] + query_bias[layer_index]).astype(bf16)
        key_rows = projected[:, 1].astype(bf16)
        value_rows = (projected[:, 2] + value_bias[layer_index]).astype(bf16)
        attended_low, log_total = attention_forward(query_rows, key_rows, value_rows, slot_count)
        middle = (
            stream
            + branch_sum(jnp.dot(attended_low, out_layer, preferred_element_type=f32))
            + row_part[layer_index, 4]
        )
        mixed_low = layer_norm(middle, row_part[layer_index, 2], row_part[layer_index, 3]).astype(
            bf16
        )
        hidden = jnp.dot(mixed_low, up_layer, preferred_element_type=f32) + hidden_bias[layer_index]
        activated_low = gelu_exact(hidden).astype(bf16)
        next_stream = (
            middle
            + branch_sum(jnp.dot(activated_low, down_layer, preferred_element_type=f32))
            + row_part[layer_index, 5]
        )
        kept_layers.append(
            (
                stream,
                normed_low,
                query_rows,
                key_rows,
                value_rows,
                log_total,
                attended_low,
                middle,
                mixed_low,
                hidden,
                activated_low,
            )
        )
        stream = next_stream
    output_tokens = (stream.reshape(slot_count, seq_len, model_width) * live_slots).astype(bf16)
    back_weights = (
        lax.all_gather(qkv_weight.astype(bf16), "dp", axis=1, tiled=True),
        lax.all_gather(out_weight.astype(bf16), "dp", axis=2, tiled=True),
        lax.all_gather(up_weight.astype(bf16), "dp", axis=1, tiled=True),
        lax.all_gather(down_weight.astype(bf16), "dp", axis=2, tiled=True),
    )
    first_rank = (mp_index == 0).astype(f32)
    upstream = (cotangent.astype(f32) * live_slots).reshape(row_count, model_width)
    qkv_grads = [None] * layers
    out_grads = [None] * layers
    up_grads = [None] * layers
    down_grads = [None] * layers
    row_grads = [None] * layers
    column_grads = [None] * layers
    for layer_index in reversed(range(layers)):
        (
            stream_in,
            normed_low,
            query_rows,
            key_rows,
            value_rows,
            log_total,
            attended_low,
            middle,
            mixed_low,
            hidden,
            activated_low,
        ) = kept_layers[layer_index]
        qkv_layer, out_layer, up_layer, down_layer = (
            back_weights[0][layer_index],
            back_weights[1][layer_index],
            back_weights[2][layer_index],
            back_weights[3][layer_index],
        )
        upstream_low = upstream.astype(bf16)
        down_grads[layer_index] = jnp.einsum(
            "rf,rd->fd", activated_low, upstream_low, preferred_element_type=f32
        )
        ignored, gelu_back = jax.vjp(gelu_exact, hidden)
        hidden_low = gelu_back(
            jnp.einsum("rd,fd->rf", upstream_low, down_layer, preferred_element_type=f32)
        )[0].astype(bf16)
        up_grads[layer_index] = jnp.einsum(
            "rd,rf->df", mixed_low, hidden_low, preferred_element_type=f32
        )
        hidden_bias_grad = jnp.sum(hidden_low.astype(f32), axis=0)
        mixed_grad = input_sum(
            jnp.einsum("rf,df->rd", hidden_low, up_layer, preferred_element_type=f32)
        )
        ignored, second_back = jax.vjp(
            layer_norm, middle, row_part[layer_index, 2], row_part[layer_index, 3]
        )
        middle_part, gain_second_grad, shift_second_grad = second_back(mixed_grad)
        middle_grad = upstream + middle_part
        down_bias_grad = jnp.sum(upstream, axis=0)
        middle_low = middle_grad.astype(bf16)
        out_grads[layer_index] = jnp.einsum(
            "re,rd->ed", attended_low, middle_low, preferred_element_type=f32
        )
        out_bias_grad = jnp.sum(middle_grad, axis=0)
        attended_grad = jnp.einsum(
            "rd,ed->re", middle_low, out_layer, preferred_element_type=f32
        ).astype(bf16)
        query_grad, key_grad, value_grad = attention_backward(
            query_rows, key_rows, value_rows, log_total, attended_grad, slot_count
        )
        stacked = jnp.stack([query_grad, key_grad, value_grad], axis=1)
        qkv_grads[layer_index] = jnp.einsum(
            "rd,rce->dce", normed_low, stacked, preferred_element_type=f32
        )
        normed_grad = input_sum(
            jnp.einsum("rce,dce->rd", stacked, qkv_layer, preferred_element_type=f32)
        )
        ignored, first_back = jax.vjp(
            layer_norm, stream_in, row_part[layer_index, 0], row_part[layer_index, 1]
        )
        stream_part, gain_first_grad, shift_first_grad = first_back(normed_grad)
        upstream = middle_grad + stream_part
        row_grads[layer_index] = (
            jnp.stack(
                [
                    gain_first_grad,
                    shift_first_grad,
                    gain_second_grad,
                    shift_second_grad,
                    out_bias_grad,
                    down_bias_grad,
                ]
            )
            * first_rank
        )
        column_grads[layer_index] = jnp.concatenate(
            [
                jnp.sum(query_grad.astype(f32), axis=0),
                jnp.sum(value_grad.astype(f32), axis=0),
                hidden_bias_grad,
            ]
        )
    input_grad = upstream.reshape(slot_count, seq_len, model_width)
    qkv_grad, out_grad, up_grad, down_grad = (
        lax.psum_scatter(jnp.stack(qkv_grads), "dp", scatter_dimension=1, tiled=True),
        lax.psum_scatter(jnp.stack(out_grads), "dp", scatter_dimension=2, tiled=True),
        lax.psum_scatter(jnp.stack(up_grads), "dp", scatter_dimension=1, tiled=True),
        lax.psum_scatter(jnp.stack(down_grads), "dp", scatter_dimension=2, tiled=True),
    )
    owner_mask = (jnp.arange(mp_count, dtype=jnp.int32) == mp_index).astype(f32)
    placed = jnp.stack(column_grads)[:, None, :] * owner_mask[None, :, None]
    vector_grad = jnp.concatenate(
        [jnp.stack(row_grads).reshape(layers, mp_count, row_width), placed], axis=2
    )
    vector_grad = (
        vector_grad.reshape(layers, mp_count, dp_count, -1)
        .transpose(0, 2, 1, 3)
        .reshape(layers, -1)
    )
    vector_grad = lax.psum_scatter(
        vector_grad, ("dp", "mp"), scatter_dimension=1, tiled=True
    ).reshape(vectors.shape)
    matrix_rate = 3.0 / D**0.5
    qkv_new = adam_update(qkv_weight, qkv_first, qkv_second, qkv_grad, matrix_rate, 0.1)
    out_new = adam_update(out_weight, out_first, out_second, out_grad, matrix_rate, 0.1)
    up_new = adam_update(up_weight, up_first, up_second, up_grad, matrix_rate, 0.1)
    down_new = adam_update(down_weight, down_first, down_second, down_grad, matrix_rate, 0.1)
    vector_new = adam_update(vectors, vector_first, vector_second, vector_grad, 0.5, 0.0)
    return (
        output_tokens,
        input_grad,
        qkv_new[0],
        qkv_new[1],
        qkv_new[2],
        out_new[0],
        out_new[1],
        out_new[2],
        up_new[0],
        up_new[1],
        up_new[2],
        down_new[0],
        down_new[1],
        down_new[2],
        vector_new[0],
        vector_new[1],
        vector_new[2],
    )


def solution(mesh):
    placed = (
        P("dp", None, None),
        P("dp", None, None),
        P("dp"),
        P(None, "dp", None, "mp"),
        P(None, "mp", "dp"),
        P(None, "dp", "mp"),
        P(None, "mp", "dp"),
        P(None, "mp", "dp", None),
        P(None, "dp", None, "mp"),
        P(None, "dp", None, "mp"),
        P(None, "mp", "dp"),
        P(None, "mp", "dp"),
        P(None, "dp", "mp"),
        P(None, "dp", "mp"),
        P(None, "mp", "dp"),
        P(None, "mp", "dp"),
        P(None, "mp", "dp", None),
        P(None, "mp", "dp", None),
    )
    return jax.shard_map(
        on_device,
        mesh=mesh,
        in_specs=placed,
        out_specs=(
            P("dp", None, None),
            P("dp", None, None),
            P(None, "dp", None, "mp"),
            P(None, "dp", None, "mp"),
            P(None, "dp", None, "mp"),
            P(None, "mp", "dp"),
            P(None, "mp", "dp"),
            P(None, "mp", "dp"),
            P(None, "dp", "mp"),
            P(None, "dp", "mp"),
            P(None, "dp", "mp"),
            P(None, "mp", "dp"),
            P(None, "mp", "dp"),
            P(None, "mp", "dp"),
            P(None, "mp", "dp", None),
            P(None, "mp", "dp", None),
            P(None, "mp", "dp", None),
        ),
        check_vma=False,
    )
```

profile of v0, /device:TPU:0, one launch (start us, length us, event | category | flops | bytes accessed | tf_op | source)
XLA Modules:
  0.0 1471.5 jit_solution(17214857193684062355)
XLA Ops:
  10.4 75.7 %all-gather = f32[2,1,1,9216]{0,2,1,3:T(1,128)} all-gather(f32[2,1,1,288]{0,2,1,3:T(1,128)S(1)} %copy.325), channel_id=2, replica_groups=mesh['dp'=8,'mp'=4] {'dp','mp'}, dimensions={3}, use_global_device_ids=true | all-gather | bytes 76032 | tf_op jit(solution)/shard_map/all_gather | solution.py:150
  96.3 3.8 convert_element_type.336
  101.1 32.1 %all_gather.21 = bf16[2,192,768]{1,0,2:T(2,128)(2,1)S(1)} all-gather(bf16[2,192,96]{1,0,2:T(2,128)(2,1)S(1)} %copy.335), channel_id=1, replica_groups=mesh['dp'=8,'mp'=4] {'dp'}, dimensions={2}, use_global_device_ids=true | all-gather | bytes 663552 | tf_op jit(solution)/shard_map/all_gather | solution.py:146
  136.0 8.7 fusion.125
  144.7 6.4 copy.401
  151.0 3.7 fusion.127
  173.0 4.2 fusion.44
  190.1 5.3 reshape.466
  195.4 40.6 %all-reduce.11.cloned.1.call-done = bf16[1576,768]{1,0:T(8,128)(2,1)} async-done(((bf16[1576,768]{1,0:T(8,128)(2,1)}), bf16[1576,768]{1,0:T(8,128)(2,1)}) %all-reduce.11.cloned.1.call-update) | async-done | bytes 2420752 | tf_op jit(solution)/shard_map/psum | solution.py:107
  236.0 3.9 fusion.122
  243.2 48.0 %all-gather.7.cloned.1.call-done = bf16[2,768,768]{2,1,0:T(8,128)(2,1)} async-done(((bf16[2,96,768]{2,1,0:T(8,128)(2,1)}), bf16[2,768,768]{2,1,0:T(8,128)(2,1)}) %all-gather.7.cloned.1.call-update) | async-done | bytes 2359312 | tf_op jit(solution)/shard_map/all_gather | solution.py:147
  291.1 14.7 multiply_convert_fusion.4
  305.9 38.8 %all-gather.9.cloned.1.call-done = bf16[2,768,768]{1,2,0:T(8,128)(2,1)} async-done(((bf16[2,768,96]{1,2,0:T(8,128)(2,1)}), bf16[2,768,768]{1,2,0:T(8,128)(2,1)}) %all-gather.9.cloned.1.call-update) | async-done | bytes 2359312 | tf_op jit(solution)/shard_map/all_gather | solution.py:148
  344.7 5.6 convolution_convert_fusion.4
  351.9 4.4 copy.403
  356.3 49.4 %all-reduce.13.cloned.1.call-done = bf16[1576,768]{1,0:T(8,128)(2,1)} async-done(((bf16[1576,768]{1,0:T(8,128)(2,1)}), bf16[1576,768]{1,0:T(8,128)(2,1)}) %all-reduce.13.cloned.1.call-update) | async-done | bytes 2420752 | tf_op jit(solution)/shard_map/psum | solution.py:107
  405.6 3.9 fusion.120
  426.7 3.7 fusion.45
  439.2 6.2 fusion.104
  445.3 3.8 convert_element_type.372
  449.1 45.5 %all-reduce.15.cloned.1.call-done = bf16[1576,768]{1,0:T(8,128)(2,1)} async-done(((bf16[1576,768]{1,0:T(8,128)(2,1)}), bf16[1576,768]{1,0:T(8,128)(2,1)}) %all-reduce.15.cloned.1.call-update) | async-done | bytes 2420752 | tf_op jit(solution)/shard_map/psum | solution.py:107
  494.6 3.9 fusion.119
  502.5 32.7 %multiply_convert_fusion.3 = (bf16[1576,768]{1,0:T(8,128)(2,1)}, f32[1576,768]{1,0:T(8,128)S(1)}, f32[1576,768]{1,0:T(8,128)S(1)}) fusion(f32[768]{0:T(1024)S(1)} %get-tuple-element.147, bf16[1576,768]{1,0:T(8,128)(2,1)S(1)} %add_convert_fusion.3, bf16[2,768,768]{2,1,0:T(8,128)(2,1)S(1)} %copy-done.91), kind=kOutput, calls=%fused_computation.58 | convolution fusion | flops 1939009536 | bytes 15708160 | tf_op jit(solution)/shard_map/dot_general | solution.py:190
  535.2 5.2 convert_reduce_fusion.4
  545.4 5.1 reshape.472
  550.6 51.7 %all-reduce.17.cloned.1.call-done = bf16[1576,768]{1,0:T(8,128)(2,1)} async-done(((bf16[1576,768]{1,0:T(8,128)(2,1)}), bf16[1576,768]{1,0:T(8,128)(2,1)}) %all-reduce.17.cloned.1.call-update) | async-done | bytes 2420752 | tf_op jit(solution)/shard_map/psum | solution.py:111
  602.3 5.5 convert_reduce_fusion.3
  607.8 5.7 fusion.14
  613.4 4.3 fusion.113
  625.1 4.0 convert_reduce_fusion.7
  629.1 4.4 multiply_reduce_fusion.1
  642.5 4.7 bitcast_convert_fusion.1
  647.7 56.5 %all-reduce.19.cloned.1.call-done = bf16[1576,768]{1,0:T(8,128)(2,1)} async-done(((bf16[1576,768]{1,0:T(8,128)(2,1)}), bf16[1576,768]{1,0:T(8,128)(2,1)}) %all-reduce.19.cloned.1.call-update) | async-done | bytes 2420752 | tf_op jit(solution)/shard_map/psum | solution.py:111
  704.2 4.9 convert_reduce_fusion.2
  709.1 5.1 fusion.15
  714.2 5.0 fusion.111
  719.2 4.6 convert_reduce_fusion.5
  729.0 5.3 convolution_convert_fusion.2
  734.2 51.5 %all-reduce.21.cloned.1.call-done = bf16[1576,768]{1,0:T(8,128)(2,1)} async-done(((bf16[1576,768]{1,0:T(8,128)(2,1)}), bf16[1576,768]{1,0:T(8,128)(2,1)}) %all-reduce.21.cloned.1.call-update) | async-done | bytes 2420752 | tf_op jit(solution)/shard_map/psum | solution.py:111
  785.8 4.9 convert_reduce_fusion.1
  790.7 4.9 fusion.16
  795.6 5.0 fusion.112
  805.2 3.7 convert_reduce_fusion.9
  809.0 4.4 multiply_reduce_fusion
  822.0 5.0 bitcast_convert_fusion
  828.0 6.9 fusion.37
  838.6 7.1 convolution_bitcast_fusion
  850.8 72.8 %all-reduce.25.cloned.1.call-done = (bf16[1576,768]{1,0:T(8,128)(2,1)}, bf16[1576,768]{1,0:T(8,128)(2,1)}) async-done(((bf16[1576,768]{1,0:T(8,128)(2,1)}, bf16[1576,768]{1,0:T(8,128)(2,1)}), (bf16[1576,768]{1,0:T(8,128)(2,1)}, bf16[1576,768]{1,0:T(8,128)(2,1)})) %all-reduce.25.cloned.1.call-update) | async-done | bytes 4841488 | tf_op jit(solution)/shard_map/psum | solution.py:107
  923.5 9.6 convert_reduce_fusion
  939.0 4.8 pad_maximum_fusion.1
  943.8 8.2 copy.367
  952.1 5.0 convolution_bitcast_fusion.1
  962.2 4.2 fusion.129
  966.5 4.4 fusion.30
  972.9 6.8 copy.392
  979.7 8.0 reshape.489
  997.5 6.1 add_add_fusion.4
  1003.6 5.3 reshape.475
  1008.9 6.3 copy.377
  1015.2 5.3 reshape.471
  1025.4 77.7 %reduce-scatter.17.cloned.1.call-done = f32[288,2]{1,0:T(8,128)} async-done(((f32[9216,2]{1,0:T(8,128)}), f32[288,2]{1,0:T(8,128)}) %reduce-scatter.17.cloned.1.call-update) | async-done | bytes 2320
  1105.9 170.0 %all-reduce.23.cloned.1.call-done = f32[2,768,768]{1,0,2:T(2,128)} async-done(((f32[2,768,768]{1,0,2:T(2,128)}), f32[2,768,768]{1,0,2:T(2,128)}) %all-reduce.23.cloned.1.call-update) | async-done | bytes 4718608
  1279.8 94.4 %reduce-scatter.11.cloned.1.call-done = f32[2,96,768]{2,1,0:T(8,128)} async-done(((f32[2,768,768]{2,1,0:T(8,128)}), f32[2,96,768]{2,1,0:T(8,128)}) %reduce-scatter.11.cloned.1.call-update) | async-done | bytes 589840 | tf_op jit(solution)/shard_map/reduce_scatter | solution.py:316
  1377.0 80.3 %reduce-scatter.13.cloned.1.call-done = f32[96,1152]{1,0:T(8,128)} async-done(((f32[768,1152]{1,0:T(8,128)}), f32[96,1152]{1,0:T(8,128)}) %reduce-scatter.13.cloned.1.call-update) | async-done | bytes 442384
  (427 shorter events, 175.1 us)
Async XLA Ops:
  7.2 128.8 %all-gather.5.cloned.1.call-start = ((), (), s32[]{:S(2)}) async-start(), calls=%async_computation.4 | async-start | bytes 2654208 | tf_op jit(solution)/shard_map/all_gather | solution.py:145
  9.5 226.5 %all-reduce.11.cloned.1.call-start = ((), (), s32[]{:S(2)}) async-start(), calls=%async_computation.5 | async-start | bytes 4841472 | tf_op jit(solution)/shard_map/psum | solution.py:107
  10.4 79.4 %copy-start.7 = (bf16[8,197,768]{2,0,1:T(8,128)(2,1)S(1)}, bf16[8,197,768]{2,0,1:T(8,128)(2,1)}, u32[]{:S(2)}) copy-start(bf16[8,197,768]{2,0,1:T(8,128)(2,1)} %param.18) | copy-start | bytes 7262212
  93.2 148.4 %copy-start.54 = (f32[768]{0:T(1024)}, f32[768]{0:T(1024)S(1)}, u32[]{:S(2)}) copy-start(f32[768]{0:T(1024)S(1)} %get-tuple-element.143) | copy-start | bytes 9220
  94.4 6.6 copy-start.43
  100.9 62.0 %copy-start.64 = (f32[3,64]{1,0:T(4,128)}, f32[3,64]{1,0:T(4,128)S(1)}, u32[]{:S(2)}) copy-start(f32[3,64]{1,0:T(4,128)S(1)} %add.350) | copy-start | bytes 2308
  101.0 72.0 %copy-start.66 = (f32[3,64]{1,0:T(4,128)}, f32[3,64]{1,0:T(4,128)S(1)}, u32[]{:S(2)}) copy-start(f32[3,64]{1,0:T(4,128)S(1)} %add.347) | copy-start | bytes 2308
  135.9 44.5 %copy-start.27 = (bf16[1,192,768]{2,1,0:T(8,128)(2,1)}, bf16[1,192,768]{2,1,0:T(8,128)(2,1)S(1)}, u32[]{:S(2)}) copy-start(bf16[1,192,768]{2,1,0:T(8,128)(2,1)S(1)} %copy.402) | copy-start | bytes 884740
  169.4 7.8 copy-start.41
  180.5 8.8 copy-start.22
  182.8 108.4 %all-gather.7.cloned.1.call-start = ((), (), s32[]{:S(2)}) async-start(), calls=%async_computation.6 | async-start | bytes 2654208 | tf_op jit(solution)/shard_map/all_gather | solution.py:147
  184.7 160.0 %all-gather.9.cloned.1.call-start = ((), (), s32[]{:S(2)}) async-start(), calls=%async_computation.7 | async-start | bytes 2654208 | tf_op jit(solution)/shard_map/all_gather | solution.py:148
  186.6 219.1 %all-reduce.13.cloned.1.call-start = ((), (), s32[]{:S(2)}) async-start(), calls=%async_computation.8 | async-start | bytes 4841472 | tf_op jit(solution)/shard_map/psum | solution.py:107
  190.1 101.1 %copy-start.81 = (f32[768]{0:T(1024)}, f32[768]{0:T(1024)S(1)}, u32[]{:S(2)}) copy-start(f32[768]{0:T(1024)S(1)} %get-tuple-element.148) | copy-start | bytes 9220
  190.1 45.9 %copy-start.77 = (f32[768]{0:T(1024)S(1)}, f32[768]{0:T(1024)}, u32[]{:S(2)}) copy-start(f32[768]{0:T(1024)} %get-tuple-element.144) | copy-start | bytes 9220
  243.1 62.7 %copy-start.29 = (bf16[1576,768]{1,0:T(8,128)(2,1)}, bf16[1576,768]{1,0:T(8,128)(2,1)S(1)}, u32[]{:S(2)}) copy-start(bf16[1576,768]{1,0:T(8,128)(2,1)S(1)} %add_convert_fusion.5) | copy-start | bytes 7262212
  350.2 55.4 %copy-start.76 = (f32[768]{0:T(1024)S(1)}, f32[768]{0:T(1024)}, u32[]{:S(2)}) copy-start(f32[768]{0:T(1024)} %get-tuple-element.141) | copy-start | bytes 9220
  350.3 144.4 %all-reduce.15.cloned.1.call-start = ((), (), s32[]{:S(2)}) async-start(), calls=%async_computation.9 | async-start | bytes 4841472 | tf_op jit(solution)/shard_map/psum | solution.py:107
  437.7 164.6 %all-reduce.17.cloned.1.call-start = ((), (), s32[]{:S(2)}) async-start(), calls=%async_computation.10 | async-start | bytes 4841472 | tf_op jit(solution)/shard_map/psum | solution.py:111
  445.3 49.3 %copy-start.74 = (f32[768]{0:T(1024)S(1)}, f32[768]{0:T(1024)}, u32[]{:S(2)}) copy-start(f32[768]{0:T(1024)} %get-tuple-element.138) | copy-start | bytes 9220
  500.7 34.5 %copy-start.32 = (bf16[1576,768]{1,0:T(8,128)(2,1)}, bf16[1576,768]{1,0:T(8,128)(2,1)S(1)}, u32[]{:S(2)}) copy-start(bf16[1576,768]{1,0:T(8,128)(2,1)S(1)} %add_convert_fusion.3) | copy-start | bytes 7262212
  502.5 32.7 %copy-start.33 = (bf16[1576,768]{1,0:T(8,128)(2,1)S(1)}, bf16[1576,768]{1,0:T(8,128)(2,1)}, u32[]{:S(2)}) copy-start(bf16[1576,768]{1,0:T(8,128)(2,1)} %convert_element_type.372) | copy-start | bytes 7262212
  502.5 32.7 %copy-start.89 = (bf16[2,768,768]{1,2,0:T(8,128)(2,1)S(1)}, bf16[2,768,768]{1,2,0:T(8,128)(2,1)}, u32[]{:S(2)}) copy-start(bf16[2,768,768]{1,2,0:T(8,128)(2,1)} %all-gather.9.cloned.1.call-done) | copy-start | bytes 7077892
  545.4 158.8 %all-reduce.19.cloned.1.call-start = ((), (), s32[]{:S(2)}) async-start(), calls=%async_computation.11 | async-start | bytes 4841472 | tf_op jit(solution)/shard_map/psum | solution.py:111
  625.1 8.4 slice-start.2
  647.2 138.5 %all-reduce.21.cloned.1.call-start = ((), (), s32[]{:S(2)}) async-start(), calls=%async_computation.12 | async-start | bytes 4841472 | tf_op jit(solution)/shard_map/psum | solution.py:111
  709.0 10.1 slice-start.8
  709.1 10.1 slice-start.10
  728.9 194.7 %all-reduce.25.cloned.1.call-start = ((), (), s32[]{:S(2)}) async-start(), calls=%async_computation.18 | async-start | bytes 9682944 | tf_op jit(solution)/shard_map/psum | solution.py:107
  728.9 56.9 %copy-start.47 = (f32[1576]{0:T(1024)S(1)}, f32[1576]{0:T(1024)}, u32[]{:S(2)}) copy-start(f32[1576]{0:T(1024)} %copy-done.46) | copy-start | bytes 18916
  728.9 56.8 %copy-start.55 = (f32[768]{0:T(1024)S(1)}, f32[768]{0:T(1024)}, u32[]{:S(2)}) copy-start(f32[768]{0:T(1024)} %copy-done.54) | copy-start | bytes 9220
  734.2 56.4 %copy-start.59 = (f32[1576]{0:T(1024)S(1)}, f32[1576]{0:T(1024)}, u32[]{:S(2)}) copy-start(f32[1576]{0:T(1024)} %copy-done.58) | copy-start | bytes 18916
  734.2 56.4 %copy-start.53 = (f32[1576]{0:T(1024)S(1)}, f32[1576]{0:T(1024)}, u32[]{:S(2)}) copy-start(f32[1576]{0:T(1024)} %copy-done.52) | copy-start | bytes 18916
  795.6 7.3 copy-start.28
  805.2 8.2 slice-start
  827.0 167.4 %reduce-scatter.15.cloned.1.call-start = ((), (), s32[]{:S(2)}) async-start(), calls=%async_computation.15 | async-start | bytes 1327104
  827.9 7.0 copy-start.70
  827.9 7.0 copy-start.69
  828.0 7.1 copy-start.80
  828.0 7.3 copy-start.24
  835.3 10.4 slice-start.6
  838.6 7.1 slice-start.7
  838.6 7.1 copy-start.23
  846.5 77.0 %copy-start.57 = (f32[768]{0:T(1024)S(1)}, f32[768]{0:T(1024)}, u32[]{:S(2)}) copy-start(f32[768]{0:T(1024)} %copy-done.56) | copy-start | bytes 9220
  846.5 77.0 %copy-start.78 = (f32[768]{0:T(1024)S(1)}, f32[768]{0:T(1024)}, u32[]{:S(2)}) copy-start(f32[768]{0:T(1024)} %get-tuple-element.135) | copy-start | bytes 9220
  846.6 86.5 %slice-start.4 = ((s8[4841472]{0:T(1024)(128)(4,1)}), s8[647168]{0:T(1024)(128)(4,1)S(1)}, s32[]{:S(2)}) async-start(s8[4841472]{0:T(1024)(128)(4,1)} %bitcast.195), calls=%async_computation.23 | async-start | bytes 1294336
  849.7 253.3 %reduce-scatter.17.cloned.1.call-start = ((), (), s32[]{:S(2)}) async-start(), calls=%async_computation.16 | async-start | bytes 4866048
  923.5 9.6 slice-start.5
  923.5 9.6 copy-start.8
  939.0 336.9 %all-reduce.23.cloned.1.call-start = ((), (), s32[]{:S(2)}) async-start(), calls=%async_computation.17 | async-start | bytes 9437184
  952.1 422.0 %reduce-scatter.11.cloned.1.call-start = ((), (), s32[]{:S(2)}) async-start(), calls=%async_computation.13 | async-start | bytes 5308416 | tf_op jit(solution)/shard_map/reduce_scatter | solution.py:316
  962.0 495.3 %reduce-scatter.13.cloned.1.call-start = ((), (), s32[]{:S(2)}) async-start(), calls=%async_computation.14 | async-start | bytes 3981312
  979.7 8.1 copy-start.34
  987.8 7.9 copy-start.44
  987.8 7.9 copy-start.51
  1020.5 83.6 %copy-start.79 = (f32[2,1,1,288]{3,2,1,0:T(1,128)S(1)}, f32[2,1,1,288]{3,2,1,0:T(1,128)}, u32[]{:S(2)}) copy-start(f32[2,1,1,288]{3,2,1,0:T(1,128)} %param.25) | copy-start | bytes 6916
  1020.5 83.6 %copy-start.85 = (f32[2,1,1,288]{3,2,1,0:T(1,128)S(1)}, f32[2,1,1,288]{3,2,1,0:T(1,128)}, u32[]{:S(2)}) copy-start(f32[2,1,1,288]{3,2,1,0:T(1,128)} %param.35) | copy-start | bytes 6916
  1020.5 83.6 %copy-start.86 = (f32[2,1,1,288]{3,2,1,0:T(1,128)S(1)}, f32[2,1,1,288]{3,2,1,0:T(1,128)}, u32[]{:S(2)}) copy-start(f32[2,1,1,288]{3,2,1,0:T(1,128)} %param.34) | copy-start | bytes 6916
  1023.5 253.6 %copy-start.35 = (f32[2,768,96]{1,2,0:T(8,128)S(1)}, f32[2,768,96]{1,2,0:T(8,128)}, u32[]{:S(2)}) copy-start(f32[2,768,96]{1,2,0:T(8,128)} %param.24) | copy-start | bytes 1769476
  1023.5 253.5 %copy-start.45 = (f32[2,768,96]{1,2,0:T(8,128)S(1)}, f32[2,768,96]{1,2,0:T(8,128)}, u32[]{:S(2)}) copy-start(f32[2,768,96]{1,2,0:T(8,128)} %param.33) | copy-start | bytes 1769476
  1023.5 350.6 %copy-start.36 = (f32[2,96,768]{2,1,0:T(8,128)S(1)}, f32[2,96,768]{2,1,0:T(8,128)}, u32[]{:S(2)}) copy-start(f32[2,96,768]{2,1,0:T(8,128)} %param.23) | copy-start | bytes 1769476
  1277.0 183.0 %copy-start.37 = (f32[2,96,3,192]{1,3,2,0:T(8,128)S(1)}, f32[2,96,3,192]{1,3,2,0:T(8,128)}, u32[]{:S(2)}) copy-start(f32[2,96,3,192]{1,3,2,0:T(8,128)} %copy.366) | copy-start | bytes 1327108
  1277.0 183.0 %copy-start.38 = (f32[2,96,3,192]{1,3,2,0:T(8,128)S(1)}, f32[2,96,3,192]{1,3,2,0:T(8,128)}, u32[]{:S(2)}) copy-start(f32[2,96,3,192]{1,3,2,0:T(8,128)} %copy.363) | copy-start | bytes 1327108
  1277.1 183.0 %copy-start.39 = (f32[2,96,3,192]{1,3,2,0:T(8,128)S(1)}, f32[2,96,3,192]{1,3,2,0:T(8,128)}, u32[]{:S(2)}) copy-start(f32[2,96,3,192]{1,3,2,0:T(8,128)} %copy.364) | copy-start | bytes 1327108
  (60 other events, 190.8 us)
Sparse Core Ops, SparseCore 0:
  10.8 65.3 all-gather.4
  182.9 53.0 all-reduce.10
  239.0 52.1 all-gather.6
  294.0 50.6 all-gather.8
  350.4 55.2 all-reduce.12
  437.8 56.7 all-reduce.14
  545.5 56.7 all-reduce.16
  647.4 56.7 all-reduce.18
  729.0 56.7 all-reduce.20
  827.2 96.3 all-reduce.24
  927.5 64.1 reduce-scatter.14
  997.1 105.9 reduce-scatter.16
  1107.1 168.7 all-reduce.22
  1279.8 94.2 reduce-scatter.10
  1378.0 79.2 reduce-scatter.12
where the time goes:
time: 1480 us; the launch traced here: 1470 us
  waiting for transfers between devices  877 us (59%)
  local copies, waits for them, and re-layouts  182 us (12%)
  matrix products  166 us (11%)
  other arithmetic  119 us (8%)
  blocking collectives  108 us (7%)
  between operations  17.3 us (1%)
    unnamed x19, waiting for transfers between devices  328 us
    psum x4, waiting for transfers between devices, branch_sum(): return lax.psum(partial_rows.astype(jnp.bfloat16), 'mp').astype(jnp.float32)  208 us
    psum x3, waiting for transfers between devices, input_sum(): return lax.psum(partial_rows.astype(jnp.bfloat16), 'mp').astype(jnp.float32)  160 us
    reduce_scatter x1, waiting for transfers between devices, on_device(): lax.psum_scatter(jnp.stack(up_grads), 'dp', scatter_dimension=1, tiled=True)  94.4 us
    unnamed x253, local copies, waits for them, and re-layouts  83.2 us
    all_gather x1, blocking collectives, on_device(): lax.all_gather(vectors.reshape(layers, -1), ('dp', 'mp'), axis=1, tiled=T...  75.7 us
    all_gather x1, waiting for transfers between devices, on_device(): lax.all_gather(up_weight.astype(bf16), 'dp', axis=1, tiled=True)  48 us
    dot_general x2, matrix products, on_device(): jnp.dot(mixed_low, up_layer, preferred_element_type=f32)  47.4 us
  transfers between devices with their start and end apart: 15, of which 13 were waited for; matrix products, arithmetic and copies ran while one was open for 14% of the time, Pallas kernels for 0%

commit v1 on v0

v1 whole, which is shorter than its diff:
```python
import functools

import jax
import jax.numpy as jnp
from jax import lax
from jax.experimental import pallas as pl
from jax.experimental.pallas import tpu as pltpu
from jax.sharding import PartitionSpec as P

D = 768
HEAD_DIM = 64
STEP = 10
ROW_TILE = 16

norm_epsilon = 1e-06
bf16 = jnp.bfloat16
f32 = jnp.float32


def norm_stats(values):
    average = jnp.mean(values, axis=-1, keepdims=True)
    centered = values - average
    variance = jnp.mean(centered * centered, axis=-1, keepdims=True)
    scale = lax.rsqrt(variance + norm_epsilon)
    return centered * scale, scale


def norm_back(values, gain_row, grad_rows):
    unit_rows, scale = norm_stats(values)
    scaled = grad_rows * gain_row
    back = scale * (
        scaled
        - jnp.mean(scaled, axis=-1, keepdims=True)
        - unit_rows * jnp.mean(scaled * unit_rows, axis=-1, keepdims=True)
    )
    return back, jnp.sum(grad_rows * unit_rows, axis=0), jnp.sum(grad_rows, axis=0)


def gelu_exact(values):
    return values * 0.5 * (1.0 + lax.erf(values * 0.5**0.5))


def gelu_slope(values):
    bell = jnp.exp(-0.5 * values * values) * (2.0 * jnp.pi) ** -0.5
    return 0.5 * (1.0 + lax.erf(values * 0.5**0.5)) + values * bell


def adam_update(weight, first_moment, second_moment, gradient, step_rate, decay_rate):
    first_new = 0.9 * first_moment + 0.1 * gradient
    second_new = 0.95 * second_moment + 0.05 * gradient * gradient
    first_hat = first_new / (1.0 - 0.9**STEP)
    second_hat = second_new / (1.0 - 0.95**STEP)
    weight_new = weight - step_rate * (
        first_hat / (jnp.sqrt(second_hat) + 1e-08) + decay_rate * weight
    )
    return (first_new, second_new, weight_new)


def dot_nn(left, right):
    return lax.dot_general(left, right, (((1,), (0,)), ((), ())), preferred_element_type=f32)


def dot_nt(left, right):
    return lax.dot_general(left, right, (((1,), (1,)), ((), ())), preferred_element_type=f32)


def dot_tn(left, right):
    return lax.dot_general(left, right, (((0,), (0,)), ((), ())), preferred_element_type=f32)


def head_probs(query, key, seq_len):
    scores = dot_nt(query, key) * HEAD_DIM ** (-0.5)
    column = lax.broadcasted_iota(jnp.int32, scores.shape, 1)
    scores = jnp.where(column < seq_len, scores, -1e30)
    raised = jnp.exp(scores - jnp.max(scores, axis=-1, keepdims=True))
    return raised * (1.0 / jnp.sum(raised, axis=-1, keepdims=True))


def attention_forward_kernel(seq_len, qkv_ref, out_ref):
    width = out_ref.shape[1]
    for at in range(0, width, HEAD_DIM):
        query = qkv_ref[:, at : at + HEAD_DIM]
        key = qkv_ref[:, width + at : width + at + HEAD_DIM]
        value = qkv_ref[:, 2 * width + at : 2 * width + at + HEAD_DIM]
        probs = head_probs(query, key, seq_len).astype(bf16)
        out_ref[:, at : at + HEAD_DIM] = dot_nn(probs, value).astype(bf16)


def attention_backward_kernel(seq_len, qkv_ref, grad_ref, out_ref):
    width = grad_ref.shape[1]
    for at in range(0, width, HEAD_DIM):
        query = qkv_ref[:, at : at + HEAD_DIM]
        key = qkv_ref[:, width + at : width + at + HEAD_DIM]
        value = qkv_ref[:, 2 * width + at : 2 * width + at + HEAD_DIM]
        grad = grad_ref[:, at : at + HEAD_DIM]
        probs = head_probs(query, key, seq_len)
        value_grad = dot_tn(probs.astype(bf16), grad)
        prob_grad = dot_nt(grad, value)
        score_grad = (
            probs * (prob_grad - jnp.sum(probs * prob_grad, axis=-1, keepdims=True))
        ).astype(bf16)
        query_grad = dot_nn(score_grad, key) * HEAD_DIM ** (-0.5)
        key_grad = dot_tn(score_grad, query) * HEAD_DIM ** (-0.5)
        out_ref[:, at : at + HEAD_DIM] = query_grad.astype(bf16)
        out_ref[:, width + at : width + at + HEAD_DIM] = key_grad.astype(bf16)
        out_ref[:, 2 * width + at : 2 * width + at + HEAD_DIM] = value_grad.astype(bf16)


def image_block(rows, columns):
    return pl.BlockSpec((rows, columns), lambda image: (image, 0))


def attention_forward(qkv_rows, images, seq_len):
    rows, width = qkv_rows.shape
    pad_len = rows // images
    return pl.pallas_call(
        functools.partial(attention_forward_kernel, seq_len),
        grid=(images,),
        in_specs=[image_block(pad_len, width)],
        out_specs=image_block(pad_len, width // 3),
        out_shape=jax.ShapeDtypeStruct((rows, width // 3), bf16),
        cost_estimate=pl.CostEstimate(
            flops=4 * rows * pad_len * (width // 3),
            bytes_accessed=rows * width * 3,
            transcendentals=rows * pad_len * (width // 3 // HEAD_DIM),
        ),
    )(qkv_rows)


def attention_backward(qkv_rows, grad_rows, images, seq_len):
    rows, width = qkv_rows.shape
    pad_len = rows // images
    return pl.pallas_call(
        functools.partial(attention_backward_kernel, seq_len),
        grid=(images,),
        in_specs=[image_block(pad_len, width), image_block(pad_len, width // 3)],
        out_specs=image_block(pad_len, width),
        out_shape=jax.ShapeDtypeStruct((rows, width), bf16),
        cost_estimate=pl.CostEstimate(
            flops=10 * rows * pad_len * (width // 3),
            bytes_accessed=rows * width * 5,
            transcendentals=rows * pad_len * (width // 3 // HEAD_DIM),
        ),
    )(qkv_rows, grad_rows)


def on_device(
    inputs,
    cotangent,
    counts,
    qkv_weight,
    out_weight,
    up_weight,
    down_weight,
    vectors,
    qkv_first,
    qkv_second,
    out_first,
    out_second,
    up_first,
    up_second,
    down_first,
    down_second,
    vector_first,
    vector_second,
):
    slot_count, seq_len, model_width = inputs.shape
    dp_count = lax.axis_size("dp")
    mp_count = lax.axis_size("mp")
    mp_index = lax.axis_index("mp")
    layers, shard_rows, _, head_cols = qkv_weight.shape
    hidden_cols = up_weight.shape[2]
    qkv_cols = 3 * head_cols
    row_width = 6 * model_width // mp_count
    half = mp_count // 2
    side = mp_index // half
    pair_swap = [(i, i ^ 1) for i in range(mp_count)]
    side_swap = [(i, (i + half) % mp_count) for i in range(mp_count)]
    own_at = mp_index
    other_at = lax.rem(mp_index + half, mp_count)
    images = slot_count // 2
    pad_len = -(-seq_len // ROW_TILE) * ROW_TILE
    rows = images * pad_len

    def to_pair(values):
        return lax.ppermute(values, "mp", pair_swap)

    def to_side(values):
        return lax.ppermute(values, "mp", side_swap)

    def pair_sum(partial_rows):
        low = partial_rows.astype(bf16)
        return low.astype(f32) + to_pair(low).astype(f32)

    vector_rows = lax.all_gather(vectors.reshape(1, -1), ("dp", "mp"), axis=0, tiled=True)
    vector_blocks = (
        vector_rows.reshape(dp_count, mp_count, layers, -1)
        .transpose(2, 1, 0, 3)
        .reshape(layers, mp_count, -1)
    )
    row_part = vector_blocks[:, :, :row_width].reshape(layers, 6, model_width)
    tails = vector_blocks[:, :, row_width:]
    tail_pair = [lax.dynamic_index_in_dim(tails, at, 1, keepdims=False) for at in (own_at, other_at)]

    def shard_pieces(layer):
        qkv_out = jnp.concatenate(
            [qkv_weight[layer].reshape(shard_rows, qkv_cols), out_weight[layer].T], axis=1
        )
        return qkv_out, up_weight[layer], down_weight[layer].T

    pieces = []
    for layer in range(layers):
        layer_pieces = []
        for piece in shard_pieces(layer):
            own = lax.all_gather(piece.astype(bf16), "dp", axis=0, tiled=True)
            layer_pieces.append((own, to_side(own)))
        pieces.append(layer_pieces)

    def own_images(values):
        mine = lax.dynamic_slice_in_dim(values, side * images, images, 0)
        mine = jnp.pad(mine, ((0, 0), (0, pad_len - seq_len), (0, 0)))
        return mine.reshape(rows, model_width).astype(f32)

    def all_images(values):
        own = values.reshape(images, pad_len, model_width)[:, :seq_len]
        other = to_side(own)
        return lax.dynamic_slice_in_dim(
            jnp.concatenate([own, other, own]), side * images, slot_count, 0
        )

    live = (
        (side * images + jnp.arange(images, dtype=jnp.int32) < counts[0])
        .astype(f32)
        .reshape(images, 1, 1)
    )

    def mask_live(values):
        return (values.reshape(images, pad_len, model_width) * live).reshape(rows, model_width)

    stream = own_images(inputs)
    kept = []
    for layer in range(layers):
        gain1, shift1, gain2, shift2, out_bias, down_bias = (row_part[layer, i] for i in range(6))
        attn_pair, up_pair, down_pair = pieces[layer]
        normed = (norm_stats(stream)[0] * gain1 + shift1).astype(bf16)
        qkv_pair, attended_pair, hidden_pair, active_pair = [], [], [], []
        branch = None
        for weight, tail in zip(attn_pair, tail_pair):
            bias = jnp.concatenate(
                [
                    tail[layer, :head_cols],
                    jnp.zeros((head_cols,), f32),
                    tail[layer, head_cols : 2 * head_cols],
                ]
            )
            qkv = (dot_nn(normed, weight[:, :qkv_cols]) + bias).astype(bf16)
            attended = attention_forward(qkv, images, seq_len)
            term = dot_nt(attended, weight[:, qkv_cols:])
            branch = term if branch is None else branch + term
            qkv_pair.append(qkv)
            attended_pair.append(attended)
        middle = stream + pair_sum(branch) + out_bias
        mixed = (norm_stats(middle)[0] * gain2 + shift2).astype(bf16)
        branch = None
        for up, down, tail in zip(up_pair, down_pair, tail_pair):
            hidden = dot_nn(mixed, up) + tail[layer, 2 * head_cols :]
            active = gelu_exact(hidden).astype(bf16)
            term = dot_nt(active, down)
            branch = term if branch is None else branch + term
            hidden_pair.append(hidden)
            active_pair.append(active)
        following = middle + pair_sum(branch) + down_bias
        kept.append((stream, normed, qkv_pair, attended_pair, middle, mixed, hidden_pair, active_pair))
        stream = following
    output_tokens = all_images(mask_live(stream).astype(bf16))

    def owner_sum(own_grad, other_grad):
        arrived = to_side(other_grad.astype(bf16))
        total = (own_grad + arrived.astype(f32)).astype(bf16)
        return lax.psum_scatter(total, "dp", scatter_dimension=0, tiled=True).astype(f32)

    upstream = mask_live(own_images(cotangent))
    grads = [None] * layers
    row_grads = [None] * layers
    column_grads = [None] * layers
    for layer in reversed(range(layers)):
        stream_in, normed, qkv_pair, attended_pair, middle, mixed, hidden_pair, active_pair = kept[
            layer
        ]
        gain1, gain2 = row_part[layer, 0], row_part[layer, 2]
        attn_pair, up_pair, down_pair = pieces[layer]
        upstream_low = upstream.astype(bf16)
        down_bias_grad = jnp.sum(upstream, axis=0)
        down_pieces, up_pieces, hidden_sums, qkv_sums = [], [], [], []
        branch = None
        for up, down, hidden, active in zip(up_pair, down_pair, hidden_pair, active_pair):
            down_pieces.append(dot_tn(upstream_low, active))
            hidden_low = (dot_nn(upstream_low, down) * gelu_slope(hidden)).astype(bf16)
            up_pieces.append(dot_tn(mixed, hidden_low))
            hidden_sums.append(jnp.sum(hidden_low.astype(f32), axis=0))
            term = dot_nt(hidden_low, up)
            branch = term if branch is None else branch + term
        mixed_grad = pair_sum(branch)
        down_grad = owner_sum(*down_pieces)
        up_grad = owner_sum(*up_pieces)
        middle_part, gain2_grad, shift2_grad = norm_back(middle, gain2, mixed_grad)
        middle_grad = upstream + middle_part
        middle_low = middle_grad.astype(bf16)
        out_bias_grad = jnp.sum(middle_grad, axis=0)
        attn_pieces = []
        branch = None
        for weight, qkv, attended in zip(attn_pair, qkv_pair, attended_pair):
            attended_grad = dot_nn(middle_low, weight[:, qkv_cols:]).astype(bf16)
            qkv_grad = attention_backward(qkv, attended_grad, images, seq_len)
            attn_pieces.append(
                jnp.concatenate([dot_tn(normed, qkv_grad), dot_tn(middle_low, attended)], axis=1)
            )
            sums = jnp.sum(qkv_grad.astype(f32), axis=0)
            qkv_sums.append(jnp.concatenate([sums[:head_cols], sums[2 * head_cols :]]))
            term = dot_nt(qkv_grad, weight[:, :qkv_cols])
            branch = term if branch is None else branch + term
        normed_grad = pair_sum(branch)
        attn_grad = owner_sum(*attn_pieces)
        stream_part, gain1_grad, shift1_grad = norm_back(stream_in, gain1, normed_grad)
        upstream = middle_grad + stream_part
        grads[layer] = (
            attn_grad[:, :qkv_cols].reshape(shard_rows, 3, head_cols),
            attn_grad[:, qkv_cols:].T,
            up_grad,
            down_grad.T,
        )
        row_grads[layer] = jnp.stack(
            [gain1_grad, shift1_grad, gain2_grad, shift2_grad, out_bias_grad, down_bias_grad]
        )
        column_grads[layer] = [
            jnp.concatenate([a, b]) for a, b in zip(qkv_sums, hidden_sums)
        ]
    input_grad = all_images(upstream.astype(bf16)).astype(f32)

    first_mask = (lax.rem(mp_index, 2) == 0).astype(f32)
    block_id = jnp.arange(mp_count, dtype=jnp.int32)
    placed = sum(
        jnp.stack([column_grads[layer][which] for layer in range(layers)])[:, None, :]
        * (block_id == at).astype(f32)[None, :, None]
        for which, at in enumerate((own_at, other_at))
    )
    row_blocks = (jnp.stack(row_grads) * first_mask).reshape(layers, mp_count, row_width)
    vector_grad = (
        jnp.concatenate([row_blocks, placed], axis=2)
        .reshape(layers, mp_count, dp_count, -1)
        .transpose(2, 1, 0, 3)
        .reshape(dp_count * mp_count, -1)
    )
    vector_grad = lax.psum_scatter(
        vector_grad, ("dp", "mp"), scatter_dimension=0, tiled=True
    ).reshape(vectors.shape)

    matrix_rate = 3.0 / D**0.5

    def update(which, weight, first, second):
        gradient = jnp.stack([grads[layer][which] for layer in range(layers)])
        return adam_update(weight, first, second, gradient, matrix_rate, 0.1)

    qkv_new = update(0, qkv_weight, qkv_first, qkv_second)
    out_new = update(1, out_weight, out_first, out_second)
    up_new = update(2, up_weight, up_first, up_second)
    down_new = update(3, down_weight, down_first, down_second)
    vector_new = adam_update(vectors, vector_first, vector_second, vector_grad, 0.5, 0.0)
    return (
        output_tokens,
        input_grad,
        qkv_new[0],
        qkv_new[1],
        qkv_new[2],
        out_new[0],
        out_new[1],
        out_new[2],
        up_new[0],
        up_new[1],
        up_new[2],
        down_new[0],
        down_new[1],
        down_new[2],
        vector_new[0],
        vector_new[1],
        vector_new[2],
    )


def solution(mesh):
    placed = (
        P("dp", None, None),
        P("dp", None, None),
        P("dp"),
        P(None, "dp", None, "mp"),
        P(None, "mp", "dp"),
        P(None, "dp", "mp"),
        P(None, "mp", "dp"),
        P(None, "mp", "dp", None),
        P(None, "dp", None, "mp"),
        P(None, "dp", None, "mp"),
        P(None, "mp", "dp"),
        P(None, "mp", "dp"),
        P(None, "dp", "mp"),
        P(None, "dp", "mp"),
        P(None, "mp", "dp"),
        P(None, "mp", "dp"),
        P(None, "mp", "dp", None),
        P(None, "mp", "dp", None),
    )
    return jax.shard_map(
        on_device,
        mesh=mesh,
        in_specs=placed,
        out_specs=(
            P("dp", None, None),
            P("dp", None, None),
            P(None, "dp", None, "mp"),
            P(None, "dp", None, "mp"),
            P(None, "dp", None, "mp"),
            P(None, "mp", "dp"),
            P(None, "mp", "dp"),
            P(None, "mp", "dp"),
            P(None, "dp", "mp"),
            P(None, "dp", "mp"),
            P(None, "dp", "mp"),
            P(None, "mp", "dp"),
            P(None, "mp", "dp"),
            P(None, "mp", "dp"),
            P(None, "mp", "dp", None),
            P(None, "mp", "dp", None),
            P(None, "mp", "dp", None),
        ),
        check_vma=False,
    )
```

time: 1480 us -> 955 us (0.65)
  waiting for transfers between devices: 877 us -> 560 us
  local copies, waits for them, and re-layouts: 182 us -> 50.7 us
  Pallas kernels: 0 us -> 65.1 us
  blocking collectives: 108 us -> 43.6 us
  matrix products: 166 us -> 115 us
  other arithmetic: 119 us -> 75.5 us
  starting transfers between devices: 1.82 us -> 18.5 us
    psum x7 -> x0, waiting for transfers between devices: 368 us -> none  [the longest x4 208 us: branch_sum(): return lax.psum(partial_rows.astype(jnp.bfloat16), 'mp').astype(jnp.float32)]
    unnamed x19 -> x16, waiting for transfers between devices: 328 us -> 57.8 us
    ppermute x0 -> x22, waiting for transfers between devices: none -> 195 us  [the longest x14 195 us: to_side(): return lax.ppermute(values, 'mp', side_swap)]
    reduce_scatter x1 -> x4, waiting for transfers between devices: 94.4 us -> 230 us  [owner_sum(): lax.psum_scatter(total, 'dp', scatter_dimension=0, tiled=True).astype(f32)]
    pallas_call x0 -> x8, Pallas kernels: none -> 65.1 us  [the longest x4 41.4 us: attention_backward(): pl.pallas_call(functools.partial(attention_backward_kernel, seq_len), gri...]
    all_gather x2 -> x1, blocking collectives: 108 us -> 43.6 us  [on_device(): lax.all_gather(vectors.reshape(1, -1), ('dp', 'mp'), axis=0, tiled=True)]
    unnamed x253 -> x177, local copies, waits for them, and re-layouts: 83.2 us -> 28.6 us
    reduce_sum x18 -> x16, other arithmetic: 59.9 us -> 22.3 us  [the longest x4 12.7 us: norm_back(): jnp.sum(grad_rows * unit_rows, axis=0)]
  transfers between devices with their start and end apart: 15 -> 35, of which waited for: 13 -> 18; matrix products, arithmetic and copies ran while one was open for 14% -> 21% of each run, Pallas kernels for 0% -> 5%
where the time goes in v1:
time: 955 us; the launch traced here: 945 us
  waiting for transfers between devices  560 us (59%)
  matrix products  115 us (12%)
  other arithmetic  75.5 us (8%)
  Pallas kernels  65.1 us (7%)
  local copies, waits for them, and re-layouts  50.7 us (5%)
  blocking collectives  43.6 us (5%)
  starting transfers between devices  18.5 us (2%)
  between operations  16.7 us (2%)
    reduce_scatter x4, waiting for transfers between devices, owner_sum(): lax.psum_scatter(total, 'dp', scatter_dimension=0, tiled=True).astype(f32)  230 us
    ppermute x14, waiting for transfers between devices, to_side(): return lax.ppermute(values, 'mp', side_swap)  195 us
    all_gather x6, waiting for transfers between devices, on_device(): own = lax.all_gather(piece.astype(bf16), 'dp', axis=0, tiled=True)  77.8 us
    unnamed x16, waiting for transfers between devices  57.8 us
    all_gather x1, blocking collectives, on_device(): lax.all_gather(vectors.reshape(1, -1), ('dp', 'mp'), axis=0, tiled=True)  43.6 us
    pallas_call x4, Pallas kernels, attention_backward(): pl.pallas_call(functools.partial(attention_backward_kernel, seq_len), gri...  41.4 us
    dot_general x16, matrix products, dot_nn(): lax.dot_general(left, right, (((1,), (0,)), ((), ())), preferred_element_...  39.7 us
    dot_general x16, matrix products, dot_nt(): lax.dot_general(left, right, (((1,), (1,)), ((), ())), preferred_element_...  39 us
  transfers between devices with their start and end apart: 35, of which 18 were waited for; matrix products, arithmetic and copies ran while one was open for 21% of the time, Pallas kernels for 5%

profile of v1, /device:TPU:0, one launch (start us, length us, event | category | flops | bytes accessed | tf_op | source)
XLA Modules:
  0.0 945.1 jit_solution(14585055295082912473)
XLA Ops:
  13.3 4.7 constant_dynamic-slice_fusion
  20.9 43.6 %all-gather.2 = f32[32,1,576]{2,1,0:T(1,128)S(1)} all-gather(f32[1,1,576]{2,1,0:T(1,128)S(1)} %reshape.280), channel_id=1, replica_groups=mesh['dp'=8,'mp'=4] {'dp','mp'}, dimensions={0}, use_global_device_ids=true | all-gather | bytes 76032 | tf_op jit(solution)/shard_map/all_gather | solution.py:195
  74.4 5.9 shard_map.305
  80.3 3.3 fusion.67
  83.6 11.3 %collective-permute-done = bf16[768,768]{1,0:T(8,128)(2,1)} collective-permute-done((bf16[768,768]{1,0:T(8,128)(2,1)}, bf16[768,768]{1,0:T(8,128)(2,1)}, u32[]{:S(2)}, u32[]{:S(2)}) %collective-permute-start) | collective-permute-done | bytes 1179680 | tf_op jit(solution)/shard_map/ppermute | solution.py:189
  94.9 3.4 add_convert_fusion.19.qkv_ref
  98.3 5.9 shard_map.306
  104.2 3.7 add_convert_fusion.11
  108.9 31.2 %all-gather.12.cloned.1.call-done = bf16[768,768]{1,0:T(8,128)(2,1)} async-done(((bf16[96,768]{1,0:T(8,128)(2,1)}), bf16[768,768]{1,0:T(8,128)(2,1)}) %all-gather.12.cloned.1.call-update) | async-done | bytes 1179664 | tf_op jit(solution)/shard_map/all_gather | solution.py:215
  144.6 4.1 add_convert_fusion.10
  148.7 2.9 multiply_convert_fusion.4
  151.6 4.3 multiply_convert_fusion.3
  157.1 9.6 %collective-permute-done.3 = bf16[768,768]{1,0:T(8,128)(2,1)S(1)} collective-permute-done((bf16[768,768]{1,0:T(8,128)(2,1)}, bf16[768,768]{1,0:T(8,128)(2,1)S(1)}, u32[]{:S(2)}, u32[]{:S(2)}) %collective-permute-start.3) | collective-permute-done | bytes 1179680 | tf_op jit(solution)/shard_map/ppermute | solution.py:189
  168.1 14.5 %all-gather.14.cloned.1.call-done = bf16[768,768]{1,0:T(8,128)(2,1)} async-done(((bf16[96,768]{1,0:T(8,128)(2,1)}), bf16[768,768]{1,0:T(8,128)(2,1)}) %all-gather.14.cloned.1.call-update) | async-done | bytes 1179664 | tf_op jit(solution)/shard_map/all_gather | solution.py:215
  185.2 4.1 add_add_fusion.1
  193.4 16.0 %collective-permute-done.5 = bf16[768,768]{1,0:T(8,128)(2,1)} collective-permute-done((bf16[768,768]{1,0:T(8,128)(2,1)}, bf16[768,768]{1,0:T(8,128)(2,1)}, u32[]{:S(2)}, u32[]{:S(2)}) %collective-permute-start.5) | collective-permute-done | bytes 1179680 | tf_op jit(solution)/shard_map/ppermute | solution.py:189
  209.4 3.4 add_convert_fusion.17.qkv_ref
  212.8 6.0 shard_map.307
  218.8 5.9 shard_map.308
  226.5 2.8 add_convert_fusion.7
  235.6 32.1 %all-gather.16.cloned.1.call-done = bf16[768,768]{1,0:T(8,128)(2,1)} async-done(((bf16[96,768]{1,0:T(8,128)(2,1)}), bf16[768,768]{1,0:T(8,128)(2,1)}) %all-gather.16.cloned.1.call-update) | async-done | bytes 1179664 | tf_op jit(solution)/shard_map/all_gather | solution.py:215
  278.9 2.9 multiply_convert_fusion.1
  281.8 12.8 %collective-permute-done.8 = bf16[768,768]{1,0:T(8,128)(2,1)S(1)} collective-permute-done((bf16[768,768]{1,0:T(8,128)(2,1)}, bf16[768,768]{1,0:T(8,128)(2,1)S(1)}, u32[]{:S(2)}, u32[]{:S(2)}) %collective-permute-start.8) | collective-permute-done | bytes 1179680 | tf_op jit(solution)/shard_map/ppermute | solution.py:189
  297.1 4.0 add_convert_fusion.4
  305.3 3.9 multiply_reduce_fusion
  309.3 4.2 fusion.87
  318.9 10.3 %shard_map.309 = bf16[832,576]{1,0:T(8,128)(2,1)} custom-call(bf16[832,576]{1,0:T(8,128)(2,1)} %add_convert_fusion.18.qkv_ref, bf16[832,192]{1,0:T(8,128)(2,1)} %copy.130.grad_ref), custom_call_target="tpu_custom_call" | custom-call | flops 332267520 | bytes 2396160 | tf_op jit(solution)/shard_map/pallas_call | solution.py:133
  332.3 10.6 %shard_map.310 = bf16[832,576]{1,0:T(8,128)(2,1)} custom-call(bf16[832,576]{1,0:T(8,128)(2,1)} %add_convert_fusion.17.qkv_ref, bf16[832,192]{1,0:T(8,128)(2,1)} %copy.131.grad_ref), custom_call_target="tpu_custom_call" | custom-call | flops 332267520 | bytes 2396160 | tf_op jit(solution)/shard_map/pallas_call | solution.py:133
  342.9 2.8 fusion.46
  345.8 3.5 add_convert_fusion.3
  349.3 4.4 convolution_convert_fusion.2
  357.8 3.1 multiply_reduce_fusion.1
  374.2 4.0 add_convert_fusion.2
  380.2 27.4 %collective-permute-done.17 = bf16[768,768]{0,1:T(8,128)(2,1)S(1)} collective-permute-done((bf16[768,768]{0,1:T(8,128)(2,1)S(1)}, bf16[768,768]{0,1:T(8,128)(2,1)S(1)}, u32[]{:S(2)}, u32[]{:S(2)}) %collective-permute-start.17) | collective-permute-done | bytes 1179680 | tf_op jit(solution)/shard_map/ppermute | solution.py:189
  411.5 2.8 multiply_reduce_fusion.2
  414.4 2.5 fusion.86
  421.6 10.3 %shard_map.311 = bf16[832,576]{1,0:T(8,128)(2,1)} custom-call(bf16[832,576]{1,0:T(8,128)(2,1)} %add_convert_fusion.20.qkv_ref, bf16[832,192]{1,0:T(8,128)(2,1)} %copy.132.grad_ref), custom_call_target="tpu_custom_call" | custom-call | flops 332267520 | bytes 2396160 | tf_op jit(solution)/shard_map/pallas_call | solution.py:133
  434.6 10.2 %shard_map.312 = bf16[832,576]{1,0:T(8,128)(2,1)} custom-call(bf16[832,576]{1,0:T(8,128)(2,1)} %add_convert_fusion.19.qkv_ref, bf16[832,192]{1,0:T(8,128)(2,1)} %copy.133.grad_ref), custom_call_target="tpu_custom_call" | custom-call | flops 332267520 | bytes 2396160 | tf_op jit(solution)/shard_map/pallas_call | solution.py:133
  446.1 3.5 add_convert_fusion.1
  453.8 2.7 multiply_reduce_fusion.3
  457.7 4.5 add_convert_fusion.15
  462.5 3.3 convolution_convert_fusion.3
  467.3 26.8 %collective-permute-done.18 = bf16[768,768]{1,0:T(8,128)(2,1)S(1)} collective-permute-done((bf16[768,768]{1,0:T(8,128)(2,1)S(1)}, bf16[768,768]{1,0:T(8,128)(2,1)S(1)}, u32[]{:S(2)}, u32[]{:S(2)}) %collective-permute-start.18) | collective-permute-done | bytes 1179680 | tf_op jit(solution)/shard_map/ppermute | solution.py:189
  496.8 3.3 convolution_convert_fusion
  501.6 26.0 %collective-permute-done.21 = bf16[768,768]{1,0:T(8,128)(2,1)S(1)} collective-permute-done((bf16[768,768]{1,0:T(8,128)(2,1)S(1)}, bf16[768,768]{1,0:T(8,128)(2,1)S(1)}, u32[]{:S(2)}, u32[]{:S(2)}) %collective-permute-start.21) | collective-permute-done | bytes 1179680 | tf_op jit(solution)/shard_map/ppermute | solution.py:189
  530.3 3.3 convolution_convert_fusion.1
  535.0 25.1 %collective-permute-done.20 = bf16[768,768]{1,0:T(8,128)(2,1)S(1)} collective-permute-done((bf16[768,768]{1,0:T(8,128)(2,1)S(1)}, bf16[768,768]{1,0:T(8,128)(2,1)S(1)}, u32[]{:S(2)}, u32[]{:S(2)}) %collective-permute-start.20) | collective-permute-done | bytes 1179680 | tf_op jit(solution)/shard_map/ppermute | solution.py:189
  560.1 2.6 add_convert_fusion.14
  564.9 2.7 convolution_convert_fusion.5
  570.3 2.5 slice.286
  575.1 23.1 %collective-permute-done.16 = bf16[768,768]{0,1:T(8,128)(2,1)} collective-permute-done((bf16[768,768]{0,1:T(8,128)(2,1)}, bf16[768,768]{0,1:T(8,128)(2,1)}, u32[]{:S(2)}, u32[]{:S(2)}) %collective-permute-start.16) | collective-permute-done | bytes 1179680 | tf_op jit(solution)/shard_map/ppermute | solution.py:189
  598.2 2.6 fusion.30
  603.3 3.3 add_convert_fusion
  608.2 16.4 %collective-permute-done.10 = bf16[4,197,768]{2,1,0:T(8,128)(2,1)} collective-permute-done((bf16[4,197,768]{2,1,0:T(8,128)(2,1)}, bf16[4,197,768]{2,1,0:T(8,128)(2,1)}, u32[]{:S(2)}, u32[]{:S(2)}) %collective-permute-start.10) | collective-permute-done | bytes 1210400 | tf_op jit(solution)/shard_map/ppermute | solution.py:189
  624.6 2.9 fusion.29
  634.6 34.1 %reduce-scatter.13.cloned.1.call-done = bf16[96,768]{1,0:T(8,128)(2,1)} async-done(((bf16[768,768]{1,0:T(8,128)(2,1)}), bf16[96,768]{1,0:T(8,128)(2,1)}) %reduce-scatter.13.cloned.1.call-update) | async-done | bytes 147472 | tf_op jit(solution)/shard_map/reduce_scatter | solution.py:280
  668.6 66.3 %reduce-scatter.11.cloned.1.call-done = bf16[96,768]{1,0:T(8,128)(2,1)} async-done(((bf16[768,768]{1,0:T(8,128)(2,1)}), bf16[96,768]{1,0:T(8,128)(2,1)}) %reduce-scatter.11.cloned.1.call-update) | async-done | bytes 147472 | tf_op jit(solution)/shard_map/reduce_scatter | solution.py:280
  734.9 2.9 multiply_subtract_fusion.1
  737.8 63.6 %reduce-scatter.17.cloned.1.call-done = bf16[96,768]{1,0:T(8,128)(2,1)} async-done(((bf16[768,768]{1,0:T(8,128)(2,1)}), bf16[96,768]{1,0:T(8,128)(2,1)}) %reduce-scatter.17.cloned.1.call-update) | async-done | bytes 147472 | tf_op jit(solution)/shard_map/reduce_scatter | solution.py:280
  801.4 66.3 %reduce-scatter.15.cloned.1.call-done = bf16[96,768]{1,0:T(8,128)(2,1)} async-done(((bf16[768,768]{1,0:T(8,128)(2,1)}), bf16[96,768]{1,0:T(8,128)(2,1)}) %reduce-scatter.15.cloned.1.call-update) | async-done | bytes 147472 | tf_op jit(solution)/shard_map/reduce_scatter | solution.py:280
  867.7 2.7 multiply_subtract_fusion
  870.4 2.6 fusion.27
  873.0 3.7 copy.141
  876.7 57.6 %reduce-scatter.19.cloned.1.call-done = bf16[96,768]{1,0:T(8,128)(2,1)} async-done(((bf16[768,768]{1,0:T(8,128)(2,1)}), bf16[96,768]{1,0:T(8,128)(2,1)}) %reduce-scatter.19.cloned.1.call-update) | async-done | bytes 147472
  (400 shorter events, 135.4 us)
Async XLA Ops:
  7.2 59.2 %all-gather.10.cloned.1.call-start = ((), (), s32[]{:S(2)}) async-start(), calls=%async_computation.6 | async-start | bytes 1327104 | tf_op jit(solution)/shard_map/all_gather | solution.py:215
  10.5 98.1 %all-gather.18.cloned.1.call-start = ((), (), s32[]{:S(2)}) async-start(), calls=%async_computation.14 | async-start | bytes 1327104 | tf_op jit(solution)/shard_map/all_gather | solution.py:215
  11.3 128.7 %all-gather.12.cloned.1.call-start = ((), (), s32[]{:S(2)}) async-start(), calls=%async_computation.7 | async-start | bytes 1327104 | tf_op jit(solution)/shard_map/all_gather | solution.py:215
  12.2 170.4 %all-gather.14.cloned.1.call-start = ((), (), s32[]{:S(2)}) async-start(), calls=%async_computation.8 | async-start | bytes 1327104 | tf_op jit(solution)/shard_map/all_gather | solution.py:215
  13.3 220.9 %all-gather.20.cloned.1.call-start = ((), (), s32[]{:S(2)}) async-start(), calls=%async_computation.15 | async-start | bytes 1327104 | tf_op jit(solution)/shard_map/all_gather | solution.py:215
  66.4 28.6 %collective-permute-start = (bf16[768,768]{1,0:T(8,128)(2,1)}, bf16[768,768]{1,0:T(8,128)(2,1)}, u32[]{:S(2)}, u32[]{:S(2)}) collective-permute-start(bf16[768,768]{1,0:T(8,128)(2,1)} %all-gather.10.cloned.1.call-done), channel_id=1, source_target_pairs={{0,2},{1,3},{2,0},{3,1},{4,6},{5,7},{6,4},{7,5},{8,10},{9,11},{10,... | collective-permute-start | bytes 3538952 | tf_op jit(solution)/shard_map/ppermute | solution.py:189
  68.8 75.7 %copy-start.2 = (f32[4,208,768]{2,1,0:T(8,128)}, f32[4,208,768]{2,1,0:T(8,128)S(1)}, u32[]{:S(2)}) copy-start(f32[4,208,768]{2,1,0:T(8,128)S(1)} %copy.116) | copy-start | bytes 7667716
  80.3 14.7 %copy-start.33 = (bf16[832,768]{1,0:T(8,128)(2,1)S(1)}, bf16[832,768]{1,0:T(8,128)(2,1)}, u32[]{:S(2)}) copy-start(bf16[832,768]{1,0:T(8,128)(2,1)} %copy-done.32) | copy-start | bytes 3833860
  107.9 33.6 %collective-permute-start.1 = (bf16[832,768]{1,0:T(8,128)(2,1)}, bf16[832,768]{1,0:T(8,128)(2,1)}, u32[]{:S(2)}, u32[]{:S(2)}) collective-permute-start(bf16[832,768]{1,0:T(8,128)(2,1)} %add_convert_fusion.11), channel_id=1, source_target_pairs={{0,1},{1,0},{2,3},{3,2},{4,5},{5,4},{6,7},{7,6},{8,9},{9,8},{10,11... | collective-permute-start | bytes 3833864 | tf_op jit(solution)/shard_map/ppermute | solution.py:186
  107.9 159.8 %all-gather.16.cloned.1.call-start = ((), (), s32[]{:S(2)}) async-start(), calls=%async_computation.9 | async-start | bytes 1327104 | tf_op jit(solution)/shard_map/all_gather | solution.py:215
  108.5 43.0 %collective-permute-start.2 = (bf16[768,768]{1,0:T(8,128)(2,1)}, bf16[768,768]{1,0:T(8,128)(2,1)}, u32[]{:S(2)}, u32[]{:S(2)}) collective-permute-start(bf16[768,768]{1,0:T(8,128)(2,1)} %bitcast.183), channel_id=1, source_target_pairs={{0,2},{1,3},{2,0},{3,1},{4,6},{5,7},{6,4},{7,5},{8,10},{9,11},{10,... | collective-permute-start | bytes 3538952 | tf_op jit(solution)/shard_map/ppermute | solution.py:189
  140.0 26.7 %collective-permute-start.3 = (bf16[768,768]{1,0:T(8,128)(2,1)}, bf16[768,768]{1,0:T(8,128)(2,1)S(1)}, u32[]{:S(2)}, u32[]{:S(2)}) collective-permute-start(bf16[768,768]{1,0:T(8,128)(2,1)} %all-gather.12.cloned.1.call-done), channel_id=1, source_target_pairs={{0,2},{1,3},{2,0},{3,1},{4,6},{5,7},{6,4},{7,5},{8,10},{9,11},{10,... | collective-permute-start | bytes 3538952 | tf_op jit(solution)/shard_map/ppermute | solution.py:189
  155.8 10.9 %copy-start.70 = (bf16[832,768]{1,0:T(8,128)(2,1)}, bf16[832,768]{1,0:T(8,128)(2,1)S(1)}, u32[]{:S(2)}) copy-start(bf16[832,768]{1,0:T(8,128)(2,1)S(1)} %get-tuple-element.147) | copy-start | bytes 3833860
  167.9 16.1 %copy-start.44 = (bf16[832,768]{1,0:T(8,128)(2,1)}, bf16[832,768]{1,0:T(8,128)(2,1)S(1)}, u32[]{:S(2)}) copy-start(bf16[832,768]{1,0:T(8,128)(2,1)S(1)} %add_convert_fusion.9) | copy-start | bytes 3833860
  167.9 16.1 %collective-permute-start.4 = (bf16[832,768]{1,0:T(8,128)(2,1)S(1)}, bf16[832,768]{1,0:T(8,128)(2,1)S(1)}, u32[]{:S(2)}, u32[]{:S(2)}) collective-permute-start(bf16[832,768]{1,0:T(8,128)(2,1)S(1)} %add_convert_fusion.9), channel_id=1, source_target_pairs={{0,1},{1,0},{2,3},{3,2},{4,5},{5,4},{6,7},{7,6},{8,9},{9,8},{10,11... | collective-permute-start | bytes 3833864 | tf_op jit(solution)/shard_map/ppermute | solution.py:186
  168.0 461.3 %reduce-scatter.21.cloned.1.call-start = ((), (), s32[]{:S(2)}) async-start(), calls=%async_computation.17 | async-start | bytes 1327104
  182.6 26.8 %collective-permute-start.5 = (bf16[768,768]{1,0:T(8,128)(2,1)}, bf16[768,768]{1,0:T(8,128)(2,1)}, u32[]{:S(2)}, u32[]{:S(2)}) collective-permute-start(bf16[768,768]{1,0:T(8,128)(2,1)} %all-gather.14.cloned.1.call-done), channel_id=1, source_target_pairs={{0,2},{1,3},{2,0},{3,1},{4,6},{5,7},{6,4},{7,5},{8,10},{9,11},{10,... | collective-permute-start | bytes 3538952 | tf_op jit(solution)/shard_map/ppermute | solution.py:189
  190.4 19.0 %copy-start.40 = (bf16[832,768]{1,0:T(8,128)(2,1)}, bf16[832,768]{1,0:T(8,128)(2,1)S(1)}, u32[]{:S(2)}) copy-start(bf16[832,768]{1,0:T(8,128)(2,1)S(1)} %add_convert_fusion.8) | copy-start | bytes 3833860
  229.3 39.9 %collective-permute-start.6 = (bf16[832,768]{1,0:T(8,128)(2,1)}, bf16[832,768]{1,0:T(8,128)(2,1)}, u32[]{:S(2)}, u32[]{:S(2)}) collective-permute-start(bf16[832,768]{1,0:T(8,128)(2,1)} %add_convert_fusion.7), channel_id=1, source_target_pairs={{0,1},{1,0},{2,3},{3,2},{4,5},{5,4},{6,7},{7,6},{8,9},{9,8},{10,11... | collective-permute-start | bytes 3833864 | tf_op jit(solution)/shard_map/ppermute | solution.py:186
  234.1 44.7 %collective-permute-start.7 = (bf16[768,768]{1,0:T(8,128)(2,1)}, bf16[768,768]{1,0:T(8,128)(2,1)}, u32[]{:S(2)}, u32[]{:S(2)}) collective-permute-start(bf16[768,768]{1,0:T(8,128)(2,1)} %bitcast.184), channel_id=1, source_target_pairs={{0,2},{1,3},{2,0},{3,1},{4,6},{5,7},{6,4},{7,5},{8,10},{9,11},{10,... | collective-permute-start | bytes 3538952 | tf_op jit(solution)/shard_map/ppermute | solution.py:189
  267.7 26.9 %collective-permute-start.8 = (bf16[768,768]{1,0:T(8,128)(2,1)}, bf16[768,768]{1,0:T(8,128)(2,1)S(1)}, u32[]{:S(2)}, u32[]{:S(2)}) collective-permute-start(bf16[768,768]{1,0:T(8,128)(2,1)} %all-gather.16.cloned.1.call-done), channel_id=1, source_target_pairs={{0,2},{1,3},{2,0},{3,1},{4,6},{5,7},{6,4},{7,5},{8,10},{9,11},{10,... | collective-permute-start | bytes 3538952 | tf_op jit(solution)/shard_map/ppermute | solution.py:189
  274.9 26.2 %copy-start.76 = (bf16[832,768]{1,0:T(8,128)(2,1)}, bf16[832,768]{1,0:T(8,128)(2,1)S(1)}, u32[]{:S(2)}) copy-start(bf16[832,768]{1,0:T(8,128)(2,1)S(1)} %get-tuple-element.149) | copy-start | bytes 3833860
  281.8 20.6 %copy-start.71 = (bf16[832,768]{1,0:T(8,128)(2,1)}, bf16[832,768]{1,0:T(8,128)(2,1)S(1)}, u32[]{:S(2)}) copy-start(bf16[832,768]{1,0:T(8,128)(2,1)S(1)} %get-tuple-element.151) | copy-start | bytes 3833860
  301.1 4.2 collective-permute-start.11
  304.6 4.7 collective-permute-start.9
  349.3 8.5 collective-permute-start.12
  349.3 6.4 copy-start.22
  349.3 6.4 copy-start.41
  353.7 104.0 %collective-permute-start.19 = (bf16[768,768]{1,0:T(8,128)(2,1)}, bf16[768,768]{1,0:T(8,128)(2,1)}, u32[]{:S(2)}, u32[]{:S(2)}) collective-permute-start(bf16[768,768]{1,0:T(8,128)(2,1)} %convolution_convert_fusion.2), channel_id=1, source_target_pairs={{0,2},{1,3},{2,0},{3,1},{4,6},{5,7},{6,4},{7,5},{8,10},{9,11},{10,... | collective-permute-start | bytes 3538952 | tf_op jit(solution)/shard_map/ppermute | solution.py:189
  357.0 50.6 %collective-permute-start.17 = (bf16[768,768]{0,1:T(8,128)(2,1)S(1)}, bf16[768,768]{0,1:T(8,128)(2,1)S(1)}, u32[]{:S(2)}, u32[]{:S(2)}) collective-permute-start(bf16[768,768]{0,1:T(8,128)(2,1)S(1)} %pad_maximum_fusion.1), channel_id=1, source_target_pairs={{0,2},{1,3},{2,0},{3,1},{4,6},{5,7},{6,4},{7,5},{8,10},{9,11},{10,... | collective-permute-start | bytes 3538952 | tf_op jit(solution)/shard_map/ppermute | solution.py:189
  363.6 6.9 copy-start.38
  378.3 33.2 %collective-permute-start.13 = (bf16[832,768]{1,0:T(8,128)(2,1)}, bf16[832,768]{1,0:T(8,128)(2,1)}, u32[]{:S(2)}, u32[]{:S(2)}) collective-permute-start(bf16[832,768]{1,0:T(8,128)(2,1)} %add_convert_fusion.2), channel_id=1, source_target_pairs={{0,1},{1,0},{2,3},{3,2},{4,5},{5,4},{6,7},{7,6},{8,9},{9,8},{10,11... | collective-permute-start | bytes 3833864 | tf_op jit(solution)/shard_map/ppermute | solution.py:186
  411.4 221.7 %all-reduce.5.cloned.1.call-start = ((), (), s32[]{:S(2)}) async-start(), calls=%async_computation.18 | async-start | bytes 163840
  418.5 13.3 %copy-start.12 = (bf16[832,768]{1,0:T(8,128)(2,1)}, bf16[832,768]{1,0:T(8,128)(2,1)S(1)}, u32[]{:S(2)}) copy-start(bf16[832,768]{1,0:T(8,128)(2,1)S(1)} %convert_element_type.356) | copy-start | bytes 3833860
  431.8 13.0 %copy-start.17 = (bf16[832,576]{1,0:T(8,128)(2,1)S(1)}, bf16[832,576]{1,0:T(8,128)(2,1)}, u32[]{:S(2)}) copy-start(bf16[832,576]{1,0:T(8,128)(2,1)} %shard_map.311) | copy-start | bytes 2875396
  433.7 11.2 %copy-start.51 = (bf16[768,768]{1,0:T(8,128)(2,1)S(1)}, bf16[768,768]{1,0:T(8,128)(2,1)}, u32[]{:S(2)}) copy-start(bf16[768,768]{1,0:T(8,128)(2,1)} %all-gather.10.cloned.1.call-done) | copy-start | bytes 3538948
  449.7 4.1 collective-permute-start.14
  457.6 211.0 %reduce-scatter.13.cloned.1.call-start = ((), (), s32[]{:S(2)}) async-start(), calls=%async_computation.11 | async-start | bytes 1327104 | tf_op jit(solution)/shard_map/reduce_scatter | solution.py:280
  462.2 272.7 %reduce-scatter.11.cloned.1.call-start = ((), (), s32[]{:S(2)}) async-start(), calls=%async_computation.10 | async-start | bytes 1327104 | tf_op jit(solution)/shard_map/reduce_scatter | solution.py:280
  462.5 31.7 %copy-start.43 = (bf16[832,768]{1,0:T(8,128)(2,1)S(1)}, bf16[832,768]{1,0:T(8,128)(2,1)}, u32[]{:S(2)}) copy-start(bf16[832,768]{1,0:T(8,128)(2,1)} %copy-done.42) | copy-start | bytes 3833860
  462.5 31.7 %copy-start.80 = (bf16[832,768]{1,0:T(8,128)(2,1)S(1)}, bf16[832,768]{1,0:T(8,128)(2,1)}, u32[]{:S(2)}) copy-start(bf16[832,768]{1,0:T(8,128)(2,1)} %copy-done.79) | copy-start | bytes 3833860
  465.8 28.4 %collective-permute-start.18 = (bf16[768,768]{1,0:T(8,128)(2,1)S(1)}, bf16[768,768]{1,0:T(8,128)(2,1)S(1)}, u32[]{:S(2)}, u32[]{:S(2)}) collective-permute-start(bf16[768,768]{1,0:T(8,128)(2,1)S(1)} %convolution_convert_fusion.3), channel_id=1, source_target_pairs={{0,2},{1,3},{2,0},{3,1},{4,6},{5,7},{6,4},{7,5},{8,10},{9,11},{10,... | collective-permute-start | bytes 3538952 | tf_op jit(solution)/shard_map/ppermute | solution.py:189
  496.7 304.6 %reduce-scatter.17.cloned.1.call-start = ((), (), s32[]{:S(2)}) async-start(), calls=%async_computation.13 | async-start | bytes 1327104 | tf_op jit(solution)/shard_map/reduce_scatter | solution.py:280
  496.8 30.9 %copy-start.36 = (bf16[832,768]{1,0:T(8,128)(2,1)S(1)}, bf16[832,768]{1,0:T(8,128)(2,1)}, u32[]{:S(2)}) copy-start(bf16[832,768]{1,0:T(8,128)(2,1)} %bitcast_convert_fusion) | copy-start | bytes 3833860
  496.8 30.9 %copy-start.77 = (bf16[832,768]{1,0:T(8,128)(2,1)S(1)}, bf16[832,768]{1,0:T(8,128)(2,1)}, u32[]{:S(2)}) copy-start(bf16[832,768]{1,0:T(8,128)(2,1)} %copy-done.76) | copy-start | bytes 3833860
  500.1 27.6 %collective-permute-start.21 = (bf16[768,768]{1,0:T(8,128)(2,1)S(1)}, bf16[768,768]{1,0:T(8,128)(2,1)S(1)}, u32[]{:S(2)}, u32[]{:S(2)}) collective-permute-start(bf16[768,768]{1,0:T(8,128)(2,1)S(1)} %convolution_convert_fusion), channel_id=1, source_target_pairs={{0,2},{1,3},{2,0},{3,1},{4,6},{5,7},{6,4},{7,5},{8,10},{9,11},{10,... | collective-permute-start | bytes 3538952 | tf_op jit(solution)/shard_map/ppermute | solution.py:189
  530.2 337.5 %reduce-scatter.15.cloned.1.call-start = ((), (), s32[]{:S(2)}) async-start(), calls=%async_computation.12 | async-start | bytes 1327104 | tf_op jit(solution)/shard_map/reduce_scatter | solution.py:280
  530.2 29.9 %copy-start.39 = (bf16[832,768]{1,0:T(8,128)(2,1)S(1)}, bf16[832,768]{1,0:T(8,128)(2,1)}, u32[]{:S(2)}) copy-start(bf16[832,768]{1,0:T(8,128)(2,1)} %copy-done.38) | copy-start | bytes 3833860
  530.3 29.9 %copy-start.75 = (bf16[832,768]{1,0:T(8,128)(2,1)S(1)}, bf16[832,768]{1,0:T(8,128)(2,1)}, u32[]{:S(2)}) copy-start(bf16[832,768]{1,0:T(8,128)(2,1)} %copy-done.74) | copy-start | bytes 3833860
  533.6 29.5 %copy-start.30 = (bf16[832,192]{1,0:T(8,128)(2,1)S(1)}, bf16[832,192]{1,0:T(8,128)(2,1)}, u32[]{:S(2)}) copy-start(bf16[832,192]{1,0:T(8,128)(2,1)} %shard_map.306) | copy-start | bytes 958468
  533.6 26.6 %collective-permute-start.20 = (bf16[768,768]{1,0:T(8,128)(2,1)S(1)}, bf16[768,768]{1,0:T(8,128)(2,1)S(1)}, u32[]{:S(2)}, u32[]{:S(2)}) collective-permute-start(bf16[768,768]{1,0:T(8,128)(2,1)S(1)} %convolution_convert_fusion.1), channel_id=1, source_target_pairs={{0,2},{1,3},{2,0},{3,1},{4,6},{5,7},{6,4},{7,5},{8,10},{9,11},{10,... | collective-permute-start | bytes 3538952 | tf_op jit(solution)/shard_map/ppermute | solution.py:189
  562.7 371.5 %reduce-scatter.19.cloned.1.call-start = ((), (), s32[]{:S(2)}) async-start(), calls=%async_computation.16 | async-start | bytes 1327104
  568.8 29.4 %collective-permute-start.16 = (bf16[768,768]{0,1:T(8,128)(2,1)}, bf16[768,768]{0,1:T(8,128)(2,1)}, u32[]{:S(2)}, u32[]{:S(2)}) collective-permute-start(bf16[768,768]{0,1:T(8,128)(2,1)} %pad_maximum_fusion), channel_id=1, source_target_pairs={{0,2},{1,3},{2,0},{3,1},{4,6},{5,7},{6,4},{7,5},{8,10},{9,11},{10,... | collective-permute-start | bytes 3538952 | tf_op jit(solution)/shard_map/ppermute | solution.py:189
  572.8 51.8 %collective-permute-start.10 = (bf16[4,197,768]{2,1,0:T(8,128)(2,1)}, bf16[4,197,768]{2,1,0:T(8,128)(2,1)}, u32[]{:S(2)}, u32[]{:S(2)}) collective-permute-start(bf16[4,197,768]{2,1,0:T(8,128)(2,1)} %slice.286), channel_id=1, source_target_pairs={{0,2},{1,3},{2,0},{3,1},{4,6},{5,7},{6,4},{7,5},{8,10},{9,11},{10,... | collective-permute-start | bytes 3631112 | tf_op jit(solution)/shard_map/ppermute | solution.py:189
  606.7 263.7 %collective-permute-start.15 = (bf16[4,197,768]{2,1,0:T(8,128)(2,1)S(1)}, bf16[4,197,768]{2,1,0:T(8,128)(2,1)}, u32[]{:S(2)}, u32[]{:S(2)}) collective-permute-start(bf16[4,197,768]{2,1,0:T(8,128)(2,1)S(1)} %slice.287), channel_id=1, source_target_pairs={{0,2},{1,3},{2,0},{3,1},{4,6},{5,7},{6,4},{7,5},{8,10},{9,11},{10,... | collective-permute-start | bytes 3631112 | tf_op jit(solution)/shard_map/ppermute | solution.py:189
  627.4 6.5 copy-start.59
  627.5 6.5 copy-start.60
  627.5 6.5 copy-start.61
  629.4 105.5 %copy-start.27 = (f32[2,96,768]{2,1,0:T(8,128)S(1)}, f32[2,96,768]{2,1,0:T(8,128)}, u32[]{:S(2)}) copy-start(f32[2,96,768]{2,1,0:T(8,128)} %param.23) | copy-start | bytes 1769476
  631.3 236.4 %copy-start.29 = (f32[2,768,96]{1,2,0:T(8,128)S(1)}, f32[2,768,96]{1,2,0:T(8,128)}, u32[]{:S(2)}) copy-start(f32[2,768,96]{1,2,0:T(8,128)} %param.24) | copy-start | bytes 1769476
  631.5 236.2 %copy-start.49 = (f32[2,768,96]{1,2,0:T(8,128)S(1)}, f32[2,768,96]{1,2,0:T(8,128)}, u32[]{:S(2)}) copy-start(f32[2,768,96]{1,2,0:T(8,128)} %param.33) | copy-start | bytes 1769476
  876.7 59.0 %copy-start.25 = (f32[2,96,3,192]{3,1,2,0:T(8,128)S(1)}, f32[2,96,3,192]{3,1,2,0:T(8,128)}, u32[]{:S(2)}) copy-start(f32[2,96,3,192]{3,1,2,0:T(8,128)} %param.21) | copy-start | bytes 1327108
  876.7 59.0 %copy-start.47 = (f32[2,96,3,192]{3,1,2,0:T(8,128)S(1)}, f32[2,96,3,192]{3,1,2,0:T(8,128)}, u32[]{:S(2)}) copy-start(f32[2,96,3,192]{3,1,2,0:T(8,128)} %param.27) | copy-start | bytes 1327108
  876.7 59.0 %copy-start.48 = (f32[2,96,3,192]{3,1,2,0:T(8,128)S(1)}, f32[2,96,3,192]{3,1,2,0:T(8,128)}, u32[]{:S(2)}) copy-start(f32[2,96,3,192]{3,1,2,0:T(8,128)} %param.26) | copy-start | bytes 1327108
  (54 other events, 145.1 us)
Sparse Core Ops, SparseCore 0:
  10.8 43.7 all-gather.9
  57.4 39.9 all-gather.17
  100.1 39.8 all-gather.11
  142.6 39.9 all-gather.13
  185.2 39.9 all-gather.19
  227.8 39.8 all-gather.15
  411.5 62.6 reduce-scatter.20
  480.4 118.7 all-reduce.4
  602.6 65.9 reduce-scatter.12
  671.8 62.9 reduce-scatter.10
  738.3 63.0 reduce-scatter.16
  804.6 63.0 reduce-scatter.14
  871.1 63.1 reduce-scatter.18

commit v2 on v1

--- a/solution.py
+++ b/solution.py
@@ -142,6 +142,35 @@
             transcendentals=rows * pad_len * (width // 3 // HEAD_DIM),
         ),
     )(qkv_rows, grad_rows)
+
+
+def bit_swap(axis, bit, size):
+    return [(i, i ^ (1 << bit)) for i in range(size)]
+
+
+def swap_bit(values, axis, bit):
+    return lax.ppermute(values, axis, bit_swap(axis, bit, lax.axis_size(axis)))
+
+
+def own_bit(axis, bit):
+    return lax.rem(lax.axis_index(axis) // (1 << bit), 2)
+
+
+def double_bit(values, dim, axis, bit):
+    other = swap_bit(values, axis, bit)
+    return jnp.where(
+        own_bit(axis, bit) == 0,
+        jnp.concatenate([values, other], dim),
+        jnp.concatenate([other, values], dim),
+    )
+
+
+def halve_bit(values, dim, axis, bit):
+    mine = own_bit(axis, bit)
+    theirs = lax.dynamic_index_in_dim(values, 1 - mine, dim, keepdims=True)
+    kept = lax.dynamic_index_in_dim(values, mine, dim, keepdims=True)
+    arrived = swap_bit(theirs, axis, bit)
+    return (kept.astype(f32) + arrived.astype(f32)).astype(values.dtype)
 
 
 def on_device(
@@ -192,9 +221,18 @@
         low = partial_rows.astype(bf16)
         return low.astype(f32) + to_pair(low).astype(f32)
 
-    vector_rows = lax.all_gather(vectors.reshape(1, -1), ("dp", "mp"), axis=0, tiled=True)
+    dp_bits = dp_count.bit_length() - 1
+    mp_bits = mp_count.bit_length() - 1
+    dp_dims = {bit: dp_bits - 1 - bit for bit in range(dp_bits)}
+    high_bits = [bit for bit in range(1, dp_bits)]
+
+    spread = vectors.reshape((1,) * (dp_bits + mp_bits) + (layers, -1))
+    for bit in range(mp_bits):
+        spread = double_bit(spread, dp_bits + mp_bits - 1 - bit, "mp", bit)
+    for bit in range(dp_bits):
+        spread = double_bit(spread, dp_dims[bit], "dp", bit)
     vector_blocks = (
-        vector_rows.reshape(dp_count, mp_count, layers, -1)
+        spread.reshape(dp_count, mp_count, layers, -1)
         .transpose(2, 1, 0, 3)
         .reshape(layers, mp_count, -1)
     )
@@ -202,19 +240,36 @@
     tails = vector_blocks[:, :, row_width:]
     tail_pair = [lax.dynamic_index_in_dim(tails, at, 1, keepdims=False) for at in (own_at, other_at)]
 
-    def shard_pieces(layer):
-        qkv_out = jnp.concatenate(
-            [qkv_weight[layer].reshape(shard_rows, qkv_cols), out_weight[layer].T], axis=1
-        )
-        return qkv_out, up_weight[layer], down_weight[layer].T
+    def gather_side_last(shard):
+        held = shard.reshape((1,) * dp_bits + shard.shape)
+        for bit in high_bits + [0]:
+            held = double_bit(held, dp_dims[bit], "dp", bit)
+        own = held.reshape(-1, shard.shape[1])
+        return own, to_side(own)
+
+    def gather_low_last(shard):
+        held = shard.reshape((1,) * dp_bits + shard.shape)
+        for bit in high_bits:
+            held = double_bit(held, dp_dims[bit], "dp", bit)
+        both = jnp.stack([held, to_side(held)])
+        both = double_bit(both, 1 + dp_dims[0], "dp", 0).reshape(2, -1, shard.shape[1])
+        return both[0], both[1]
 
     pieces = []
     for layer in range(layers):
-        layer_pieces = []
-        for piece in shard_pieces(layer):
-            own = lax.all_gather(piece.astype(bf16), "dp", axis=0, tiled=True)
-            layer_pieces.append((own, to_side(own)))
-        pieces.append(layer_pieces)
+        attn_shard = jnp.concatenate(
+            [qkv_weight[layer].reshape(shard_rows, qkv_cols), out_weight[layer].T], axis=1
+        ).astype(bf16)
+        mlp_shard = jnp.concatenate([up_weight[layer], down_weight[layer].T], axis=1).astype(bf16)
+        attn_pair = gather_side_last(attn_shard)
+        mlp_pair = gather_low_last(mlp_shard)
+        pieces.append(
+            (
+                attn_pair,
+                [both[:, :hidden_cols] for both in mlp_pair],
+                [both[:, hidden_cols:] for both in mlp_pair],
+            )
+        )
 
     def own_images(values):
         mine = lax.dynamic_slice_in_dim(values, side * images, images, 0)
@@ -274,10 +329,46 @@
         stream = following
     output_tokens = all_images(mask_live(stream).astype(bf16))
 
-    def owner_sum(own_grad, other_grad):
-        arrived = to_side(other_grad.astype(bf16))
-        total = (own_grad + arrived.astype(f32)).astype(bf16)
-        return lax.psum_scatter(total, "dp", scatter_dimension=0, tiled=True).astype(f32)
+    def block_dims(values):
+        return values.reshape((2,) * dp_bits + (shard_rows, values.shape[-1]))
+
+    flying = []
+
+    def halving(bits, skip):
+        return [
+            functools.partial(
+                lambda bit, values: halve_bit(values, skip + dp_dims[bit], "dp", bit), bit
+            )
+            for bit in bits
+        ]
+
+    def sum_side_first(own_grad, other_grad):
+        arrived = to_side(other_grad)
+        total = block_dims((own_grad.astype(f32) + arrived.astype(f32)).astype(bf16))
+        flying.append([total, halving([0] + high_bits[::-1], 0)])
+        return flying[-1]
+
+    def sum_low_first(own_grad, other_grad):
+        def side_step(both):
+            arrived = to_side(both[1])
+            return (both[0].astype(f32) + arrived.astype(f32)).astype(bf16)
+
+        both = jnp.stack([block_dims(own_grad), block_dims(other_grad)])
+        both = halve_bit(both, 1 + dp_dims[0], "dp", 0)
+        flying.append([both, [side_step] + halving(high_bits[::-1], 0)])
+        return flying[-1]
+
+    def tick(values):
+        active = [entry for entry in flying if entry[1]]
+        values, arrived = lax.optimization_barrier((values, [entry[0] for entry in active]))
+        for entry, value in zip(active, arrived):
+            entry[0] = entry[1].pop(0)(value)
+        return values
+
+    def settle(entry):
+        while entry[1]:
+            entry[0] = entry[1].pop(0)(entry[0])
+        return entry[0].reshape(shard_rows, -1).astype(f32)
 
     upstream = mask_live(own_images(cotangent))
     grads = [None] * layers
@@ -294,15 +385,19 @@
         down_pieces, up_pieces, hidden_sums, qkv_sums = [], [], [], []
         branch = None
         for up, down, hidden, active in zip(up_pair, down_pair, hidden_pair, active_pair):
-            down_pieces.append(dot_tn(upstream_low, active))
+            down_pieces.append(dot_tn(upstream_low, active).astype(bf16))
             hidden_low = (dot_nn(upstream_low, down) * gelu_slope(hidden)).astype(bf16)
-            up_pieces.append(dot_tn(mixed, hidden_low))
+            up_pieces.append(dot_tn(mixed, hidden_low).astype(bf16))
             hidden_sums.append(jnp.sum(hidden_low.astype(f32), axis=0))
             term = dot_nt(hidden_low, up)
             branch = term if branch is None else branch + term
-        mixed_grad = pair_sum(branch)
-        down_grad = owner_sum(*down_pieces)
-        up_grad = owner_sum(*up_pieces)
+        mixed_grad = pair_sum(tick(branch))
+        mixed_grad, down_pieces, up_pieces = lax.optimization_barrier(
+            (mixed_grad, down_pieces, up_pieces)
+        )
+        mixed_grad = tick(mixed_grad)
+        down_grad = sum_side_first(*down_pieces)
+        up_grad = sum_low_first(*up_pieces)
         middle_part, gain2_grad, shift2_grad = norm_back(middle, gain2, mixed_grad)
         middle_grad = upstream + middle_part
         middle_low = middle_grad.astype(bf16)
@@ -312,23 +407,30 @@
         for weight, qkv, attended in zip(attn_pair, qkv_pair, attended_pair):
             attended_grad = dot_nn(middle_low, weight[:, qkv_cols:]).astype(bf16)
             qkv_grad = attention_backward(qkv, attended_grad, images, seq_len)
+            qkv_grad, middle_low = tick((qkv_grad, middle_low))
             attn_pieces.append(
-                jnp.concatenate([dot_tn(normed, qkv_grad), dot_tn(middle_low, attended)], axis=1)
+                jnp.concatenate(
+                    [
+                        dot_tn(normed, qkv_grad).astype(bf16),
+                        dot_tn(middle_low, attended).astype(bf16),
+                    ],
+                    axis=1,
+                )
             )
             sums = jnp.sum(qkv_grad.astype(f32), axis=0)
             qkv_sums.append(jnp.concatenate([sums[:head_cols], sums[2 * head_cols :]]))
             term = dot_nt(qkv_grad, weight[:, :qkv_cols])
             branch = term if branch is None else branch + term
         normed_grad = pair_sum(branch)
-        attn_grad = owner_sum(*attn_pieces)
+        normed_grad, attn_pieces = tick((normed_grad, attn_pieces))
+        cut = attn_pieces[0].shape[1] // 2
+        attn_grad = [
+            sum_side_first(*[piece[:, :cut] for piece in attn_pieces]),
+            sum_low_first(*[piece[:, cut:] for piece in attn_pieces]),
+        ]
         stream_part, gain1_grad, shift1_grad = norm_back(stream_in, gain1, normed_grad)
         upstream = middle_grad + stream_part
-        grads[layer] = (
-            attn_grad[:, :qkv_cols].reshape(shard_rows, 3, head_cols),
-            attn_grad[:, qkv_cols:].T,
-            up_grad,
-            down_grad.T,
-        )
+        grads[layer] = (attn_grad, up_grad, down_grad)
         row_grads[layer] = jnp.stack(
             [gain1_grad, shift1_grad, gain2_grad, shift2_grad, out_bias_grad, down_bias_grad]
         )
@@ -349,16 +451,31 @@
         jnp.concatenate([row_blocks, placed], axis=2)
         .reshape(layers, mp_count, dp_count, -1)
         .transpose(2, 1, 0, 3)
-        .reshape(dp_count * mp_count, -1)
-    )
-    vector_grad = lax.psum_scatter(
-        vector_grad, ("dp", "mp"), scatter_dimension=0, tiled=True
-    ).reshape(vectors.shape)
+        .reshape((2,) * (dp_bits + mp_bits) + (layers, -1))
+    )
+    vector_grad = tick(vector_grad)
+    for bit in reversed(range(dp_bits)):
+        vector_grad = halve_bit(vector_grad, dp_dims[bit], "dp", bit)
+    for bit in reversed(range(mp_bits)):
+        vector_grad = halve_bit(vector_grad, dp_bits + mp_bits - 1 - bit, "mp", bit)
+    vector_grad = vector_grad.reshape(vectors.shape)
 
     matrix_rate = 3.0 / D**0.5
 
+    settled = []
+    for attn_grad, up_grad, down_grad in grads:
+        attn_grad = jnp.concatenate([settle(entry) for entry in attn_grad], axis=1)
+        settled.append(
+            (
+                attn_grad[:, :qkv_cols].reshape(shard_rows, 3, head_cols),
+                attn_grad[:, qkv_cols:].T,
+                settle(up_grad),
+                settle(down_grad).T,
+            )
+        )
+
     def update(which, weight, first, second):
-        gradient = jnp.stack([grads[layer][which] for layer in range(layers)])
+        gradient = jnp.stack([settled[layer][which] for layer in range(layers)])
         return adam_update(weight, first, second, gradient, matrix_rate, 0.1)
 
     qkv_new = update(0, qkv_weight, qkv_first, qkv_second)

time: 955 us -> 701 us (0.73)
  waiting for transfers between devices: 560 us -> 195 us
  local copies, waits for them, and re-layouts: 50.7 us -> 117 us
  other arithmetic: 75.5 us -> 134 us
  starting transfers between devices: 18.5 us -> 65.4 us
  blocking collectives: 43.6 us -> 0 us
  between operations: 16.7 us -> 4.05 us
    reduce_scatter x4 -> x0, waiting for transfers between devices: 230 us -> none  [owner_sum(): lax.psum_scatter(total, 'dp', scatter_dimension=0, tiled=True).astype(f32)]
    ppermute x0 -> x46, waiting for transfers between devices: none -> 151 us  [swap_bit(): return lax.ppermute(values, axis, bit_swap(axis, bit, lax.axis_size(axis)))]
    ppermute x14, waiting for transfers between devices: 195 us -> 43.3 us  [to_side(): return lax.ppermute(values, 'mp', side_swap)]
    all_gather x6 -> x0, waiting for transfers between devices: 77.8 us -> none  [on_device(): own = lax.all_gather(piece.astype(bf16), 'dp', axis=0, tiled=True)]
    unnamed x16 -> x0, waiting for transfers between devices: 57.8 us -> none
    ppermute x0 -> x46, starting transfers between devices: none -> 47.5 us  [swap_bit(): return lax.ppermute(values, axis, bit_swap(axis, bit, lax.axis_size(axis)))]
    all_gather x1 -> x0, blocking collectives: 43.6 us -> none  [on_device(): lax.all_gather(vectors.reshape(1, -1), ('dp', 'mp'), axis=0, tiled=True)]
    convert_element_type x4 -> x30, other arithmetic: 4.71 us -> 29.1 us  [the longest x16 16.5 us: halve_bit(): return (kept.astype(f32) + arrived.astype(f32)).astype(values.dtype)]
  transfers between devices with their start and end apart: 35 -> 68, of which waited for: 18 -> 32; matrix products, arithmetic and copies ran while one was open for 21% -> 41% of each run, Pallas kernels for 5% -> 9%
where the time goes in v2:
time: 701 us; the launch traced here: 690 us
  waiting for transfers between devices  195 us (28%)
  other arithmetic  134 us (19%)
  local copies, waits for them, and re-layouts  117 us (17%)
  matrix products  109 us (16%)
  starting transfers between devices  65.4 us (9%)
  Pallas kernels  64.9 us (9%)
    ppermute x46, waiting for transfers between devices, swap_bit(): return lax.ppermute(values, axis, bit_swap(axis, bit, lax.axis_size(axis)))  151 us
    ppermute x46, starting transfers between devices, swap_bit(): return lax.ppermute(values, axis, bit_swap(axis, bit, lax.axis_size(axis)))  47.5 us
    dot_general x16, matrix products, dot_nn(): lax.dot_general(left, right, (((1,), (0,)), ((), ())), preferred_element_...  45 us
    ppermute x14, waiting for transfers between devices, to_side(): return lax.ppermute(values, 'mp', side_swap)  43.3 us
    pallas_call x4, Pallas kernels, attention_backward(): pl.pallas_call(functools.partial(attention_backward_kernel, seq_len), gri...  41.4 us
    unnamed x340, local copies, waits for them, and re-layouts  40.4 us
    dot_general x16, matrix products, dot_nt(): lax.dot_general(left, right, (((1,), (1,)), ((), ())), preferred_element_...  35.2 us
    dot_general x16, matrix products, dot_tn(): lax.dot_general(left, right, (((0,), (0,)), ((), ())), preferred_element_...  28.9 us
  transfers between devices with their start and end apart: 68, of which 32 were waited for; matrix products, arithmetic and copies ran while one was open for 41% of the time, Pallas kernels for 9%

profile of v2, /device:TPU:0, one launch (start us, length us, event | category | flops | bytes accessed | tf_op | source)
XLA Modules:
  0.0 689.8 jit_solution(2578515731793706078)
XLA Ops:
  3.7 3.0 collective-permute-start.10
  11.3 3.7 constant_dynamic-slice_fusion.28
  20.7 2.9 fusion.157
  36.4 3.0 collective-permute-start.4
  53.0 3.1 add_convert_fusion.10
  58.7 14.9 %collective-permute-done.6 = bf16[1,2,1,96,768]{3,4,2,1,0:T(8,128)(2,1)S(1)} collective-permute-done((bf16[1,2,1,96,768]{3,4,2,1,0:T(8,128)(2,1)S(1)}, bf16[1,2,1,96,768]{3,4,2,1,0:T(8,128)(2,1)S(1)}, u32[]{:S(2)}, u32[]{:S(2)}) %collective-permute-start.6) | collective-permute-done | bytes 294944 | tf_op jit(solution)/shard_map/ppermute | solution.py:152
  79.9 9.5 %collective-permute-done.7 = bf16[2,2,1,96,768]{4,3,2,1,0:T(8,128)(2,1)} collective-permute-done((bf16[2,2,1,96,768]{4,3,2,1,0:T(8,128)(2,1)}, bf16[2,2,1,96,768]{4,3,2,1,0:T(8,128)(2,1)}, u32[]{:S(2)}, u32[]{:S(2)}) %collective-permute-start.7) | collective-permute-done | bytes 589856 | tf_op jit(solution)/shard_map/ppermute | solution.py:152
  91.7 3.3 maximum_select_fusion.2
  100.9 5.1 collective-permute-done.11
  112.3 5.9 shard_map.305
  118.2 3.4 fusion.108
  121.6 5.3 collective-permute-done.8
  126.8 3.4 add_convert_fusion.17.qkv_ref
  130.2 5.9 shard_map.306
  142.0 7.1 %collective-permute-done.12 = bf16[2,2,1,96,1536]{4,3,1,0,2:T(8,128)(2,1)} collective-permute-done((bf16[2,2,1,96,1536]{4,3,1,0,2:T(8,128)(2,1)}, bf16[2,2,1,96,1536]{4,3,1,0,2:T(8,128)(2,1)}, u32[]{:S(2)}, u32[]{:S(2)}) %collective-permute-start.12) | collective-permute-done | bytes 1179680 | tf_op jit(solution)/shard_map/ppermute | solution.py:218
  154.5 22.4 %collective-permute-done.21 = bf16[1,2,1,96,1536]{4,3,2,1,0:T(8,128)(2,1)S(1)} collective-permute-done((bf16[1,2,1,96,1536]{4,3,2,1,0:T(8,128)(2,1)S(1)}, bf16[1,2,1,96,1536]{4,3,2,1,0:T(8,128)(2,1)S(1)}, u32[]{:S(2)}, u32[]{:S(2)}) %collective-permute-start.21) | collective-permute-done | bytes 589856 | tf_op jit(solution)/shard_map/ppermute | solution.py:152
  183.2 17.8 %collective-permute-done.13 = bf16[2,2,2,1,96,1536]{5,4,3,2,1,0:T(8,128)(2,1)S(1)} collective-permute-done((bf16[2,2,2,1,96,1536]{5,4,3,2,1,0:T(8,128)(2,1)S(1)}, bf16[2,2,2,1,96,1536]{5,4,3,2,1,0:T(8,128)(2,1)S(1)}, u32[]{:S(2)}, u32[]{:S(2)}) %collective-permute-start.13) | collective-permute-done | bytes 2359328 | tf_op jit(solution)/shard_map/ppermute | solution.py:152
  201.0 2.7 maximum_select_fusion
  204.1 2.9 multiply_convert_fusion.3
  208.3 3.3 multiply_convert_fusion.4
  241.1 3.0 pad_maximum_fusion.1
  244.7 2.9 add_add_fusion.1
  248.8 19.2 %collective-permute-done.18 = bf16[768,768]{1,0:T(8,128)(2,1)} collective-permute-done((bf16[768,768]{1,0:T(8,128)(2,1)}, bf16[768,768]{1,0:T(8,128)(2,1)}, u32[]{:S(2)}, u32[]{:S(2)}) %collective-permute-start.18) | collective-permute-done | bytes 1179680 | tf_op jit(solution)/shard_map/ppermute | solution.py:218
  268.0 3.4 add_convert_fusion.15.qkv_ref
  271.4 5.9 shard_map.308
  277.3 3.7 add_convert_fusion.16.qkv_ref
  281.0 5.9 shard_map.307
  290.5 7.0 %collective-permute-done.23 = bf16[2,2,2,1,96,1536]{5,4,2,1,3,0:T(8,128)(2,1)} collective-permute-done((bf16[2,2,2,1,96,1536]{5,4,2,1,3,0:T(8,128)(2,1)}, bf16[2,2,2,1,96,1536]{5,4,2,1,3,0:T(8,128)(2,1)}, u32[]{:S(2)}, u32[]{:S(2)}) %collective-permute-start.23) | collective-permute-done | bytes 2359328 | tf_op jit(solution)/shard_map/ppermute | solution.py:152
  297.5 4.1 maximum_select_fusion.1
  304.7 3.2 multiply_convert_fusion.1
  307.9 2.9 convert_reduce_fusion
  310.9 3.2 multiply_convert_fusion.2
  314.1 2.9 convert_reduce_fusion.2
  334.3 2.8 fusion.168
  346.3 10.2 %shard_map.309 = bf16[832,576]{1,0:T(8,128)(2,1)} custom-call(bf16[832,576]{1,0:T(8,128)(2,1)} %add_convert_fusion.16.qkv_ref, bf16[832,192]{1,0:T(8,128)(2,1)} %copy.341.grad_ref), custom_call_target="tpu_custom_call" | custom-call | flops 332267520 | bytes 2396160 | tf_op jit(solution)/shard_map/pallas_call | solution.py:133
  356.6 3.6 collective-permute-done.28
  373.0 10.4 %shard_map.310 = bf16[832,576]{1,0:T(8,128)(2,1)} custom-call(bf16[832,576]{1,0:T(8,128)(2,1)} %add_convert_fusion.15.qkv_ref, bf16[832,192]{1,0:T(8,128)(2,1)} %copy.344.grad_ref), custom_call_target="tpu_custom_call" | custom-call | flops 332267520 | bytes 2396160 | tf_op jit(solution)/shard_map/pallas_call | solution.py:133
  383.4 4.6 collective-permute-done.25
  388.0 2.8 fusion.29
  392.7 6.6 collective-permute-done.30
  402.8 2.9 collective-permute-start.32
  408.8 3.6 add_convert_fusion.2
  415.1 8.1 %collective-permute-done.33 = bf16[1,2,1,96,768]{4,3,2,1,0:T(8,128)(2,1)} collective-permute-done((bf16[1,2,1,96,768]{4,3,2,1,0:T(8,128)(2,1)S(1)}, bf16[1,2,1,96,768]{4,3,2,1,0:T(8,128)(2,1)}, u32[]{:S(2)}, u32[]{:S(2)}) %collective-permute-start.33) | collective-permute-done | bytes 294944 | tf_op jit(solution)/shard_map/ppermute | solution.py:152
  424.2 5.2 collective-permute-done.32
  439.2 2.9 convert_reduce_fusion.1
  443.6 2.8 fusion.57
  447.3 3.3 convert_reduce_fusion.3
  457.8 4.7 convolution_add_fusion
  467.3 4.1 convolution_convert_fusion.2
  482.3 5.7 collective-permute-done.37
  494.3 2.7 collective-permute-start.39
  505.6 10.3 %shard_map.311 = bf16[832,576]{1,0:T(8,128)(2,1)} custom-call(bf16[832,576]{1,0:T(8,128)(2,1)} %add_convert_fusion.18.qkv_ref, bf16[832,192]{1,0:T(8,128)(2,1)} %copy.352.grad_ref), custom_call_target="tpu_custom_call" | custom-call | flops 332267520 | bytes 2396160 | tf_op jit(solution)/shard_map/pallas_call | solution.py:133
  534.9 10.4 %shard_map.312 = bf16[832,576]{1,0:T(8,128)(2,1)} custom-call(bf16[832,576]{1,0:T(8,128)(2,1)} %add_convert_fusion.17.qkv_ref, bf16[832,192]{1,0:T(8,128)(2,1)} %copy.355.grad_ref), custom_call_target="tpu_custom_call" | custom-call | flops 332267520 | bytes 2396160 | tf_op jit(solution)/shard_map/pallas_call | solution.py:133
  573.5 8.8 %collective-permute-done.47 = bf16[1,2,1,96,768]{4,3,2,1,0:T(8,128)(2,1)} collective-permute-done((bf16[1,2,1,96,768]{4,3,2,1,0:T(8,128)(2,1)}, bf16[1,2,1,96,768]{4,3,2,1,0:T(8,128)(2,1)}, u32[]{:S(2)}, u32[]{:S(2)}) %collective-permute-start.47) | collective-permute-done | bytes 294944 | tf_op jit(solution)/shard_map/ppermute | solution.py:152
  583.3 4.7 collective-permute-done.46
  589.8 3.0 convert_add_fusion
  611.1 3.1 add_convert_fusion
  622.1 3.3 collective-permute-done.63
  626.5 2.8 collective-permute-done.64
  635.4 9.1 %collective-permute-done.66 = f32[1,1,1,1,2,2,288]{6,5,4,3,2,1,0:T(2,128)S(1)} collective-permute-done((f32[1,1,1,1,2,2,288]{6,5,4,3,2,1,0:T(2,128)S(1)}, f32[1,1,1,1,2,2,288]{6,5,4,3,2,1,0:T(2,128)S(1)}, u32[]{:S(2)}, u32[]{:S(2)}) %collective-permute-start.66) | collective-permute-done | bytes 4640 | tf_op jit(solution)/shard_map/ppermute | solution.py:152
  648.6 5.5 collective-permute-done.51
  654.4 6.2 collective-permute-done.55
  660.8 2.9 collective-permute-done.52
  685.8 3.7 copy.379
  (731 shorter events, 328.8 us)
Async XLA Ops:
  3.7 73.5 %collective-permute-start.10 = (bf16[1,1,1,96,1536]{4,3,2,1,0:T(8,128)(2,1)}, bf16[1,1,1,96,1536]{4,3,2,1,0:T(8,128)(2,1)}, u32[]{:S(2)}, u32[]{:S(2)}) collective-permute-start(bf16[1,1,1,96,1536]{4,3,2,1,0:T(8,128)(2,1)} %pad_maximum_fusion.8), channel_id=1, source_target_pairs={{0,8},{4,12},{8,0},{12,4},{16,24},{20,28},{24,16},{28,20},{1,9},{5... | collective-permute-start | bytes 884744 | tf_op jit(solution)/shard_map/ppermute | solution.py:152
  7.7 48.4 %collective-permute-start.5 = (bf16[1,1,1,96,768]{3,4,2,1,0:T(8,128)(2,1)}, bf16[1,1,1,96,768]{3,4,2,1,0:T(8,128)(2,1)S(1)}, u32[]{:S(2)}, u32[]{:S(2)}) collective-permute-start(bf16[1,1,1,96,768]{3,4,2,1,0:T(8,128)(2,1)} %pad_maximum_fusion.16), channel_id=1, source_target_pairs={{0,8},{4,12},{8,0},{12,4},{16,24},{20,28},{24,16},{28,20},{1,9},{5... | collective-permute-start | bytes 442376 | tf_op jit(solution)/shard_map/ppermute | solution.py:152
  8.6 49.1 %collective-permute-start.15 = (bf16[1,1,1,96,768]{3,4,2,1,0:T(8,128)(2,1)}, bf16[1,1,1,96,768]{3,4,2,1,0:T(8,128)(2,1)S(1)}, u32[]{:S(2)}, u32[]{:S(2)}) collective-permute-start(bf16[1,1,1,96,768]{3,4,2,1,0:T(8,128)(2,1)} %pad_maximum_fusion.18), channel_id=1, source_target_pairs={{0,8},{4,12},{8,0},{12,4},{16,24},{20,28},{24,16},{28,20},{1,9},{5... | collective-permute-start | bytes 442376 | tf_op jit(solution)/shard_map/ppermute | solution.py:152
  10.6 13.8 %collective-permute-start = (f32[1,1,1,1,1,2,288]{6,0,5,4,3,2,1:T(1,128)S(1)}, f32[1,1,1,1,1,2,288]{6,0,5,4,3,2,1:T(1,128)S(1)}, u32[]{:S(2)}, u32[]{:S(2)}) collective-permute-start(f32[1,1,1,1,1,2,288]{6,0,5,4,3,2,1:T(1,128)S(1)} %bitcast.415), channel_id=1, source_target_pairs={{0,1},{1,0},{2,3},{3,2},{4,5},{5,4},{6,7},{7,6},{8,9},{9,8},{10,11... | collective-permute-start | bytes 6920 | tf_op jit(solution)/shard_map/ppermute | solution.py:152
  11.3 127.5 %collective-permute-start.20 = (bf16[1,1,1,96,1536]{4,3,2,1,0:T(8,128)(2,1)}, bf16[1,1,1,96,1536]{4,3,2,1,0:T(8,128)(2,1)}, u32[]{:S(2)}, u32[]{:S(2)}) collective-permute-start(bf16[1,1,1,96,1536]{4,3,2,1,0:T(8,128)(2,1)} %pad_maximum_fusion.10), channel_id=1, source_target_pairs={{0,8},{4,12},{8,0},{12,4},{16,24},{20,28},{24,16},{28,20},{1,9},{5... | collective-permute-start | bytes 884744 | tf_op jit(solution)/shard_map/ppermute | solution.py:152
  31.9 3.9 collective-permute-start.3
  36.4 7.0 %collective-permute-start.4 = (f32[1,2,2,2,2,2,288]{6,0,5,4,3,2,1:T(1,128)}, f32[1,2,2,2,2,2,288]{6,0,5,4,3,2,1:T(1,128)}, u32[]{:S(2)}, u32[]{:S(2)}) collective-permute-start(f32[1,2,2,2,2,2,288]{6,0,5,4,3,2,1:T(1,128)} %broadcast_select_fusion), channel_id=1, source_target_pairs={{0,16},{4,20},{8,24},{12,28},{16,0},{20,4},{24,8},{28,12},{1,17},{... | collective-permute-start | bytes 110600 | tf_op jit(solution)/shard_map/ppermute | solution.py:152
  56.2 17.3 %collective-permute-start.6 = (bf16[1,2,1,96,768]{3,4,2,1,0:T(8,128)(2,1)S(1)}, bf16[1,2,1,96,768]{3,4,2,1,0:T(8,128)(2,1)S(1)}, u32[]{:S(2)}, u32[]{:S(2)}) collective-permute-start(bf16[1,2,1,96,768]{3,4,2,1,0:T(8,128)(2,1)S(1)} %maximum_select_fusion.11), channel_id=1, source_target_pairs={{0,16},{4,20},{8,24},{12,28},{16,0},{20,4},{24,8},{28,12},{1,17},{... | collective-permute-start | bytes 884744 | tf_op jit(solution)/shard_map/ppermute | solution.py:152
  75.0 14.5 %collective-permute-start.7 = (bf16[2,2,1,96,768]{4,3,2,1,0:T(8,128)(2,1)}, bf16[2,2,1,96,768]{4,3,2,1,0:T(8,128)(2,1)}, u32[]{:S(2)}, u32[]{:S(2)}) collective-permute-start(bf16[2,2,1,96,768]{4,3,2,1,0:T(8,128)(2,1)} %copy.316), channel_id=1, source_target_pairs={{0,4},{4,0},{8,12},{12,8},{16,20},{20,16},{24,28},{28,24},{1,5},{5... | collective-permute-start | bytes 1769480 | tf_op jit(solution)/shard_map/ppermute | solution.py:152
  79.3 26.8 %collective-permute-start.11 = (bf16[1,2,1,96,1536]{4,3,1,0,2:T(8,128)(2,1)}, bf16[1,2,1,96,1536]{4,3,1,0,2:T(8,128)(2,1)}, u32[]{:S(2)}, u32[]{:S(2)}) collective-permute-start(bf16[1,2,1,96,1536]{4,3,1,0,2:T(8,128)(2,1)} %fusion.96), channel_id=1, source_target_pairs={{0,16},{4,20},{8,24},{12,28},{16,0},{20,4},{24,8},{28,12},{1,17},{... | collective-permute-start | bytes 1769480 | tf_op jit(solution)/shard_map/ppermute | solution.py:152
  97.6 29.2 %collective-permute-start.8 = (bf16[768,768]{1,0:T(8,128)(2,1)}, bf16[768,768]{1,0:T(8,128)(2,1)}, u32[]{:S(2)}, u32[]{:S(2)}) collective-permute-start(bf16[768,768]{1,0:T(8,128)(2,1)} %bitcast.374), channel_id=1, source_target_pairs={{0,2},{1,3},{2,0},{3,1},{4,6},{5,7},{6,4},{7,5},{8,10},{9,11},{10,... | collective-permute-start | bytes 3538952 | tf_op jit(solution)/shard_map/ppermute | solution.py:218
  108.6 40.5 %collective-permute-start.12 = (bf16[2,2,1,96,1536]{4,3,1,0,2:T(8,128)(2,1)}, bf16[2,2,1,96,1536]{4,3,1,0,2:T(8,128)(2,1)}, u32[]{:S(2)}, u32[]{:S(2)}) collective-permute-start(bf16[2,2,1,96,1536]{4,3,1,0,2:T(8,128)(2,1)} %bitcast_select_fusion), channel_id=1, source_target_pairs={{0,2},{1,3},{2,0},{3,1},{4,6},{5,7},{6,4},{7,5},{8,10},{9,11},{10,... | collective-permute-start | bytes 3538952 | tf_op jit(solution)/shard_map/ppermute | solution.py:218
  138.8 40.8 %collective-permute-start.9 = (bf16[832,768]{1,0:T(8,128)(2,1)S(1)}, bf16[832,768]{1,0:T(8,128)(2,1)S(1)}, u32[]{:S(2)}, u32[]{:S(2)}) collective-permute-start(bf16[832,768]{1,0:T(8,128)(2,1)S(1)} %add_convert_fusion.9), channel_id=1, source_target_pairs={{0,1},{1,0},{2,3},{3,2},{4,5},{5,4},{6,7},{7,6},{8,9},{9,8},{10,11... | collective-permute-start | bytes 3833864 | tf_op jit(solution)/shard_map/ppermute | solution.py:215
  140.4 36.5 %collective-permute-start.21 = (bf16[1,2,1,96,1536]{4,3,2,1,0:T(8,128)(2,1)S(1)}, bf16[1,2,1,96,1536]{4,3,2,1,0:T(8,128)(2,1)S(1)}, u32[]{:S(2)}, u32[]{:S(2)}) collective-permute-start(bf16[1,2,1,96,1536]{4,3,2,1,0:T(8,128)(2,1)S(1)} %maximum_select_fusion.9), channel_id=1, source_target_pairs={{0,16},{4,20},{8,24},{12,28},{16,0},{20,4},{24,8},{28,12},{1,17},{... | collective-permute-start | bytes 1769480 | tf_op jit(solution)/shard_map/ppermute | solution.py:152
  150.7 50.3 %collective-permute-start.13 = (bf16[2,2,2,1,96,1536]{5,4,3,2,1,0:T(8,128)(2,1)S(1)}, bf16[2,2,2,1,96,1536]{5,4,3,2,1,0:T(8,128)(2,1)S(1)}, u32[]{:S(2)}, u32[]{:S(2)}) collective-permute-start(bf16[2,2,2,1,96,1536]{5,4,3,2,1,0:T(8,128)(2,1)S(1)} %pad_maximum_fusion), channel_id=1, source_target_pairs={{0,4},{4,0},{8,12},{12,8},{16,20},{20,16},{24,28},{28,24},{1,5},{5... | collective-permute-start | bytes 7077896 | tf_op jit(solution)/shard_map/ppermute | solution.py:152
  152.4 61.5 %collective-permute-start.16 = (bf16[1,2,1,96,768]{3,4,2,1,0:T(8,128)(2,1)S(1)}, bf16[1,2,1,96,768]{3,4,2,1,0:T(8,128)(2,1)S(1)}, u32[]{:S(2)}, u32[]{:S(2)}) collective-permute-start(bf16[1,2,1,96,768]{3,4,2,1,0:T(8,128)(2,1)S(1)} %maximum_select_fusion.13), channel_id=1, source_target_pairs={{0,16},{4,20},{8,24},{12,28},{16,0},{20,4},{24,8},{28,12},{1,17},{... | collective-permute-start | bytes 884744 | tf_op jit(solution)/shard_map/ppermute | solution.py:152
  178.1 63.0 %collective-permute-start.22 = (bf16[2,2,1,96,1536]{4,3,2,1,0:T(8,128)(2,1)}, bf16[2,2,1,96,1536]{4,3,2,1,0:T(8,128)(2,1)}, u32[]{:S(2)}, u32[]{:S(2)}) collective-permute-start(bf16[2,2,1,96,1536]{4,3,2,1,0:T(8,128)(2,1)} %fusion.39), channel_id=1, source_target_pairs={{0,2},{1,3},{2,0},{3,1},{4,6},{5,7},{6,4},{7,5},{8,10},{9,11},{10,... | collective-permute-start | bytes 3538952 | tf_op jit(solution)/shard_map/ppermute | solution.py:218
  213.9 30.8 %collective-permute-start.14 = (bf16[832,768]{1,0:T(8,128)(2,1)}, bf16[832,768]{1,0:T(8,128)(2,1)}, u32[]{:S(2)}, u32[]{:S(2)}) collective-permute-start(bf16[832,768]{1,0:T(8,128)(2,1)} %add_convert_fusion.7), channel_id=1, source_target_pairs={{0,1},{1,0},{2,3},{3,2},{4,5},{5,4},{6,7},{7,6},{8,9},{9,8},{10,11... | collective-permute-start | bytes 3833864 | tf_op jit(solution)/shard_map/ppermute | solution.py:215
  215.3 18.3 %collective-permute-start.17 = (bf16[2,2,1,96,768]{4,3,2,1,0:T(8,128)(2,1)}, bf16[2,2,1,96,768]{4,3,2,1,0:T(8,128)(2,1)}, u32[]{:S(2)}, u32[]{:S(2)}) collective-permute-start(bf16[2,2,1,96,768]{4,3,2,1,0:T(8,128)(2,1)} %copy.329), channel_id=1, source_target_pairs={{0,4},{4,0},{8,12},{12,8},{16,20},{20,16},{24,28},{28,24},{1,5},{5... | collective-permute-start | bytes 1769480 | tf_op jit(solution)/shard_map/ppermute | solution.py:152
  239.6 28.4 %collective-permute-start.18 = (bf16[768,768]{1,0:T(8,128)(2,1)}, bf16[768,768]{1,0:T(8,128)(2,1)}, u32[]{:S(2)}, u32[]{:S(2)}) collective-permute-start(bf16[768,768]{1,0:T(8,128)(2,1)} %bitcast.62), channel_id=1, source_target_pairs={{0,2},{1,3},{2,0},{3,1},{4,6},{5,7},{6,4},{7,5},{8,10},{9,11},{10,... | collective-permute-start | bytes 3538952 | tf_op jit(solution)/shard_map/ppermute | solution.py:218
  244.1 53.4 %collective-permute-start.23 = (bf16[2,2,2,1,96,1536]{5,4,2,1,3,0:T(8,128)(2,1)}, bf16[2,2,2,1,96,1536]{5,4,2,1,3,0:T(8,128)(2,1)}, u32[]{:S(2)}, u32[]{:S(2)}) collective-permute-start(bf16[2,2,2,1,96,1536]{5,4,2,1,3,0:T(8,128)(2,1)} %pad_maximum_fusion.1), channel_id=1, source_target_pairs={{0,4},{4,0},{8,12},{12,8},{16,20},{20,16},{24,28},{28,24},{1,5},{5... | collective-permute-start | bytes 7077896 | tf_op jit(solution)/shard_map/ppermute | solution.py:152
  290.4 11.9 %collective-permute-start.19 = (bf16[832,768]{1,0:T(8,128)(2,1)S(1)}, bf16[832,768]{1,0:T(8,128)(2,1)S(1)}, u32[]{:S(2)}, u32[]{:S(2)}) collective-permute-start(bf16[832,768]{1,0:T(8,128)(2,1)S(1)} %add_convert_fusion.5), channel_id=1, source_target_pairs={{0,1},{1,0},{2,3},{3,2},{4,5},{5,4},{6,7},{7,6},{8,9},{9,8},{10,11... | collective-permute-start | bytes 3833864 | tf_op jit(solution)/shard_map/ppermute | solution.py:215
  319.4 11.0 %collective-permute-start.26 = (bf16[832,768]{1,0:T(8,128)(2,1)S(1)}, bf16[832,768]{1,0:T(8,128)(2,1)S(1)}, u32[]{:S(2)}, u32[]{:S(2)}) collective-permute-start(bf16[832,768]{1,0:T(8,128)(2,1)S(1)} %convolution_add_fusion.1), channel_id=1, source_target_pairs={{0,1},{1,0},{2,3},{3,2},{4,5},{5,4},{6,7},{7,6},{8,9},{9,8},{10,11... | collective-permute-start | bytes 3833864 | tf_op jit(solution)/shard_map/ppermute | solution.py:215
  321.9 12.3 %collective-permute-start.24 = (bf16[832,768]{1,0:T(8,128)(2,1)S(1)}, bf16[832,768]{1,0:T(8,128)(2,1)S(1)}, u32[]{:S(2)}, u32[]{:S(2)}) collective-permute-start(bf16[832,768]{1,0:T(8,128)(2,1)S(1)} %add_convert_fusion.3), channel_id=1, source_target_pairs={{0,1},{1,0},{2,3},{3,2},{4,5},{5,4},{6,7},{7,6},{8,9},{9,8},{10,11... | collective-permute-start | bytes 3833864 | tf_op jit(solution)/shard_map/ppermute | solution.py:215
  331.9 28.2 %collective-permute-start.28 = (bf16[2,2,2,1,96,768]{5,4,2,1,3,0:T(8,128)(2,1)}, bf16[2,2,2,1,96,768]{5,4,2,1,3,0:T(8,128)(2,1)}, u32[]{:S(2)}, u32[]{:S(2)}) collective-permute-start(bf16[2,2,2,1,96,768]{5,4,2,1,3,0:T(8,128)(2,1)} %fusion.36), channel_id=1, source_target_pairs={{0,4},{4,0},{8,12},{12,8},{16,20},{20,16},{24,28},{28,24},{1,5},{5... | collective-permute-start | bytes 3538952 | tf_op jit(solution)/shard_map/ppermute | solution.py:152
  332.4 29.6 %collective-permute-start.27 = (bf16[768,768]{1,0:T(8,128)(2,1)}, bf16[768,768]{1,0:T(8,128)(2,1)}, u32[]{:S(2)}, u32[]{:S(2)}) collective-permute-start(bf16[768,768]{1,0:T(8,128)(2,1)} %convolution_convert_fusion.6), channel_id=1, source_target_pairs={{0,2},{1,3},{2,0},{3,1},{4,6},{5,7},{6,4},{7,5},{8,10},{9,11},{10,... | collective-permute-start | bytes 3538952 | tf_op jit(solution)/shard_map/ppermute | solution.py:218
  344.8 43.1 %collective-permute-start.25 = (bf16[4,197,768]{2,1,0:T(8,128)(2,1)}, bf16[4,197,768]{2,1,0:T(8,128)(2,1)}, u32[]{:S(2)}, u32[]{:S(2)}) collective-permute-start(bf16[4,197,768]{2,1,0:T(8,128)(2,1)} %slice.398), channel_id=1, source_target_pairs={{0,2},{1,3},{2,0},{3,1},{4,6},{5,7},{6,4},{7,5},{8,10},{9,11},{10,... | collective-permute-start | bytes 3631112 | tf_op jit(solution)/shard_map/ppermute | solution.py:218
  364.2 35.1 %collective-permute-start.30 = (bf16[2,2,1,96,768]{4,3,2,1,0:T(8,128)(2,1)S(1)}, bf16[2,2,1,96,768]{4,3,2,1,0:T(8,128)(2,1)}, u32[]{:S(2)}, u32[]{:S(2)}) collective-permute-start(bf16[2,2,1,96,768]{4,3,2,1,0:T(8,128)(2,1)S(1)} %slice_bitcast_fusion.1), channel_id=1, source_target_pairs={{0,2},{1,3},{2,0},{3,1},{4,6},{5,7},{6,4},{7,5},{8,10},{9,11},{10,... | collective-permute-start | bytes 1769480 | tf_op jit(solution)/shard_map/ppermute | solution.py:218
  365.7 34.9 %collective-permute-start.29 = (bf16[2,2,1,96,768]{4,3,2,1,0:T(8,128)(2,1)}, bf16[2,2,1,96,768]{4,3,2,1,0:T(8,128)(2,1)}, u32[]{:S(2)}, u32[]{:S(2)}) collective-permute-start(bf16[2,2,1,96,768]{4,3,2,1,0:T(8,128)(2,1)} %constant_dynamic-slice_fusion.27), channel_id=1, source_target_pairs={{0,4},{4,0},{8,12},{12,8},{16,20},{20,16},{24,28},{28,24},{1,5},{5... | collective-permute-start | bytes 1769480 | tf_op jit(solution)/shard_map/ppermute | solution.py:152
  402.0 21.2 %collective-permute-start.33 = (bf16[1,2,1,96,768]{4,3,2,1,0:T(8,128)(2,1)S(1)}, bf16[1,2,1,96,768]{4,3,2,1,0:T(8,128)(2,1)}, u32[]{:S(2)}, u32[]{:S(2)}) collective-permute-start(bf16[1,2,1,96,768]{4,3,2,1,0:T(8,128)(2,1)S(1)} %constant_dynamic-slice_fusion.25), channel_id=1, source_target_pairs={{0,16},{4,20},{8,24},{12,28},{16,0},{20,4},{24,8},{28,12},{1,17},{... | collective-permute-start | bytes 884744 | tf_op jit(solution)/shard_map/ppermute | solution.py:152
  402.8 26.5 %collective-permute-start.32 = (bf16[1,2,1,96,768]{4,3,2,1,0:T(8,128)(2,1)}, bf16[1,2,1,96,768]{4,3,2,1,0:T(8,128)(2,1)}, u32[]{:S(2)}, u32[]{:S(2)}) collective-permute-start(bf16[1,2,1,96,768]{4,3,2,1,0:T(8,128)(2,1)} %constant_dynamic-slice_fusion.26), channel_id=1, source_target_pairs={{0,16},{4,20},{8,24},{12,28},{16,0},{20,4},{24,8},{28,12},{1,17},{... | collective-permute-start | bytes 884744 | tf_op jit(solution)/shard_map/ppermute | solution.py:152
  412.4 18.8 %collective-permute-start.31 = (bf16[832,768]{1,0:T(8,128)(2,1)}, bf16[832,768]{1,0:T(8,128)(2,1)}, u32[]{:S(2)}, u32[]{:S(2)}) collective-permute-start(bf16[832,768]{1,0:T(8,128)(2,1)} %add_convert_fusion.2), channel_id=1, source_target_pairs={{0,1},{1,0},{2,3},{3,2},{4,5},{5,4},{6,7},{7,6},{8,9},{9,8},{10,11... | collective-permute-start | bytes 3833864 | tf_op jit(solution)/shard_map/ppermute | solution.py:215
  455.7 19.7 %collective-permute-start.35 = (bf16[2,2,2,1,96,384]{5,4,2,1,3,0:T(8,128)(2,1)}, bf16[2,2,2,1,96,384]{5,4,2,1,3,0:T(8,128)(2,1)}, u32[]{:S(2)}, u32[]{:S(2)}) collective-permute-start(bf16[2,2,2,1,96,384]{5,4,2,1,3,0:T(8,128)(2,1)} %fusion.93), channel_id=1, source_target_pairs={{0,4},{4,0},{8,12},{12,8},{16,20},{20,16},{24,28},{28,24},{1,5},{5... | collective-permute-start | bytes 1769480 | tf_op jit(solution)/shard_map/ppermute | solution.py:152
  457.2 16.6 %collective-permute-start.34 = (bf16[768,384]{0,1:T(8,128)(2,1)}, bf16[768,384]{0,1:T(8,128)(2,1)}, u32[]{:S(2)}, u32[]{:S(2)}) collective-permute-start(bf16[768,384]{0,1:T(8,128)(2,1)} %get-tuple-element.248), channel_id=1, source_target_pairs={{0,2},{1,3},{2,0},{3,1},{4,6},{5,7},{6,4},{7,5},{8,10},{9,11},{10,... | collective-permute-start | bytes 1769480 | tf_op jit(solution)/shard_map/ppermute | solution.py:218
  464.6 12.4 %collective-permute-start.62 = (bf16[1,1,1,96,768]{4,3,2,1,0:T(8,128)(2,1)}, bf16[1,1,1,96,768]{4,3,2,1,0:T(8,128)(2,1)}, u32[]{:S(2)}, u32[]{:S(2)}) collective-permute-start(bf16[1,1,1,96,768]{4,3,2,1,0:T(8,128)(2,1)} %constant_dynamic-slice_fusion.8), channel_id=1, source_target_pairs={{0,8},{4,12},{8,0},{12,4},{16,24},{20,28},{24,16},{28,20},{1,9},{5... | collective-permute-start | bytes 442376 | tf_op jit(solution)/shard_map/ppermute | solution.py:152
  465.2 15.5 %collective-permute-start.60 = (bf16[1,1,1,96,768]{4,3,2,1,0:T(8,128)(2,1)}, bf16[1,1,1,96,768]{4,3,2,1,0:T(8,128)(2,1)}, u32[]{:S(2)}, u32[]{:S(2)}) collective-permute-start(bf16[1,1,1,96,768]{4,3,2,1,0:T(8,128)(2,1)} %constant_dynamic-slice_fusion.10), channel_id=1, source_target_pairs={{0,8},{4,12},{8,0},{12,4},{16,24},{20,28},{24,16},{28,20},{1,9},{5... | collective-permute-start | bytes 442376 | tf_op jit(solution)/shard_map/ppermute | solution.py:152
  476.9 11.5 %collective-permute-start.36 = (bf16[832,768]{1,0:T(8,128)(2,1)S(1)}, bf16[832,768]{1,0:T(8,128)(2,1)S(1)}, u32[]{:S(2)}, u32[]{:S(2)}) collective-permute-start(bf16[832,768]{1,0:T(8,128)(2,1)S(1)} %copy-done.67), channel_id=1, source_target_pairs={{0,1},{1,0},{2,3},{3,2},{4,5},{5,4},{6,7},{7,6},{8,9},{9,8},{10,11... | collective-permute-start | bytes 3833864 | tf_op jit(solution)/shard_map/ppermute | solution.py:215
  478.6 9.5 %collective-permute-start.37 = (bf16[2,2,1,96,384]{4,3,2,1,0:T(8,128)(2,1)S(1)}, bf16[2,2,1,96,384]{4,3,2,1,0:T(8,128)(2,1)S(1)}, u32[]{:S(2)}, u32[]{:S(2)}) collective-permute-start(bf16[2,2,1,96,384]{4,3,2,1,0:T(8,128)(2,1)S(1)} %constant_dynamic-slice_fusion.24), channel_id=1, source_target_pairs={{0,4},{4,0},{8,12},{12,8},{16,20},{20,16},{24,28},{28,24},{1,5},{5... | collective-permute-start | bytes 884744 | tf_op jit(solution)/shard_map/ppermute | solution.py:152
  479.1 9.2 %collective-permute-start.38 = (bf16[2,2,1,96,384]{4,3,2,1,0:T(8,128)(2,1)S(1)}, bf16[2,2,1,96,384]{4,3,2,1,0:T(8,128)(2,1)S(1)}, u32[]{:S(2)}, u32[]{:S(2)}) collective-permute-start(bf16[2,2,1,96,384]{4,3,2,1,0:T(8,128)(2,1)S(1)} %slice_bitcast_fusion.3), channel_id=1, source_target_pairs={{0,2},{1,3},{2,0},{3,1},{4,6},{5,7},{6,4},{7,5},{8,10},{9,11},{10,... | collective-permute-start | bytes 884744 | tf_op jit(solution)/shard_map/ppermute | solution.py:218
  490.8 27.7 %collective-permute-start.42 = (bf16[2,2,2,1,96,768]{5,4,2,1,3,0:T(8,128)(2,1)}, bf16[2,2,2,1,96,768]{5,4,2,1,3,0:T(8,128)(2,1)}, u32[]{:S(2)}, u32[]{:S(2)}) collective-permute-start(bf16[2,2,2,1,96,768]{5,4,2,1,3,0:T(8,128)(2,1)} %fusion.32), channel_id=1, source_target_pairs={{0,4},{4,0},{8,12},{12,8},{16,20},{20,16},{24,28},{28,24},{1,5},{5... | collective-permute-start | bytes 3538952 | tf_op jit(solution)/shard_map/ppermute | solution.py:152
  492.4 28.1 %collective-permute-start.41 = (bf16[768,768]{1,0:T(8,128)(2,1)}, bf16[768,768]{1,0:T(8,128)(2,1)}, u32[]{:S(2)}, u32[]{:S(2)}) collective-permute-start(bf16[768,768]{1,0:T(8,128)(2,1)} %convolution_convert_fusion.2), channel_id=1, source_target_pairs={{0,2},{1,3},{2,0},{3,1},{4,6},{5,7},{6,4},{7,5},{8,10},{9,11},{10,... | collective-permute-start | bytes 3538952 | tf_op jit(solution)/shard_map/ppermute | solution.py:218
  493.9 21.9 %collective-permute-start.40 = (bf16[1,2,1,96,384]{4,3,2,1,0:T(8,128)(2,1)S(1)}, bf16[1,2,1,96,384]{4,3,2,1,0:T(8,128)(2,1)S(1)}, u32[]{:S(2)}, u32[]{:S(2)}) collective-permute-start(bf16[1,2,1,96,384]{4,3,2,1,0:T(8,128)(2,1)S(1)} %constant_dynamic-slice_fusion.22), channel_id=1, source_target_pairs={{0,16},{4,20},{8,24},{12,28},{16,0},{20,4},{24,8},{28,12},{1,17},{... | collective-permute-start | bytes 442376 | tf_op jit(solution)/shard_map/ppermute | solution.py:152
  494.3 22.3 %collective-permute-start.39 = (bf16[1,2,1,96,384]{4,3,2,1,0:T(8,128)(2,1)S(1)}, bf16[1,2,1,96,384]{4,3,2,1,0:T(8,128)(2,1)S(1)}, u32[]{:S(2)}, u32[]{:S(2)}) collective-permute-start(bf16[1,2,1,96,384]{4,3,2,1,0:T(8,128)(2,1)S(1)} %constant_dynamic-slice_fusion.23), channel_id=1, source_target_pairs={{0,16},{4,20},{8,24},{12,28},{16,0},{20,4},{24,8},{28,12},{1,17},{... | collective-permute-start | bytes 442376 | tf_op jit(solution)/shard_map/ppermute | solution.py:152
  525.6 32.5 %collective-permute-start.44 = (bf16[2,2,1,96,768]{4,3,2,1,0:T(8,128)(2,1)}, bf16[2,2,1,96,768]{4,3,2,1,0:T(8,128)(2,1)}, u32[]{:S(2)}, u32[]{:S(2)}) collective-permute-start(bf16[2,2,1,96,768]{4,3,2,1,0:T(8,128)(2,1)} %slice_bitcast_fusion), channel_id=1, source_target_pairs={{0,2},{1,3},{2,0},{3,1},{4,6},{5,7},{6,4},{7,5},{8,10},{9,11},{10,... | collective-permute-start | bytes 1769480 | tf_op jit(solution)/shard_map/ppermute | solution.py:218
  527.9 31.4 %collective-permute-start.43 = (bf16[2,2,1,96,768]{4,3,2,1,0:T(8,128)(2,1)}, bf16[2,2,1,96,768]{4,3,2,1,0:T(8,128)(2,1)}, u32[]{:S(2)}, u32[]{:S(2)}) collective-permute-start(bf16[2,2,1,96,768]{4,3,2,1,0:T(8,128)(2,1)} %constant_dynamic-slice_fusion.21), channel_id=1, source_target_pairs={{0,4},{4,0},{8,12},{12,8},{16,20},{20,16},{24,28},{28,24},{1,5},{5... | collective-permute-start | bytes 1769480 | tf_op jit(solution)/shard_map/ppermute | solution.py:152
  547.8 5.3 collective-permute-start.58
  548.8 4.4 collective-permute-start.57
  561.6 20.7 %collective-permute-start.47 = (bf16[1,2,1,96,768]{4,3,2,1,0:T(8,128)(2,1)}, bf16[1,2,1,96,768]{4,3,2,1,0:T(8,128)(2,1)}, u32[]{:S(2)}, u32[]{:S(2)}) collective-permute-start(bf16[1,2,1,96,768]{4,3,2,1,0:T(8,128)(2,1)} %constant_dynamic-slice_fusion.19), channel_id=1, source_target_pairs={{0,16},{4,20},{8,24},{12,28},{16,0},{20,4},{24,8},{28,12},{1,17},{... | collective-permute-start | bytes 884744 | tf_op jit(solution)/shard_map/ppermute | solution.py:152
  563.8 24.2 %collective-permute-start.46 = (bf16[1,2,1,96,768]{4,3,2,1,0:T(8,128)(2,1)}, bf16[1,2,1,96,768]{4,3,2,1,0:T(8,128)(2,1)}, u32[]{:S(2)}, u32[]{:S(2)}) collective-permute-start(bf16[1,2,1,96,768]{4,3,2,1,0:T(8,128)(2,1)} %constant_dynamic-slice_fusion.20), channel_id=1, source_target_pairs={{0,16},{4,20},{8,24},{12,28},{16,0},{20,4},{24,8},{28,12},{1,17},{... | collective-permute-start | bytes 884744 | tf_op jit(solution)/shard_map/ppermute | solution.py:152
  570.5 19.3 %collective-permute-start.45 = (bf16[832,768]{1,0:T(8,128)(2,1)S(1)}, bf16[832,768]{1,0:T(8,128)(2,1)}, u32[]{:S(2)}, u32[]{:S(2)}) collective-permute-start(bf16[832,768]{1,0:T(8,128)(2,1)S(1)} %add_convert_fusion.1), channel_id=1, source_target_pairs={{0,1},{1,0},{2,3},{3,2},{4,5},{5,4},{6,7},{7,6},{8,9},{9,8},{10,11... | collective-permute-start | bytes 3833864 | tf_op jit(solution)/shard_map/ppermute | solution.py:215
  600.0 18.8 %collective-permute-start.50 = (bf16[2,2,2,1,96,384]{5,4,2,1,3,0:T(8,128)(2,1)}, bf16[2,2,2,1,96,384]{5,4,2,1,3,0:T(8,128)(2,1)}, u32[]{:S(2)}, u32[]{:S(2)}) collective-permute-start(bf16[2,2,2,1,96,384]{5,4,2,1,3,0:T(8,128)(2,1)} %fusion.89), channel_id=1, source_target_pairs={{0,4},{4,0},{8,12},{12,8},{16,20},{20,16},{24,28},{28,24},{1,5},{5... | collective-permute-start | bytes 1769480 | tf_op jit(solution)/shard_map/ppermute | solution.py:152
  600.8 15.8 %collective-permute-start.49 = (bf16[768,384]{0,1:T(8,128)(2,1)}, bf16[768,384]{0,1:T(8,128)(2,1)}, u32[]{:S(2)}, u32[]{:S(2)}) collective-permute-start(bf16[768,384]{0,1:T(8,128)(2,1)} %get-tuple-element.246), channel_id=1, source_target_pairs={{0,2},{1,3},{2,0},{3,1},{4,6},{5,7},{6,4},{7,5},{8,10},{9,11},{10,... | collective-permute-start | bytes 1769480 | tf_op jit(solution)/shard_map/ppermute | solution.py:218
  608.3 7.5 %collective-permute-start.61 = (bf16[1,1,1,96,768]{4,3,2,1,0:T(8,128)(2,1)S(1)}, bf16[1,1,1,96,768]{4,3,2,1,0:T(8,128)(2,1)S(1)}, u32[]{:S(2)}, u32[]{:S(2)}) collective-permute-start(bf16[1,1,1,96,768]{4,3,2,1,0:T(8,128)(2,1)S(1)} %constant_dynamic-slice_fusion.9), channel_id=1, source_target_pairs={{0,8},{4,12},{8,0},{12,4},{16,24},{20,28},{24,16},{28,20},{1,9},{5... | collective-permute-start | bytes 442376 | tf_op jit(solution)/shard_map/ppermute | solution.py:152
  609.1 16.4 %collective-permute-start.59 = (bf16[1,1,1,96,768]{4,3,2,1,0:T(8,128)(2,1)}, bf16[1,1,1,96,768]{4,3,2,1,0:T(8,128)(2,1)}, u32[]{:S(2)}, u32[]{:S(2)}) collective-permute-start(bf16[1,1,1,96,768]{4,3,2,1,0:T(8,128)(2,1)} %constant_dynamic-slice_fusion.11), channel_id=1, source_target_pairs={{0,8},{4,12},{8,0},{12,4},{16,24},{20,28},{24,16},{28,20},{1,9},{5... | collective-permute-start | bytes 442376 | tf_op jit(solution)/shard_map/ppermute | solution.py:152
  614.3 68.9 %collective-permute-start.48 = (bf16[4,197,768]{2,1,0:T(8,128)(2,1)S(1)}, bf16[4,197,768]{2,1,0:T(8,128)(2,1)}, u32[]{:S(2)}, u32[]{:S(2)}) collective-permute-start(bf16[4,197,768]{2,1,0:T(8,128)(2,1)S(1)} %slice.399), channel_id=1, source_target_pairs={{0,2},{1,3},{2,0},{3,1},{4,6},{5,7},{6,4},{7,5},{8,10},{9,11},{10,... | collective-permute-start | bytes 3631112 | tf_op jit(solution)/shard_map/ppermute | solution.py:218
  620.3 5.1 collective-permute-start.63
  625.4 3.9 collective-permute-start.64
  633.2 11.3 %collective-permute-start.66 = (f32[1,1,1,1,2,2,288]{6,5,4,3,2,1,0:T(2,128)S(1)}, f32[1,1,1,1,2,2,288]{6,5,4,3,2,1,0:T(2,128)S(1)}, u32[]{:S(2)}, u32[]{:S(2)}) collective-permute-start(f32[1,1,1,1,2,2,288]{6,5,4,3,2,1,0:T(2,128)S(1)} %constant_dynamic-slice_fusion.2), channel_id=1, source_target_pairs={{0,2},{1,3},{2,0},{3,1},{4,6},{5,7},{6,4},{7,5},{8,10},{9,11},{10,... | collective-permute-start | bytes 13832 | tf_op jit(solution)/shard_map/ppermute | solution.py:152
  634.1 14.1 %collective-permute-start.54 = (bf16[2,2,1,96,384]{4,3,2,1,0:T(8,128)(2,1)S(1)}, bf16[2,2,1,96,384]{4,3,2,1,0:T(8,128)(2,1)S(1)}, u32[]{:S(2)}, u32[]{:S(2)}) collective-permute-start(bf16[2,2,1,96,384]{4,3,2,1,0:T(8,128)(2,1)S(1)} %slice_bitcast_fusion.2), channel_id=1, source_target_pairs={{0,2},{1,3},{2,0},{3,1},{4,6},{5,7},{6,4},{7,5},{8,10},{9,11},{10,... | collective-permute-start | bytes 884744 | tf_op jit(solution)/shard_map/ppermute | solution.py:218
  644.7 9.5 %collective-permute-start.51 = (bf16[2,2,1,96,384]{4,3,2,1,0:T(8,128)(2,1)S(1)}, bf16[2,2,1,96,384]{4,3,2,1,0:T(8,128)(2,1)S(1)}, u32[]{:S(2)}, u32[]{:S(2)}) collective-permute-start(bf16[2,2,1,96,384]{4,3,2,1,0:T(8,128)(2,1)S(1)} %constant_dynamic-slice_fusion.18), channel_id=1, source_target_pairs={{0,4},{4,0},{8,12},{12,8},{16,20},{20,16},{24,28},{28,24},{1,5},{5... | collective-permute-start | bytes 884744 | tf_op jit(solution)/shard_map/ppermute | solution.py:152
  648.2 12.4 %collective-permute-start.55 = (bf16[1,2,1,96,384]{4,3,2,1,0:T(8,128)(2,1)S(1)}, bf16[1,2,1,96,384]{4,3,2,1,0:T(8,128)(2,1)S(1)}, u32[]{:S(2)}, u32[]{:S(2)}) collective-permute-start(bf16[1,2,1,96,384]{4,3,2,1,0:T(8,128)(2,1)S(1)} %constant_dynamic-slice_fusion.15), channel_id=1, source_target_pairs={{0,16},{4,20},{8,24},{12,28},{16,0},{20,4},{24,8},{28,12},{1,17},{... | collective-permute-start | bytes 442376 | tf_op jit(solution)/shard_map/ppermute | solution.py:152
  654.3 9.5 %collective-permute-start.52 = (bf16[1,2,1,96,384]{4,3,2,1,0:T(8,128)(2,1)S(1)}, bf16[1,2,1,96,384]{4,3,2,1,0:T(8,128)(2,1)S(1)}, u32[]{:S(2)}, u32[]{:S(2)}) collective-permute-start(bf16[1,2,1,96,384]{4,3,2,1,0:T(8,128)(2,1)S(1)} %constant_dynamic-slice_fusion.17), channel_id=1, source_target_pairs={{0,16},{4,20},{8,24},{12,28},{16,0},{20,4},{24,8},{28,12},{1,17},{... | collective-permute-start | bytes 442376 | tf_op jit(solution)/shard_map/ppermute | solution.py:152
  660.8 4.6 collective-permute-start.56
  663.9 8.0 %collective-permute-start.53 = (bf16[1,1,1,96,384]{4,3,2,1,0:T(8,128)(2,1)S(1)}, bf16[1,1,1,96,384]{4,3,2,1,0:T(8,128)(2,1)}, u32[]{:S(2)}, u32[]{:S(2)}) collective-permute-start(bf16[1,1,1,96,384]{4,3,2,1,0:T(8,128)(2,1)S(1)} %constant_dynamic-slice_fusion.16), channel_id=1, source_target_pairs={{0,8},{4,12},{8,0},{12,4},{16,24},{20,28},{24,16},{28,20},{1,9},{5... | collective-permute-start | bytes 221192 | tf_op jit(solution)/shard_map/ppermute | solution.py:152
  (165 other events, 1612.1 us)

commit v3 on v2

--- a/solution.py
+++ b/solution.py
@@ -261,6 +261,10 @@
             [qkv_weight[layer].reshape(shard_rows, qkv_cols), out_weight[layer].T], axis=1
         ).astype(bf16)
         mlp_shard = jnp.concatenate([up_weight[layer], down_weight[layer].T], axis=1).astype(bf16)
+        if layer:
+            (own, side_own), up_pair, down_pair = pieces[0]
+            own, attn_shard, mlp_shard = lax.optimization_barrier((own, attn_shard, mlp_shard))
+            pieces[0] = ((own, side_own), up_pair, down_pair)
         attn_pair = gather_side_last(attn_shard)
         mlp_pair = gather_low_last(mlp_shard)
         pieces.append(

time: 701 us -> 691 us (0.986)
  waiting for transfers between devices: 195 us -> 185 us
    unnamed x340 -> x330, local copies, waits for them, and re-layouts: 40.4 us -> 40.7 us
  transfers between devices with their start and end apart: 68 -> 68, of which waited for: 32 -> 31; matrix products, arithmetic and copies ran while one was open for 41% -> 41% of each run, Pallas kernels for 9% -> 10%
where the time goes in v3:
time: 691 us; the launch traced here: 680 us
  waiting for transfers between devices  185 us (27%)
  other arithmetic  130 us (19%)
  local copies, waits for them, and re-layouts  116 us (17%)
  matrix products  109 us (16%)
  starting transfers between devices  70.8 us (10%)
  Pallas kernels  65 us (9%)
    ppermute x46, waiting for transfers between devices, swap_bit(): return lax.ppermute(values, axis, bit_swap(axis, bit, lax.axis_size(axis)))  147 us
    ppermute x46, starting transfers between devices, swap_bit(): return lax.ppermute(values, axis, bit_swap(axis, bit, lax.axis_size(axis)))  53.8 us
    dot_general x16, matrix products, dot_nn(): lax.dot_general(left, right, (((1,), (0,)), ((), ())), preferred_element_...  44.9 us
    pallas_call x4, Pallas kernels, attention_backward(): pl.pallas_call(functools.partial(attention_backward_kernel, seq_len), gri...  41.4 us
    unnamed x330, local copies, waits for them, and re-layouts  40.7 us
    ppermute x14, waiting for transfers between devices, to_side(): return lax.ppermute(values, 'mp', side_swap)  37.8 us
    dot_general x16, matrix products, dot_nt(): lax.dot_general(left, right, (((1,), (1,)), ((), ())), preferred_element_...  35 us
    dot_general x16, matrix products, dot_tn(): lax.dot_general(left, right, (((0,), (0,)), ((), ())), preferred_element_...  28.9 us
  transfers between devices with their start and end apart: 68, of which 31 were waited for; matrix products, arithmetic and copies ran while one was open for 41% of the time, Pallas kernels for 10%

profile of v3, /device:TPU:0, one launch (start us, length us, event | category | flops | bytes accessed | tf_op | source)
XLA Modules:
  0.0 680.0 jit_solution(17092486265007893362)
XLA Ops:
  3.7 3.0 collective-permute-start.5
  8.6 3.7 constant_dynamic-slice_fusion.28
  18.5 2.9 fusion.152
  33.2 3.3 collective-permute-start.4
  44.5 3.1 add_convert_fusion.10
  49.8 14.8 %collective-permute-done.6 = bf16[1,2,1,96,768]{3,4,2,1,0:T(8,128)(2,1)S(1)} collective-permute-done((bf16[1,2,1,96,768]{3,4,2,1,0:T(8,128)(2,1)S(1)}, bf16[1,2,1,96,768]{3,4,2,1,0:T(8,128)(2,1)S(1)}, u32[]{:S(2)}, u32[]{:S(2)}) %collective-permute-start.6) | collective-permute-done | bytes 294944 | tf_op jit(solution)/shard_map/ppermute | solution.py:152
  74.9 5.7 collective-permute-done.7
  82.9 3.4 maximum_select_fusion.2
  86.2 2.7 copy.315
  91.6 6.7 collective-permute-done.11
  109.0 5.9 shard_map.305
  114.9 3.4 fusion.108
  118.3 3.4 add_convert_fusion.17.qkv_ref
  121.7 5.9 shard_map.306
  127.5 2.6 add_convert_fusion.9
  133.6 6.8 %collective-permute-done.12 = bf16[2,2,1,96,1536]{4,3,1,0,2:T(8,128)(2,1)} collective-permute-done((bf16[2,2,1,96,1536]{4,3,1,0,2:T(8,128)(2,1)}, bf16[2,2,1,96,1536]{4,3,1,0,2:T(8,128)(2,1)}, u32[]{:S(2)}, u32[]{:S(2)}) %collective-permute-start.12) | collective-permute-done | bytes 1179680 | tf_op jit(solution)/shard_map/ppermute | solution.py:218
  144.5 32.1 %collective-permute-done.21 = bf16[1,2,1,96,1536]{4,3,2,1,0:T(8,128)(2,1)S(1)} collective-permute-done((bf16[1,2,1,96,1536]{4,3,2,1,0:T(8,128)(2,1)S(1)}, bf16[1,2,1,96,1536]{4,3,2,1,0:T(8,128)(2,1)S(1)}, u32[]{:S(2)}, u32[]{:S(2)}) %collective-permute-start.21) | collective-permute-done | bytes 589856 | tf_op jit(solution)/shard_map/ppermute | solution.py:152
  182.0 10.2 %collective-permute-done.13 = bf16[2,2,2,1,96,1536]{5,4,3,2,1,0:T(8,128)(2,1)S(1)} collective-permute-done((bf16[2,2,2,1,96,1536]{5,4,3,2,1,0:T(8,128)(2,1)S(1)}, bf16[2,2,2,1,96,1536]{5,4,3,2,1,0:T(8,128)(2,1)S(1)}, u32[]{:S(2)}, u32[]{:S(2)}) %collective-permute-start.13) | collective-permute-done | bytes 2359328 | tf_op jit(solution)/shard_map/ppermute | solution.py:152
  192.2 2.7 maximum_select_fusion
  195.6 2.8 multiply_convert_fusion.3
  199.6 3.3 multiply_convert_fusion.4
  232.4 3.0 pad_maximum_fusion.1
  236.0 2.9 add_add_fusion.1
  240.2 19.2 %collective-permute-done.18 = bf16[768,768]{1,0:T(8,128)(2,1)} collective-permute-done((bf16[768,768]{1,0:T(8,128)(2,1)}, bf16[768,768]{1,0:T(8,128)(2,1)}, u32[]{:S(2)}, u32[]{:S(2)}) %collective-permute-start.18) | collective-permute-done | bytes 1179680 | tf_op jit(solution)/shard_map/ppermute | solution.py:218
  259.4 3.3 add_convert_fusion.15.qkv_ref
  262.7 5.9 shard_map.308
  268.6 3.7 add_convert_fusion.16.qkv_ref
  272.3 5.9 shard_map.307
  281.9 7.0 %collective-permute-done.23 = bf16[2,2,2,1,96,1536]{5,4,2,1,3,0:T(8,128)(2,1)} collective-permute-done((bf16[2,2,2,1,96,1536]{5,4,2,1,3,0:T(8,128)(2,1)}, bf16[2,2,2,1,96,1536]{5,4,2,1,3,0:T(8,128)(2,1)}, u32[]{:S(2)}, u32[]{:S(2)}) %collective-permute-start.23) | collective-permute-done | bytes 2359328 | tf_op jit(solution)/shard_map/ppermute | solution.py:152
  288.9 4.0 maximum_select_fusion.1
  296.0 3.2 multiply_convert_fusion.1
  299.2 2.9 convert_reduce_fusion
  302.2 3.2 multiply_convert_fusion.2
  305.4 2.9 convert_reduce_fusion.2
  325.5 2.8 fusion.163
  337.6 10.3 %shard_map.309 = bf16[832,576]{1,0:T(8,128)(2,1)} custom-call(bf16[832,576]{1,0:T(8,128)(2,1)} %add_convert_fusion.16.qkv_ref, bf16[832,192]{1,0:T(8,128)(2,1)} %copy.336.grad_ref), custom_call_target="tpu_custom_call" | custom-call | flops 332267520 | bytes 2396160 | tf_op jit(solution)/shard_map/pallas_call | solution.py:133
  347.9 3.6 collective-permute-done.28
  364.3 10.4 %shard_map.310 = bf16[832,576]{1,0:T(8,128)(2,1)} custom-call(bf16[832,576]{1,0:T(8,128)(2,1)} %add_convert_fusion.15.qkv_ref, bf16[832,192]{1,0:T(8,128)(2,1)} %copy.339.grad_ref), custom_call_target="tpu_custom_call" | custom-call | flops 332267520 | bytes 2396160 | tf_op jit(solution)/shard_map/pallas_call | solution.py:133
  374.7 4.6 collective-permute-done.25
  379.3 2.8 fusion.29
  384.0 6.6 collective-permute-done.30
  394.1 2.9 collective-permute-start.32
  400.1 3.6 add_convert_fusion.2
  406.4 6.6 collective-permute-done.33
  414.0 5.2 collective-permute-done.32
  429.0 2.9 convert_reduce_fusion.1
  433.4 2.7 fusion.57
  437.2 3.3 convert_reduce_fusion.3
  447.6 4.7 convolution_add_fusion
  457.0 4.1 convolution_convert_fusion.2
  472.1 5.7 collective-permute-done.37
  495.3 10.3 %shard_map.311 = bf16[832,576]{1,0:T(8,128)(2,1)} custom-call(bf16[832,576]{1,0:T(8,128)(2,1)} %add_convert_fusion.18.qkv_ref, bf16[832,192]{1,0:T(8,128)(2,1)} %copy.347.grad_ref), custom_call_target="tpu_custom_call" | custom-call | flops 332267520 | bytes 2396160 | tf_op jit(solution)/shard_map/pallas_call | solution.py:133
  524.7 10.4 %shard_map.312 = bf16[832,576]{1,0:T(8,128)(2,1)} custom-call(bf16[832,576]{1,0:T(8,128)(2,1)} %add_convert_fusion.17.qkv_ref, bf16[832,192]{1,0:T(8,128)(2,1)} %copy.350.grad_ref), custom_call_target="tpu_custom_call" | custom-call | flops 332267520 | bytes 2396160 | tf_op jit(solution)/shard_map/pallas_call | solution.py:133
  563.2 8.8 %collective-permute-done.47 = bf16[1,2,1,96,768]{4,3,2,1,0:T(8,128)(2,1)} collective-permute-done((bf16[1,2,1,96,768]{4,3,2,1,0:T(8,128)(2,1)}, bf16[1,2,1,96,768]{4,3,2,1,0:T(8,128)(2,1)}, u32[]{:S(2)}, u32[]{:S(2)}) %collective-permute-start.47) | collective-permute-done | bytes 294944 | tf_op jit(solution)/shard_map/ppermute | solution.py:152
  573.1 4.7 collective-permute-done.46
  579.5 3.0 convert_add_fusion
  600.8 3.1 add_convert_fusion
  616.5 2.8 collective-permute-done.64
  625.4 8.8 %collective-permute-done.66 = f32[1,1,1,1,2,2,288]{6,5,4,3,2,1,0:T(2,128)S(1)} collective-permute-done((f32[1,1,1,1,2,2,288]{6,5,4,3,2,1,0:T(2,128)S(1)}, f32[1,1,1,1,2,2,288]{6,5,4,3,2,1,0:T(2,128)S(1)}, u32[]{:S(2)}, u32[]{:S(2)}) %collective-permute-start.66) | collective-permute-done | bytes 4640 | tf_op jit(solution)/shard_map/ppermute | solution.py:152
  639.4 4.4 collective-permute-done.51
  645.2 5.7 collective-permute-done.55
  651.1 2.9 collective-permute-done.52
  673.4 2.6 fusion.27
  676.1 3.7 copy.374
  (721 shorter events, 326.1 us)
Async XLA Ops:
  3.7 43.9 %collective-permute-start.5 = (bf16[1,1,1,96,768]{3,4,2,1,0:T(8,128)(2,1)}, bf16[1,1,1,96,768]{3,4,2,1,0:T(8,128)(2,1)S(1)}, u32[]{:S(2)}, u32[]{:S(2)}) collective-permute-start(bf16[1,1,1,96,768]{3,4,2,1,0:T(8,128)(2,1)} %pad_maximum_fusion.15), channel_id=1, source_target_pairs={{0,8},{4,12},{8,0},{12,4},{16,24},{20,28},{24,16},{28,20},{1,9},{5... | collective-permute-start | bytes 442376 | tf_op jit(solution)/shard_map/ppermute | solution.py:152
  8.6 61.3 %collective-permute-start.10 = (bf16[1,1,1,96,1536]{4,3,2,1,0:T(8,128)(2,1)}, bf16[1,1,1,96,1536]{4,3,2,1,0:T(8,128)(2,1)}, u32[]{:S(2)}, u32[]{:S(2)}) collective-permute-start(bf16[1,1,1,96,1536]{4,3,2,1,0:T(8,128)(2,1)} %pad_maximum_fusion.9), channel_id=1, source_target_pairs={{0,8},{4,12},{8,0},{12,4},{16,24},{20,28},{24,16},{28,20},{1,9},{5... | collective-permute-start | bytes 884744 | tf_op jit(solution)/shard_map/ppermute | solution.py:152
  8.6 13.1 %collective-permute-start = (f32[1,1,1,1,1,2,288]{6,0,5,4,3,2,1:T(1,128)S(1)}, f32[1,1,1,1,1,2,288]{6,0,5,4,3,2,1:T(1,128)S(1)}, u32[]{:S(2)}, u32[]{:S(2)}) collective-permute-start(f32[1,1,1,1,1,2,288]{6,0,5,4,3,2,1:T(1,128)S(1)} %bitcast.406), channel_id=1, source_target_pairs={{0,1},{1,0},{2,3},{3,2},{4,5},{5,4},{6,7},{7,6},{8,9},{9,8},{10,11... | collective-permute-start | bytes 6920 | tf_op jit(solution)/shard_map/ppermute | solution.py:152
  29.2 3.9 collective-permute-start.3
  33.2 7.2 %collective-permute-start.4 = (f32[1,2,2,2,2,2,288]{6,0,5,4,3,2,1:T(1,128)S(1)}, f32[1,2,2,2,2,2,288]{6,0,5,4,3,2,1:T(1,128)}, u32[]{:S(2)}, u32[]{:S(2)}) collective-permute-start(f32[1,2,2,2,2,2,288]{6,0,5,4,3,2,1:T(1,128)S(1)} %broadcast_select_fusion), channel_id=1, source_target_pairs={{0,16},{4,20},{8,24},{12,28},{16,0},{20,4},{24,8},{28,12},{1,17},{... | collective-permute-start | bytes 110600 | tf_op jit(solution)/shard_map/ppermute | solution.py:152
  47.7 16.9 %collective-permute-start.6 = (bf16[1,2,1,96,768]{3,4,2,1,0:T(8,128)(2,1)S(1)}, bf16[1,2,1,96,768]{3,4,2,1,0:T(8,128)(2,1)S(1)}, u32[]{:S(2)}, u32[]{:S(2)}) collective-permute-start(bf16[1,2,1,96,768]{3,4,2,1,0:T(8,128)(2,1)S(1)} %maximum_select_fusion.11), channel_id=1, source_target_pairs={{0,16},{4,20},{8,24},{12,28},{16,0},{20,4},{24,8},{28,12},{1,17},{... | collective-permute-start | bytes 884744 | tf_op jit(solution)/shard_map/ppermute | solution.py:152
  66.1 14.5 %collective-permute-start.7 = (bf16[2,2,1,96,768]{4,3,2,1,0:T(8,128)(2,1)}, bf16[2,2,1,96,768]{4,3,2,1,0:T(8,128)(2,1)}, u32[]{:S(2)}, u32[]{:S(2)}) collective-permute-start(bf16[2,2,1,96,768]{4,3,2,1,0:T(8,128)(2,1)} %copy.312), channel_id=1, source_target_pairs={{0,4},{4,0},{8,12},{12,8},{16,20},{20,16},{24,28},{28,24},{1,5},{5... | collective-permute-start | bytes 1769480 | tf_op jit(solution)/shard_map/ppermute | solution.py:152
  72.1 26.2 %collective-permute-start.11 = (bf16[1,2,1,96,1536]{4,3,1,0,2:T(8,128)(2,1)}, bf16[1,2,1,96,1536]{4,3,1,0,2:T(8,128)(2,1)}, u32[]{:S(2)}, u32[]{:S(2)}) collective-permute-start(bf16[1,2,1,96,1536]{4,3,1,0,2:T(8,128)(2,1)} %fusion.96), channel_id=1, source_target_pairs={{0,16},{4,20},{8,24},{12,28},{16,0},{20,4},{24,8},{28,12},{1,17},{... | collective-permute-start | bytes 1769480 | tf_op jit(solution)/shard_map/ppermute | solution.py:152
  88.9 29.4 %collective-permute-start.8 = (bf16[768,768]{1,0:T(8,128)(2,1)}, bf16[768,768]{1,0:T(8,128)(2,1)}, u32[]{:S(2)}, u32[]{:S(2)}) collective-permute-start(bf16[768,768]{1,0:T(8,128)(2,1)} %bitcast.360), channel_id=1, source_target_pairs={{0,2},{1,3},{2,0},{3,1},{4,6},{5,7},{6,4},{7,5},{8,10},{9,11},{10,... | collective-permute-start | bytes 3538952 | tf_op jit(solution)/shard_map/ppermute | solution.py:218
  100.9 39.5 %collective-permute-start.12 = (bf16[2,2,1,96,1536]{4,3,1,0,2:T(8,128)(2,1)}, bf16[2,2,1,96,1536]{4,3,1,0,2:T(8,128)(2,1)}, u32[]{:S(2)}, u32[]{:S(2)}) collective-permute-start(bf16[2,2,1,96,1536]{4,3,1,0,2:T(8,128)(2,1)} %bitcast_select_fusion), channel_id=1, source_target_pairs={{0,2},{1,3},{2,0},{3,1},{4,6},{5,7},{6,4},{7,5},{8,10},{9,11},{10,... | collective-permute-start | bytes 3538952 | tf_op jit(solution)/shard_map/ppermute | solution.py:218
  104.8 26.9 %collective-permute-start.20 = (bf16[1,1,1,96,1536]{4,3,2,1,0:T(8,128)(2,1)S(1)}, bf16[1,1,1,96,1536]{4,3,2,1,0:T(8,128)(2,1)S(1)}, u32[]{:S(2)}, u32[]{:S(2)}) collective-permute-start(bf16[1,1,1,96,1536]{4,3,2,1,0:T(8,128)(2,1)S(1)} %bitcast.365), channel_id=1, source_target_pairs={{0,8},{4,12},{8,0},{12,4},{16,24},{20,28},{24,16},{28,20},{1,9},{5... | collective-permute-start | bytes 884744 | tf_op jit(solution)/shard_map/ppermute | solution.py:152
  104.8 25.4 %collective-permute-start.15 = (bf16[1,1,1,96,768]{3,4,2,1,0:T(8,128)(2,1)S(1)}, bf16[1,1,1,96,768]{3,4,2,1,0:T(8,128)(2,1)S(1)}, u32[]{:S(2)}, u32[]{:S(2)}) collective-permute-start(bf16[1,1,1,96,768]{3,4,2,1,0:T(8,128)(2,1)S(1)} %bitcast.388), channel_id=1, source_target_pairs={{0,8},{4,12},{8,0},{12,4},{16,24},{20,28},{24,16},{28,20},{1,9},{5... | collective-permute-start | bytes 442376 | tf_op jit(solution)/shard_map/ppermute | solution.py:152
  130.2 48.2 %collective-permute-start.9 = (bf16[832,768]{1,0:T(8,128)(2,1)S(1)}, bf16[832,768]{1,0:T(8,128)(2,1)S(1)}, u32[]{:S(2)}, u32[]{:S(2)}) collective-permute-start(bf16[832,768]{1,0:T(8,128)(2,1)S(1)} %add_convert_fusion.9), channel_id=1, source_target_pairs={{0,1},{1,0},{2,3},{3,2},{4,5},{5,4},{6,7},{7,6},{8,9},{9,8},{10,11... | collective-permute-start | bytes 3833864 | tf_op jit(solution)/shard_map/ppermute | solution.py:215
  130.4 74.8 %collective-permute-start.16 = (bf16[1,2,1,96,768]{3,4,2,1,0:T(8,128)(2,1)S(1)}, bf16[1,2,1,96,768]{3,4,2,1,0:T(8,128)(2,1)S(1)}, u32[]{:S(2)}, u32[]{:S(2)}) collective-permute-start(bf16[1,2,1,96,768]{3,4,2,1,0:T(8,128)(2,1)S(1)} %maximum_select_fusion.13), channel_id=1, source_target_pairs={{0,16},{4,20},{8,24},{12,28},{16,0},{20,4},{24,8},{28,12},{1,17},{... | collective-permute-start | bytes 884744 | tf_op jit(solution)/shard_map/ppermute | solution.py:152
  131.8 44.8 %collective-permute-start.21 = (bf16[1,2,1,96,1536]{4,3,2,1,0:T(8,128)(2,1)S(1)}, bf16[1,2,1,96,1536]{4,3,2,1,0:T(8,128)(2,1)S(1)}, u32[]{:S(2)}, u32[]{:S(2)}) collective-permute-start(bf16[1,2,1,96,1536]{4,3,2,1,0:T(8,128)(2,1)S(1)} %maximum_select_fusion.9), channel_id=1, source_target_pairs={{0,16},{4,20},{8,24},{12,28},{16,0},{20,4},{24,8},{28,12},{1,17},{... | collective-permute-start | bytes 1769480 | tf_op jit(solution)/shard_map/ppermute | solution.py:152
  141.9 50.3 %collective-permute-start.13 = (bf16[2,2,2,1,96,1536]{5,4,3,2,1,0:T(8,128)(2,1)S(1)}, bf16[2,2,2,1,96,1536]{5,4,3,2,1,0:T(8,128)(2,1)S(1)}, u32[]{:S(2)}, u32[]{:S(2)}) collective-permute-start(bf16[2,2,2,1,96,1536]{5,4,3,2,1,0:T(8,128)(2,1)S(1)} %pad_maximum_fusion), channel_id=1, source_target_pairs={{0,4},{4,0},{8,12},{12,8},{16,20},{20,16},{24,28},{28,24},{1,5},{5... | collective-permute-start | bytes 7077896 | tf_op jit(solution)/shard_map/ppermute | solution.py:152
  177.8 54.6 %collective-permute-start.22 = (bf16[2,2,1,96,1536]{4,3,2,1,0:T(8,128)(2,1)}, bf16[2,2,1,96,1536]{4,3,2,1,0:T(8,128)(2,1)}, u32[]{:S(2)}, u32[]{:S(2)}) collective-permute-start(bf16[2,2,1,96,1536]{4,3,2,1,0:T(8,128)(2,1)} %fusion.39), channel_id=1, source_target_pairs={{0,2},{1,3},{2,0},{3,1},{4,6},{5,7},{6,4},{7,5},{8,10},{9,11},{10,... | collective-permute-start | bytes 3538952 | tf_op jit(solution)/shard_map/ppermute | solution.py:218
  205.2 30.8 %collective-permute-start.14 = (bf16[832,768]{1,0:T(8,128)(2,1)}, bf16[832,768]{1,0:T(8,128)(2,1)}, u32[]{:S(2)}, u32[]{:S(2)}) collective-permute-start(bf16[832,768]{1,0:T(8,128)(2,1)} %add_convert_fusion.7), channel_id=1, source_target_pairs={{0,1},{1,0},{2,3},{3,2},{4,5},{5,4},{6,7},{7,6},{8,9},{9,8},{10,11... | collective-permute-start | bytes 3833864 | tf_op jit(solution)/shard_map/ppermute | solution.py:215
  206.6 18.3 %collective-permute-start.17 = (bf16[2,2,1,96,768]{4,3,2,1,0:T(8,128)(2,1)}, bf16[2,2,1,96,768]{4,3,2,1,0:T(8,128)(2,1)}, u32[]{:S(2)}, u32[]{:S(2)}) collective-permute-start(bf16[2,2,1,96,768]{4,3,2,1,0:T(8,128)(2,1)} %copy.324), channel_id=1, source_target_pairs={{0,4},{4,0},{8,12},{12,8},{16,20},{20,16},{24,28},{28,24},{1,5},{5... | collective-permute-start | bytes 1769480 | tf_op jit(solution)/shard_map/ppermute | solution.py:152
  231.0 28.4 %collective-permute-start.18 = (bf16[768,768]{1,0:T(8,128)(2,1)}, bf16[768,768]{1,0:T(8,128)(2,1)}, u32[]{:S(2)}, u32[]{:S(2)}) collective-permute-start(bf16[768,768]{1,0:T(8,128)(2,1)} %bitcast.61), channel_id=1, source_target_pairs={{0,2},{1,3},{2,0},{3,1},{4,6},{5,7},{6,4},{7,5},{8,10},{9,11},{10,... | collective-permute-start | bytes 3538952 | tf_op jit(solution)/shard_map/ppermute | solution.py:218
  235.5 53.4 %collective-permute-start.23 = (bf16[2,2,2,1,96,1536]{5,4,2,1,3,0:T(8,128)(2,1)}, bf16[2,2,2,1,96,1536]{5,4,2,1,3,0:T(8,128)(2,1)}, u32[]{:S(2)}, u32[]{:S(2)}) collective-permute-start(bf16[2,2,2,1,96,1536]{5,4,2,1,3,0:T(8,128)(2,1)} %pad_maximum_fusion.1), channel_id=1, source_target_pairs={{0,4},{4,0},{8,12},{12,8},{16,20},{20,16},{24,28},{28,24},{1,5},{5... | collective-permute-start | bytes 7077896 | tf_op jit(solution)/shard_map/ppermute | solution.py:152
  281.8 11.9 %collective-permute-start.19 = (bf16[832,768]{1,0:T(8,128)(2,1)S(1)}, bf16[832,768]{1,0:T(8,128)(2,1)S(1)}, u32[]{:S(2)}, u32[]{:S(2)}) collective-permute-start(bf16[832,768]{1,0:T(8,128)(2,1)S(1)} %add_convert_fusion.5), channel_id=1, source_target_pairs={{0,1},{1,0},{2,3},{3,2},{4,5},{5,4},{6,7},{7,6},{8,9},{9,8},{10,11... | collective-permute-start | bytes 3833864 | tf_op jit(solution)/shard_map/ppermute | solution.py:215
  310.7 11.0 %collective-permute-start.26 = (bf16[832,768]{1,0:T(8,128)(2,1)S(1)}, bf16[832,768]{1,0:T(8,128)(2,1)S(1)}, u32[]{:S(2)}, u32[]{:S(2)}) collective-permute-start(bf16[832,768]{1,0:T(8,128)(2,1)S(1)} %convolution_add_fusion.1), channel_id=1, source_target_pairs={{0,1},{1,0},{2,3},{3,2},{4,5},{5,4},{6,7},{7,6},{8,9},{9,8},{10,11... | collective-permute-start | bytes 3833864 | tf_op jit(solution)/shard_map/ppermute | solution.py:215
  313.3 12.3 %collective-permute-start.24 = (bf16[832,768]{1,0:T(8,128)(2,1)S(1)}, bf16[832,768]{1,0:T(8,128)(2,1)S(1)}, u32[]{:S(2)}, u32[]{:S(2)}) collective-permute-start(bf16[832,768]{1,0:T(8,128)(2,1)S(1)} %add_convert_fusion.3), channel_id=1, source_target_pairs={{0,1},{1,0},{2,3},{3,2},{4,5},{5,4},{6,7},{7,6},{8,9},{9,8},{10,11... | collective-permute-start | bytes 3833864 | tf_op jit(solution)/shard_map/ppermute | solution.py:215
  323.2 28.2 %collective-permute-start.28 = (bf16[2,2,2,1,96,768]{5,4,2,1,3,0:T(8,128)(2,1)}, bf16[2,2,2,1,96,768]{5,4,2,1,3,0:T(8,128)(2,1)}, u32[]{:S(2)}, u32[]{:S(2)}) collective-permute-start(bf16[2,2,2,1,96,768]{5,4,2,1,3,0:T(8,128)(2,1)} %fusion.36), channel_id=1, source_target_pairs={{0,4},{4,0},{8,12},{12,8},{16,20},{20,16},{24,28},{28,24},{1,5},{5... | collective-permute-start | bytes 3538952 | tf_op jit(solution)/shard_map/ppermute | solution.py:152
  323.8 29.6 %collective-permute-start.27 = (bf16[768,768]{1,0:T(8,128)(2,1)}, bf16[768,768]{1,0:T(8,128)(2,1)}, u32[]{:S(2)}, u32[]{:S(2)}) collective-permute-start(bf16[768,768]{1,0:T(8,128)(2,1)} %convolution_convert_fusion.6), channel_id=1, source_target_pairs={{0,2},{1,3},{2,0},{3,1},{4,6},{5,7},{6,4},{7,5},{8,10},{9,11},{10,... | collective-permute-start | bytes 3538952 | tf_op jit(solution)/shard_map/ppermute | solution.py:218
  336.1 43.2 %collective-permute-start.25 = (bf16[4,197,768]{2,1,0:T(8,128)(2,1)}, bf16[4,197,768]{2,1,0:T(8,128)(2,1)}, u32[]{:S(2)}, u32[]{:S(2)}) collective-permute-start(bf16[4,197,768]{2,1,0:T(8,128)(2,1)} %slice.404), channel_id=1, source_target_pairs={{0,2},{1,3},{2,0},{3,1},{4,6},{5,7},{6,4},{7,5},{8,10},{9,11},{10,... | collective-permute-start | bytes 3631112 | tf_op jit(solution)/shard_map/ppermute | solution.py:218
  355.5 35.2 %collective-permute-start.30 = (bf16[2,2,1,96,768]{4,3,2,1,0:T(8,128)(2,1)S(1)}, bf16[2,2,1,96,768]{4,3,2,1,0:T(8,128)(2,1)}, u32[]{:S(2)}, u32[]{:S(2)}) collective-permute-start(bf16[2,2,1,96,768]{4,3,2,1,0:T(8,128)(2,1)S(1)} %slice_bitcast_fusion.1), channel_id=1, source_target_pairs={{0,2},{1,3},{2,0},{3,1},{4,6},{5,7},{6,4},{7,5},{8,10},{9,11},{10,... | collective-permute-start | bytes 1769480 | tf_op jit(solution)/shard_map/ppermute | solution.py:218
  357.0 34.9 %collective-permute-start.29 = (bf16[2,2,1,96,768]{4,3,2,1,0:T(8,128)(2,1)}, bf16[2,2,1,96,768]{4,3,2,1,0:T(8,128)(2,1)}, u32[]{:S(2)}, u32[]{:S(2)}) collective-permute-start(bf16[2,2,1,96,768]{4,3,2,1,0:T(8,128)(2,1)} %constant_dynamic-slice_fusion.27), channel_id=1, source_target_pairs={{0,4},{4,0},{8,12},{12,8},{16,20},{20,16},{24,28},{28,24},{1,5},{5... | collective-permute-start | bytes 1769480 | tf_op jit(solution)/shard_map/ppermute | solution.py:152
  393.3 19.7 %collective-permute-start.33 = (bf16[1,2,1,96,768]{4,3,2,1,0:T(8,128)(2,1)S(1)}, bf16[1,2,1,96,768]{4,3,2,1,0:T(8,128)(2,1)}, u32[]{:S(2)}, u32[]{:S(2)}) collective-permute-start(bf16[1,2,1,96,768]{4,3,2,1,0:T(8,128)(2,1)S(1)} %constant_dynamic-slice_fusion.25), channel_id=1, source_target_pairs={{0,16},{4,20},{8,24},{12,28},{16,0},{20,4},{24,8},{28,12},{1,17},{... | collective-permute-start | bytes 884744 | tf_op jit(solution)/shard_map/ppermute | solution.py:152
  394.1 25.0 %collective-permute-start.32 = (bf16[1,2,1,96,768]{4,3,2,1,0:T(8,128)(2,1)}, bf16[1,2,1,96,768]{4,3,2,1,0:T(8,128)(2,1)}, u32[]{:S(2)}, u32[]{:S(2)}) collective-permute-start(bf16[1,2,1,96,768]{4,3,2,1,0:T(8,128)(2,1)} %constant_dynamic-slice_fusion.26), channel_id=1, source_target_pairs={{0,16},{4,20},{8,24},{12,28},{16,0},{20,4},{24,8},{28,12},{1,17},{... | collective-permute-start | bytes 884744 | tf_op jit(solution)/shard_map/ppermute | solution.py:152
  403.7 17.3 %collective-permute-start.31 = (bf16[832,768]{1,0:T(8,128)(2,1)}, bf16[832,768]{1,0:T(8,128)(2,1)}, u32[]{:S(2)}, u32[]{:S(2)}) collective-permute-start(bf16[832,768]{1,0:T(8,128)(2,1)} %add_convert_fusion.2), channel_id=1, source_target_pairs={{0,1},{1,0},{2,3},{3,2},{4,5},{5,4},{6,7},{7,6},{8,9},{9,8},{10,11... | collective-permute-start | bytes 3833864 | tf_op jit(solution)/shard_map/ppermute | solution.py:215
  445.5 19.7 %collective-permute-start.35 = (bf16[2,2,2,1,96,384]{5,4,2,1,3,0:T(8,128)(2,1)}, bf16[2,2,2,1,96,384]{5,4,2,1,3,0:T(8,128)(2,1)}, u32[]{:S(2)}, u32[]{:S(2)}) collective-permute-start(bf16[2,2,2,1,96,384]{5,4,2,1,3,0:T(8,128)(2,1)} %fusion.93), channel_id=1, source_target_pairs={{0,4},{4,0},{8,12},{12,8},{16,20},{20,16},{24,28},{28,24},{1,5},{5... | collective-permute-start | bytes 1769480 | tf_op jit(solution)/shard_map/ppermute | solution.py:152
  447.1 16.5 %collective-permute-start.34 = (bf16[768,384]{0,1:T(8,128)(2,1)}, bf16[768,384]{0,1:T(8,128)(2,1)}, u32[]{:S(2)}, u32[]{:S(2)}) collective-permute-start(bf16[768,384]{0,1:T(8,128)(2,1)} %get-tuple-element.254), channel_id=1, source_target_pairs={{0,2},{1,3},{2,0},{3,1},{4,6},{5,7},{6,4},{7,5},{8,10},{9,11},{10,... | collective-permute-start | bytes 1769480 | tf_op jit(solution)/shard_map/ppermute | solution.py:218
  454.3 12.3 %collective-permute-start.62 = (bf16[1,1,1,96,768]{4,3,2,1,0:T(8,128)(2,1)}, bf16[1,1,1,96,768]{4,3,2,1,0:T(8,128)(2,1)}, u32[]{:S(2)}, u32[]{:S(2)}) collective-permute-start(bf16[1,1,1,96,768]{4,3,2,1,0:T(8,128)(2,1)} %constant_dynamic-slice_fusion.8), channel_id=1, source_target_pairs={{0,8},{4,12},{8,0},{12,4},{16,24},{20,28},{24,16},{28,20},{1,9},{5... | collective-permute-start | bytes 442376 | tf_op jit(solution)/shard_map/ppermute | solution.py:152
  455.0 15.5 %collective-permute-start.60 = (bf16[1,1,1,96,768]{4,3,2,1,0:T(8,128)(2,1)}, bf16[1,1,1,96,768]{4,3,2,1,0:T(8,128)(2,1)}, u32[]{:S(2)}, u32[]{:S(2)}) collective-permute-start(bf16[1,1,1,96,768]{4,3,2,1,0:T(8,128)(2,1)} %constant_dynamic-slice_fusion.10), channel_id=1, source_target_pairs={{0,8},{4,12},{8,0},{12,4},{16,24},{20,28},{24,16},{28,20},{1,9},{5... | collective-permute-start | bytes 442376 | tf_op jit(solution)/shard_map/ppermute | solution.py:152
  466.6 11.6 %collective-permute-start.36 = (bf16[832,768]{1,0:T(8,128)(2,1)S(1)}, bf16[832,768]{1,0:T(8,128)(2,1)S(1)}, u32[]{:S(2)}, u32[]{:S(2)}) collective-permute-start(bf16[832,768]{1,0:T(8,128)(2,1)S(1)} %copy-done.68), channel_id=1, source_target_pairs={{0,1},{1,0},{2,3},{3,2},{4,5},{5,4},{6,7},{7,6},{8,9},{9,8},{10,11... | collective-permute-start | bytes 3833864 | tf_op jit(solution)/shard_map/ppermute | solution.py:215
  468.3 9.5 %collective-permute-start.37 = (bf16[2,2,1,96,384]{4,3,2,1,0:T(8,128)(2,1)S(1)}, bf16[2,2,1,96,384]{4,3,2,1,0:T(8,128)(2,1)S(1)}, u32[]{:S(2)}, u32[]{:S(2)}) collective-permute-start(bf16[2,2,1,96,384]{4,3,2,1,0:T(8,128)(2,1)S(1)} %constant_dynamic-slice_fusion.24), channel_id=1, source_target_pairs={{0,4},{4,0},{8,12},{12,8},{16,20},{20,16},{24,28},{28,24},{1,5},{5... | collective-permute-start | bytes 884744 | tf_op jit(solution)/shard_map/ppermute | solution.py:152
  468.9 9.2 %collective-permute-start.38 = (bf16[2,2,1,96,384]{4,3,2,1,0:T(8,128)(2,1)S(1)}, bf16[2,2,1,96,384]{4,3,2,1,0:T(8,128)(2,1)S(1)}, u32[]{:S(2)}, u32[]{:S(2)}) collective-permute-start(bf16[2,2,1,96,384]{4,3,2,1,0:T(8,128)(2,1)S(1)} %slice_bitcast_fusion.3), channel_id=1, source_target_pairs={{0,2},{1,3},{2,0},{3,1},{4,6},{5,7},{6,4},{7,5},{8,10},{9,11},{10,... | collective-permute-start | bytes 884744 | tf_op jit(solution)/shard_map/ppermute | solution.py:218
  480.6 27.7 %collective-permute-start.42 = (bf16[2,2,2,1,96,768]{5,4,2,1,3,0:T(8,128)(2,1)}, bf16[2,2,2,1,96,768]{5,4,2,1,3,0:T(8,128)(2,1)}, u32[]{:S(2)}, u32[]{:S(2)}) collective-permute-start(bf16[2,2,2,1,96,768]{5,4,2,1,3,0:T(8,128)(2,1)} %fusion.32), channel_id=1, source_target_pairs={{0,4},{4,0},{8,12},{12,8},{16,20},{20,16},{24,28},{28,24},{1,5},{5... | collective-permute-start | bytes 3538952 | tf_op jit(solution)/shard_map/ppermute | solution.py:152
  482.1 28.1 %collective-permute-start.41 = (bf16[768,768]{1,0:T(8,128)(2,1)}, bf16[768,768]{1,0:T(8,128)(2,1)}, u32[]{:S(2)}, u32[]{:S(2)}) collective-permute-start(bf16[768,768]{1,0:T(8,128)(2,1)} %convolution_convert_fusion.2), channel_id=1, source_target_pairs={{0,2},{1,3},{2,0},{3,1},{4,6},{5,7},{6,4},{7,5},{8,10},{9,11},{10,... | collective-permute-start | bytes 3538952 | tf_op jit(solution)/shard_map/ppermute | solution.py:218
  483.6 22.0 %collective-permute-start.40 = (bf16[1,2,1,96,384]{4,3,2,1,0:T(8,128)(2,1)S(1)}, bf16[1,2,1,96,384]{4,3,2,1,0:T(8,128)(2,1)S(1)}, u32[]{:S(2)}, u32[]{:S(2)}) collective-permute-start(bf16[1,2,1,96,384]{4,3,2,1,0:T(8,128)(2,1)S(1)} %constant_dynamic-slice_fusion.22), channel_id=1, source_target_pairs={{0,16},{4,20},{8,24},{12,28},{16,0},{20,4},{24,8},{28,12},{1,17},{... | collective-permute-start | bytes 442376 | tf_op jit(solution)/shard_map/ppermute | solution.py:152
  485.0 21.3 %collective-permute-start.39 = (bf16[1,2,1,96,384]{4,3,2,1,0:T(8,128)(2,1)S(1)}, bf16[1,2,1,96,384]{4,3,2,1,0:T(8,128)(2,1)S(1)}, u32[]{:S(2)}, u32[]{:S(2)}) collective-permute-start(bf16[1,2,1,96,384]{4,3,2,1,0:T(8,128)(2,1)S(1)} %constant_dynamic-slice_fusion.23), channel_id=1, source_target_pairs={{0,16},{4,20},{8,24},{12,28},{16,0},{20,4},{24,8},{28,12},{1,17},{... | collective-permute-start | bytes 442376 | tf_op jit(solution)/shard_map/ppermute | solution.py:152
  515.3 32.5 %collective-permute-start.44 = (bf16[2,2,1,96,768]{4,3,2,1,0:T(8,128)(2,1)}, bf16[2,2,1,96,768]{4,3,2,1,0:T(8,128)(2,1)}, u32[]{:S(2)}, u32[]{:S(2)}) collective-permute-start(bf16[2,2,1,96,768]{4,3,2,1,0:T(8,128)(2,1)} %slice_bitcast_fusion), channel_id=1, source_target_pairs={{0,2},{1,3},{2,0},{3,1},{4,6},{5,7},{6,4},{7,5},{8,10},{9,11},{10,... | collective-permute-start | bytes 1769480 | tf_op jit(solution)/shard_map/ppermute | solution.py:218
  517.6 31.4 %collective-permute-start.43 = (bf16[2,2,1,96,768]{4,3,2,1,0:T(8,128)(2,1)}, bf16[2,2,1,96,768]{4,3,2,1,0:T(8,128)(2,1)}, u32[]{:S(2)}, u32[]{:S(2)}) collective-permute-start(bf16[2,2,1,96,768]{4,3,2,1,0:T(8,128)(2,1)} %constant_dynamic-slice_fusion.21), channel_id=1, source_target_pairs={{0,4},{4,0},{8,12},{12,8},{16,20},{20,16},{24,28},{28,24},{1,5},{5... | collective-permute-start | bytes 1769480 | tf_op jit(solution)/shard_map/ppermute | solution.py:152
  537.5 5.3 collective-permute-start.58
  538.6 4.4 collective-permute-start.57
  551.3 20.7 %collective-permute-start.47 = (bf16[1,2,1,96,768]{4,3,2,1,0:T(8,128)(2,1)}, bf16[1,2,1,96,768]{4,3,2,1,0:T(8,128)(2,1)}, u32[]{:S(2)}, u32[]{:S(2)}) collective-permute-start(bf16[1,2,1,96,768]{4,3,2,1,0:T(8,128)(2,1)} %constant_dynamic-slice_fusion.19), channel_id=1, source_target_pairs={{0,16},{4,20},{8,24},{12,28},{16,0},{20,4},{24,8},{28,12},{1,17},{... | collective-permute-start | bytes 884744 | tf_op jit(solution)/shard_map/ppermute | solution.py:152
  554.6 23.2 %collective-permute-start.46 = (bf16[1,2,1,96,768]{4,3,2,1,0:T(8,128)(2,1)}, bf16[1,2,1,96,768]{4,3,2,1,0:T(8,128)(2,1)}, u32[]{:S(2)}, u32[]{:S(2)}) collective-permute-start(bf16[1,2,1,96,768]{4,3,2,1,0:T(8,128)(2,1)} %constant_dynamic-slice_fusion.20), channel_id=1, source_target_pairs={{0,16},{4,20},{8,24},{12,28},{16,0},{20,4},{24,8},{28,12},{1,17},{... | collective-permute-start | bytes 884744 | tf_op jit(solution)/shard_map/ppermute | solution.py:152
  560.2 19.3 %collective-permute-start.45 = (bf16[832,768]{1,0:T(8,128)(2,1)S(1)}, bf16[832,768]{1,0:T(8,128)(2,1)}, u32[]{:S(2)}, u32[]{:S(2)}) collective-permute-start(bf16[832,768]{1,0:T(8,128)(2,1)S(1)} %add_convert_fusion.1), channel_id=1, source_target_pairs={{0,1},{1,0},{2,3},{3,2},{4,5},{5,4},{6,7},{7,6},{8,9},{9,8},{10,11... | collective-permute-start | bytes 3833864 | tf_op jit(solution)/shard_map/ppermute | solution.py:215
  589.8 18.8 %collective-permute-start.50 = (bf16[2,2,2,1,96,384]{5,4,2,1,3,0:T(8,128)(2,1)}, bf16[2,2,2,1,96,384]{5,4,2,1,3,0:T(8,128)(2,1)}, u32[]{:S(2)}, u32[]{:S(2)}) collective-permute-start(bf16[2,2,2,1,96,384]{5,4,2,1,3,0:T(8,128)(2,1)} %fusion.89), channel_id=1, source_target_pairs={{0,4},{4,0},{8,12},{12,8},{16,20},{20,16},{24,28},{28,24},{1,5},{5... | collective-permute-start | bytes 1769480 | tf_op jit(solution)/shard_map/ppermute | solution.py:152
  590.5 15.7 %collective-permute-start.49 = (bf16[768,384]{0,1:T(8,128)(2,1)}, bf16[768,384]{0,1:T(8,128)(2,1)}, u32[]{:S(2)}, u32[]{:S(2)}) collective-permute-start(bf16[768,384]{0,1:T(8,128)(2,1)} %get-tuple-element.252), channel_id=1, source_target_pairs={{0,2},{1,3},{2,0},{3,1},{4,6},{5,7},{6,4},{7,5},{8,10},{9,11},{10,... | collective-permute-start | bytes 1769480 | tf_op jit(solution)/shard_map/ppermute | solution.py:218
  598.0 7.6 %collective-permute-start.61 = (bf16[1,1,1,96,768]{4,3,2,1,0:T(8,128)(2,1)S(1)}, bf16[1,1,1,96,768]{4,3,2,1,0:T(8,128)(2,1)S(1)}, u32[]{:S(2)}, u32[]{:S(2)}) collective-permute-start(bf16[1,1,1,96,768]{4,3,2,1,0:T(8,128)(2,1)S(1)} %constant_dynamic-slice_fusion.9), channel_id=1, source_target_pairs={{0,8},{4,12},{8,0},{12,4},{16,24},{20,28},{24,16},{28,20},{1,9},{5... | collective-permute-start | bytes 442376 | tf_op jit(solution)/shard_map/ppermute | solution.py:152
  598.7 16.8 %collective-permute-start.59 = (bf16[1,1,1,96,768]{4,3,2,1,0:T(8,128)(2,1)}, bf16[1,1,1,96,768]{4,3,2,1,0:T(8,128)(2,1)}, u32[]{:S(2)}, u32[]{:S(2)}) collective-permute-start(bf16[1,1,1,96,768]{4,3,2,1,0:T(8,128)(2,1)} %constant_dynamic-slice_fusion.11), channel_id=1, source_target_pairs={{0,8},{4,12},{8,0},{12,4},{16,24},{20,28},{24,16},{28,20},{1,9},{5... | collective-permute-start | bytes 442376 | tf_op jit(solution)/shard_map/ppermute | solution.py:152
  604.0 69.4 %collective-permute-start.48 = (bf16[4,197,768]{2,1,0:T(8,128)(2,1)S(1)}, bf16[4,197,768]{2,1,0:T(8,128)(2,1)}, u32[]{:S(2)}, u32[]{:S(2)}) collective-permute-start(bf16[4,197,768]{2,1,0:T(8,128)(2,1)S(1)} %slice.405), channel_id=1, source_target_pairs={{0,2},{1,3},{2,0},{3,1},{4,6},{5,7},{6,4},{7,5},{8,10},{9,11},{10,... | collective-permute-start | bytes 3631112 | tf_op jit(solution)/shard_map/ppermute | solution.py:218
  610.0 5.3 collective-permute-start.63
  615.4 3.9 collective-permute-start.64
  623.2 11.0 %collective-permute-start.66 = (f32[1,1,1,1,2,2,288]{6,5,4,3,2,1,0:T(2,128)S(1)}, f32[1,1,1,1,2,2,288]{6,5,4,3,2,1,0:T(2,128)S(1)}, u32[]{:S(2)}, u32[]{:S(2)}) collective-permute-start(f32[1,1,1,1,2,2,288]{6,5,4,3,2,1,0:T(2,128)S(1)} %constant_dynamic-slice_fusion.2), channel_id=1, source_target_pairs={{0,2},{1,3},{2,0},{3,1},{4,6},{5,7},{6,4},{7,5},{8,10},{9,11},{10,... | collective-permute-start | bytes 13832 | tf_op jit(solution)/shard_map/ppermute | solution.py:152
  624.0 13.8 %collective-permute-start.54 = (bf16[2,2,1,96,384]{4,3,2,1,0:T(8,128)(2,1)S(1)}, bf16[2,2,1,96,384]{4,3,2,1,0:T(8,128)(2,1)S(1)}, u32[]{:S(2)}, u32[]{:S(2)}) collective-permute-start(bf16[2,2,1,96,384]{4,3,2,1,0:T(8,128)(2,1)S(1)} %slice_bitcast_fusion.2), channel_id=1, source_target_pairs={{0,2},{1,3},{2,0},{3,1},{4,6},{5,7},{6,4},{7,5},{8,10},{9,11},{10,... | collective-permute-start | bytes 884744 | tf_op jit(solution)/shard_map/ppermute | solution.py:218
  634.3 9.5 %collective-permute-start.51 = (bf16[2,2,1,96,384]{4,3,2,1,0:T(8,128)(2,1)S(1)}, bf16[2,2,1,96,384]{4,3,2,1,0:T(8,128)(2,1)S(1)}, u32[]{:S(2)}, u32[]{:S(2)}) collective-permute-start(bf16[2,2,1,96,384]{4,3,2,1,0:T(8,128)(2,1)S(1)} %constant_dynamic-slice_fusion.18), channel_id=1, source_target_pairs={{0,4},{4,0},{8,12},{12,8},{16,20},{20,16},{24,28},{28,24},{1,5},{5... | collective-permute-start | bytes 884744 | tf_op jit(solution)/shard_map/ppermute | solution.py:152
  638.0 13.0 %collective-permute-start.55 = (bf16[1,2,1,96,384]{4,3,2,1,0:T(8,128)(2,1)S(1)}, bf16[1,2,1,96,384]{4,3,2,1,0:T(8,128)(2,1)S(1)}, u32[]{:S(2)}, u32[]{:S(2)}) collective-permute-start(bf16[1,2,1,96,384]{4,3,2,1,0:T(8,128)(2,1)S(1)} %constant_dynamic-slice_fusion.15), channel_id=1, source_target_pairs={{0,16},{4,20},{8,24},{12,28},{16,0},{20,4},{24,8},{28,12},{1,17},{... | collective-permute-start | bytes 442376 | tf_op jit(solution)/shard_map/ppermute | solution.py:152
  643.9 10.1 %collective-permute-start.52 = (bf16[1,2,1,96,384]{4,3,2,1,0:T(8,128)(2,1)S(1)}, bf16[1,2,1,96,384]{4,3,2,1,0:T(8,128)(2,1)S(1)}, u32[]{:S(2)}, u32[]{:S(2)}) collective-permute-start(bf16[1,2,1,96,384]{4,3,2,1,0:T(8,128)(2,1)S(1)} %constant_dynamic-slice_fusion.17), channel_id=1, source_target_pairs={{0,16},{4,20},{8,24},{12,28},{16,0},{20,4},{24,8},{28,12},{1,17},{... | collective-permute-start | bytes 442376 | tf_op jit(solution)/shard_map/ppermute | solution.py:152
  651.0 4.6 collective-permute-start.56
  654.1 8.0 %collective-permute-start.53 = (bf16[1,1,1,96,384]{4,3,2,1,0:T(8,128)(2,1)S(1)}, bf16[1,1,1,96,384]{4,3,2,1,0:T(8,128)(2,1)}, u32[]{:S(2)}, u32[]{:S(2)}) collective-permute-start(bf16[1,1,1,96,384]{4,3,2,1,0:T(8,128)(2,1)S(1)} %constant_dynamic-slice_fusion.16), channel_id=1, source_target_pairs={{0,8},{4,12},{8,0},{12,4},{16,24},{20,28},{24,16},{28,20},{1,9},{5... | collective-permute-start | bytes 221192 | tf_op jit(solution)/shard_map/ppermute | solution.py:152
  (160 other events, 1315.3 us)
